TPU v7x, 32 devices: a whole 2x2x4 slice. The times are simulated.
32 devices in a mesh: dp: 32 (over z, y, x, core).
Axes of the slice: x: 2, y: 2, z: 4, core: 2. Of those that a mesh axis runs over, the one named last changes fastest.
Arguments:
- experience_buffer: float32 [42, 524288], P(None, 'dp'), may hold values from -6 to 6, as said below
- sampled_indices: int32 [32, 32, 256], P('dp'), may hold values from 0 to 16383
- filled_lengths: int32 [32, 32], P('dp'), may hold values from 1 to 256, as said below
- randomizer_numbers: int32 [32, 32, 256], P('dp'), may hold values from 0 to 524287
- agent_first_matrix: float32 [17, 256], replicated, may hold values from -1.5 to 1.5
- agent_first_offset: float32 [256], replicated, may hold values from -1.5 to 1.5
- agent_second_matrix: float32 [256, 256], replicated, may hold values from -0.375 to 0.375
- agent_second_offset: float32 [256], replicated, may hold values from -1.5 to 1.5
- agent_head_matrix: float32 [256, 12], replicated, may hold values from -0.375 to 0.375
- agent_head_offset: float32 [12], replicated, may hold values from -1.5 to 1.5
- judge_first_matrix: float32 [2, 23, 256], replicated, may hold values from -1.25 to 1.25
- judge_first_offset: float32 [2, 256], replicated, may hold values from -1.5 to 1.5
- judge_second_matrix: float32 [2, 256, 256], replicated, may hold values from -0.375 to 0.375
- judge_second_offset: float32 [2, 256], replicated, may hold values from -1.5 to 1.5
- judge_output_vector: float32 [2, 256], replicated, may hold values from -0.375 to 0.375
- judge_output_offset: float32 [2], replicated, may hold values from -1.5 to 1.5
- lagged_first_matrix: float32 [2, 23, 256], replicated, may hold values from -1.25 to 1.25
- lagged_first_offset: float32 [2, 256], replicated, may hold values from -1.5 to 1.5
- lagged_second_matrix: float32 [2, 256, 256], replicated, may hold values from -0.375 to 0.375
- lagged_second_offset: float32 [2, 256], replicated, may hold values from -1.5 to 1.5
- lagged_output_vector: float32 [2, 256], replicated, may hold values from -0.375 to 0.375
- lagged_output_offset: float32 [2], replicated, may hold values from -1.5 to 1.5
- heat_exponent_level: float32 [], replicated, may hold values from -2 to 0
Outputs:
- d_actor_w1: float32 [17, 256], replicated
- d_actor_b1: float32 [256], replicated
- d_actor_w2: float32 [256, 256], replicated
- d_actor_b2: float32 [256], replicated
- d_actor_w3: float32 [256, 12], replicated
- d_actor_b3: float32 [12], replicated
- d_critic_w1: float32 [2, 23, 256], replicated
- d_critic_b1: float32 [2, 256], replicated
- d_critic_w2: float32 [2, 256, 256], replicated
- d_critic_b2: float32 [2, 256], replicated
- d_critic_w3: float32 [2, 256], replicated
- d_critic_b3: float32 [2], replicated
- d_log_alpha: float32 [], replicated
- losses: float32 [3], replicated
Inputs may be any that keep to these rules, and one draw needn't show every extreme that they name: `experience_buffer`: columns in order: state (17), action (6), reward, next state (17), done flag of 0 or 1. filled_lengths[o, p] is how many leading entries of owner o's list for storage device p are used; in every draw one storage device, drawn from the seed, receives full lists of 256 from every owner.
All inputs are finite; a program needn't handle non-finite values.
Results may differ from a plain program's by a relative error of at most 0.0003.
Values sent between devices are 32-bit elements; how exact they have to be, the bound alone decides.
A program may use at most 256 MiB of HBM per device.

v0:
```python
import math

import jax
import jax.numpy as jnp
from jax import lax
from jax.sharding import PartitionSpec as P

OBS = 17
CONTROL_WIDTH = 6


PRECISE = lax.Precision.HIGHEST
GAMMA_FACTOR = 0.99
LOG_FLOOR = -5.0
LOG_CEIL = 2.0
SOFTNESS = 0.25


def stochastic_samples_from(seed_rows, first, number):
    components = first + jnp.arange(number, dtype=jnp.int32)
    seed_base = (seed_rows % 65521)[:, None]
    mixed = (seed_base * 257 + components[None, :] * 7919 + 1) % 65521
    first_hash = (mixed * 32749 + 12345) % 65521
    second_hash = (first_hash * 32749 + 54321) % 65521
    u_one = (first_hash.astype(jnp.float32) + 0.5) / 65521.0
    u_two = (second_hash.astype(jnp.float32) + 0.5) / 65521.0
    return jnp.sqrt(-2.0 * jnp.log(u_one)) * jnp.cos(2.0 * math.pi * u_two)


def linear(inputs, weight, offset):
    return jnp.dot(inputs, weight, precision=PRECISE) + offset


def actor_forward(controller_params_pack, present_sensed_world, normal_jitter):
    first_w, first_b, second_w, second_b, third_w, third_b = controller_params_pack
    hidden = jax.nn.silu(linear(present_sensed_world, first_w, first_b))
    hidden = jax.nn.silu(linear(hidden, second_w, second_b))
    output = linear(hidden, third_w, third_b)
    center = output[:, :CONTROL_WIDTH]
    spread = LOG_FLOOR + 0.5 * (LOG_CEIL - LOG_FLOOR) * (jnp.tanh(output[:, CONTROL_WIDTH:]) + 1.0)
    latent = center + jnp.exp(spread) * normal_jitter
    squashed = jnp.tanh(latent)
    squash = 2.0 * (math.log(2.0) - latent - jax.nn.softplus(-2.0 * latent))
    chosen_move_logprob = jnp.sum(
        -0.5 * normal_jitter * normal_jitter - spread - 0.5 * math.log(2.0 * math.pi) - squash,
        axis=1,
    )
    return (squashed, chosen_move_logprob)


def critic_forward(scorer_params_pack, member, present_sensed_world, picked_controls):
    first_w, first_b, second_w, second_b, third_w, third_b = scorer_params_pack
    joined = jnp.concatenate([present_sensed_world, picked_controls], axis=1)
    hidden = jax.nn.silu(linear(joined, first_w[member], first_b[member]))
    hidden = jax.nn.silu(linear(hidden, second_w[member], second_b[member]))
    return jnp.dot(hidden, third_w[member], precision=PRECISE) + third_b[member]


def soft_min(left_q, right_q):
    return -SOFTNESS * jnp.logaddexp(-left_q / SOFTNESS, -right_q / SOFTNESS)


def split_fields(fetched):
    present_sensed_world = fetched[:, :OBS]
    picked_controls = fetched[:, OBS : OBS + CONTROL_WIDTH]
    immediate_payoff = fetched[:, OBS + CONTROL_WIDTH]
    following_observations = fetched[:, OBS + CONTROL_WIDTH + 1 : 2 * OBS + CONTROL_WIDTH + 1]
    terminal_flags = fetched[:, 2 * OBS + CONTROL_WIDTH + 1]
    return (
        present_sensed_world,
        picked_controls,
        immediate_payoff,
        following_observations,
        terminal_flags,
    )


def backed_up_returns(
    controller_params_pack,
    lagged_weights_tuple,
    alpha_coefficient,
    following_observations,
    immediate_payoff,
    terminal_flags,
    following_gaussian_draw,
):
    next_actions, following_move_logprob = actor_forward(
        controller_params_pack, following_observations, following_gaussian_draw
    )
    lesser_twin_quality = soft_min(
        critic_forward(lagged_weights_tuple, 0, following_observations, next_actions),
        critic_forward(lagged_weights_tuple, 1, following_observations, next_actions),
    )
    return immediate_payoff + GAMMA_FACTOR * (1.0 - terminal_flags) * (
        lesser_twin_quality - alpha_coefficient * following_move_logprob
    )


def slice_costs(
    controller_params_pack,
    scorer_params_pack,
    heat_exponent_level,
    present_sensed_world,
    picked_controls,
    fitting_aims,
    normal_jitter,
    occupied_marker,
):
    alpha_coefficient = jnp.exp(heat_exponent_level)
    q_first = (
        critic_forward(scorer_params_pack, 0, present_sensed_world, picked_controls) - fitting_aims
    )
    q_second = (
        critic_forward(scorer_params_pack, 1, present_sensed_world, picked_controls) - fitting_aims
    )
    critic_loss = jnp.sum(occupied_marker * 0.5 * (q_first * q_first + q_second * q_second))
    fresh, chosen_move_logprob = actor_forward(
        controller_params_pack, present_sensed_world, normal_jitter
    )
    judged_quality = soft_min(
        critic_forward(scorer_params_pack, 0, present_sensed_world, fresh),
        critic_forward(scorer_params_pack, 1, present_sensed_world, fresh),
    )
    agent_penalty_amount = jnp.sum(
        occupied_marker * (alpha_coefficient * chosen_move_logprob - judged_quality)
    )
    alpha_penalty = jnp.sum(
        occupied_marker * (-heat_exponent_level * (chosen_move_logprob - CONTROL_WIDTH))
    )
    return (critic_loss, agent_penalty_amount, alpha_penalty)


def mask_of(count_row, capacity):
    return (
        (jnp.arange(capacity, dtype=jnp.int32)[None, :] < count_row[:, None])
        .reshape(-1)
        .astype(jnp.float32)
    )


def body(
    experience_buffer,
    sampled_indices,
    filled_lengths,
    randomizer_numbers,
    agent_first_matrix,
    agent_first_offset,
    agent_second_matrix,
    agent_second_offset,
    agent_head_matrix,
    agent_head_offset,
    judge_first_matrix,
    judge_first_offset,
    judge_second_matrix,
    judge_second_offset,
    judge_output_vector,
    judge_output_offset,
    lagged_first_matrix,
    lagged_first_offset,
    lagged_second_matrix,
    lagged_second_offset,
    lagged_output_vector,
    lagged_output_offset,
    heat_exponent_level,
):
    controller_params_pack = (
        agent_first_matrix,
        agent_first_offset,
        agent_second_matrix,
        agent_second_offset,
        agent_head_matrix,
        agent_head_offset,
    )
    scorer_params_pack = (
        judge_first_matrix,
        judge_first_offset,
        judge_second_matrix,
        judge_second_offset,
        judge_output_vector,
        judge_output_offset,
    )
    lagged_weights_tuple = (
        lagged_first_matrix,
        lagged_first_offset,
        lagged_second_matrix,
        lagged_second_offset,
        lagged_output_vector,
        lagged_output_offset,
    )
    alpha_coefficient = jnp.exp(heat_exponent_level)
    peer_count = sampled_indices.shape[1]
    capacity = sampled_indices.shape[2]
    own_seeds = randomizer_numbers.reshape(-1)
    occupied_marker = mask_of(filled_lengths[0], capacity)
    normal_jitter = stochastic_samples_from(own_seeds, 0, CONTROL_WIDTH)
    asked_rows = lax.all_to_all(sampled_indices, "dp", split_axis=1, concat_axis=1, tiled=True)
    picked = jnp.take(experience_buffer, asked_rows.reshape(-1), axis=1).reshape(
        experience_buffer.shape[0], peer_count, capacity
    )
    arrived = lax.all_to_all(picked, "dp", split_axis=1, concat_axis=1, tiled=True)
    fetched = arrived.reshape(experience_buffer.shape[0], -1).T
    (
        present_sensed_world,
        picked_controls,
        immediate_payoff,
        following_observations,
        terminal_flags,
    ) = split_fields(fetched)
    fitting_aims = backed_up_returns(
        controller_params_pack,
        lagged_weights_tuple,
        alpha_coefficient,
        following_observations,
        immediate_payoff,
        terminal_flags,
        stochastic_samples_from(own_seeds, CONTROL_WIDTH, CONTROL_WIDTH),
    )

    def shard_goal_function(present_controller, present_scorer, present_heat):
        return slice_costs(
            present_controller,
            present_scorer,
            present_heat,
            present_sensed_world,
            picked_controls,
            fitting_aims,
            normal_jitter,
            occupied_marker,
        )

    penalty_totals, reverse_derivative = jax.vjp(
        shard_goal_function, controller_params_pack, scorer_params_pack, heat_exponent_level
    )
    local_count = jnp.sum(filled_lengths).astype(jnp.float32)
    zero_val = jnp.zeros((), jnp.float32)
    unit_val = jnp.ones((), jnp.float32)
    critic_local = reverse_derivative((unit_val, zero_val, zero_val))[1]
    actor_local = reverse_derivative((zero_val, unit_val, zero_val))[0]
    alpha_local = reverse_derivative((zero_val, zero_val, unit_val))[2]
    summed = lax.psum(
        (
            actor_local[0],
            actor_local[1],
            actor_local[2],
            actor_local[3],
            actor_local[4],
            actor_local[5],
            critic_local[0],
            critic_local[1],
            critic_local[2],
            critic_local[3],
            critic_local[4],
            critic_local[5],
            alpha_local,
            penalty_totals[0],
            penalty_totals[1],
            penalty_totals[2],
            local_count,
        ),
        "dp",
    )
    valid_total = summed[16]
    scaled = [piece / valid_total for piece in summed[:13]]
    losses = jnp.stack([summed[13], summed[14], summed[15]]) / valid_total
    return (
        scaled[0],
        scaled[1],
        scaled[2],
        scaled[3],
        scaled[4],
        scaled[5],
        scaled[6],
        scaled[7],
        scaled[8],
        scaled[9],
        scaled[10],
        scaled[11],
        scaled[12],
        losses,
    )


def solution(mesh):
    in_specs = (
        P(None, "dp"),
        P("dp", None, None),
        P("dp", None),
        P("dp", None, None),
        P(),
        P(),
        P(),
        P(),
        P(),
        P(),
        P(),
        P(),
        P(),
        P(),
        P(),
        P(),
        P(),
        P(),
        P(),
        P(),
        P(),
        P(),
        P(),
    )
    out_specs = (P(), P(), P(), P(), P(), P(), P(), P(), P(), P(), P(), P(), P(), P())
    return jax.shard_map(body, mesh=mesh, in_specs=in_specs, out_specs=out_specs, check_vma=False)
```

profile of v0, /device:TPU:0, one launch (start us, length us, event | category | flops | bytes accessed | tf_op | source)
XLA Modules:
  0.0 856.7 jit_solution(9132974157591795887)
XLA Ops:
  26.7 31.1 %gather_fusion = f32[8192,42]{1,0:T(8,128)} fusion(f32[42,16384]{0,1:T(8,128)} %copy.57, s32[8192]{0:T(1024)S(1)} %broadcast_clamp_fusion), kind=kCustom, calls=%fused_computation | custom fusion | bytes 2785280 | tf_op jit(solution)/shard_map/jit(_take)/gather | solution.py:197
  72.5 33.3 %all-to-all-done.1 = f32[42,32,256]{2,0,1:T(8,128)S(1)} async-done(((f32[42,32,256]{2,0,1:T(8,128)}), f32[42,32,256]{2,0,1:T(8,128)S(1)}, u32[]{:S(2)}, u32[]{:S(2)}) %all-to-all-start.1) | async-done | bytes 1376288 | tf_op jit(solution)/shard_map/all_to_all | solution.py:200
  195.7 15.1 %convolution_add_fusion = f32[8192,256]{1,0:T(8,128)} fusion(f32[256]{0:T(256)S(1)} %bitcast.254, f32[8192,256]{1,0:T(8,128)} %convolution_add_fusion.1, f32[2,256,256]{2,1,0:T(8,128)S(1)} %copy-done.66), kind=kOutput, calls=%fused_computation.23 | convolution fusion | flops 6452936704 | bytes 17040384 | tf_op jit(solution)/shard_map/jvp()/dot_general | solution.py:31
  210.8 12.1 %fusion.125 = f32[1,8192]{1,0:T(1,128)S(1)} fusion(f32[8192,256]{1,0:T(8,128)} %convolution_add_fusion, f32[2,256]{1,0:T(2,128)S(1)} %copy-done.55), kind=kOutput, calls=%fused_computation.156 | convolution fusion | flops 33554432 | bytes 8422400 | tf_op jit(solution)/shard_map/jvp()/dot_general | solution.py:56
  233.0 12.1 %fusion.121 = f32[1,8192]{1,0:T(1,128)S(1)} fusion(f32[8192,256]{1,0:T(8,128)} %convolution_add_fusion.8, f32[2,256]{1,0:T(2,128)S(1)} %copy-done.55), kind=kOutput, calls=%fused_computation.154 | convolution fusion | flops 33554432 | bytes 8422400 | tf_op jit(solution)/shard_map/jvp()/dot_general | solution.py:56
  262.5 12.1 %fusion.30 = f32[1,8192]{1,0:T(1,128)S(1)} fusion(f32[8192,256]{1,0:T(8,128)} %convolution_add_fusion.2, f32[2,256]{1,0:T(2,128)S(1)} %copy-done.69), kind=kOutput, calls=%fused_computation.70 | convolution fusion | flops 33554432 | bytes 8422400 | tf_op jit(solution)/shard_map/dot_general | solution.py:56
  291.7 12.1 %fusion.41 = f32[1,8192]{1,0:T(1,128)S(1)} fusion(f32[8192,256]{1,0:T(8,128)} %convolution_add_fusion.4, f32[2,256]{1,0:T(2,128)S(1)} %copy-done.69), kind=kOutput, calls=%fused_computation.81 | convolution fusion | flops 33554432 | bytes 8422400 | tf_op jit(solution)/shard_map/dot_general | solution.py:56
  314.2 12.3 %fusion.117 = f32[1,8192]{1,0:T(1,128)S(1)} fusion(f32[8192,256]{1,0:T(8,128)} %convolution_add_fusion.12, f32[2,256]{1,0:T(2,128)S(1)} %copy-done.55), kind=kOutput, calls=%fused_computation.152 | convolution fusion | flops 33554432 | bytes 8422400 | tf_op jit(solution)/shard_map/jvp()/dot_general | solution.py:56
  349.7 22.3 %fusion.127 = f32[1,256,256]{2,1,0:T(8,128)} fusion(f32[8192,256]{1,0:T(8,128)S(1)} %bitcast.192, f32[8192,256]{1,0:T(8,128)} %convolution_add_fusion, f32[8192]{0:T(1024)S(1)} %get-tuple-element.130, f32[256]{0:T(256)S(1)} %bitcast.234), kind=kOutput, calls=%fused_computation.157 | convolution fusion | flops 6471811072 | bytes 17073152 | tf_op jit(solution)/shard_map/transpose(jvp())/dot_general | solution.py:31
  372.0 15.3 %fusion.315 = (f32[256]{0:T(256)}, f32[8192,256]{1,0:T(8,128)}) fusion(f32[8192,256]{1,0:T(8,128)S(1)} %bitcast.192, f32[2,256,256]{2,1,0:T(8,128)S(1)} %copy-done.66, f32[8192,256]{1,0:T(8,128)} %convolution_add_fusion, f32[8192]{0:T(1024)S(1)} %get-tuple-element.130, f32[256]{0:T(256)S(1)} %bitcast.235), kind=kOutput, calls=%fused_computation.406 | convolution fusion | flops 6484393984 | bytes 25462784 | tf_op jit(solution)/shard_map/transpose(jvp())/dot_general | solution.py:31
  388.0 22.1 %fusion.136 = f32[1,256,256]{2,1,0:T(8,128)} fusion(f32[8192,256]{1,0:T(8,128)S(1)} %convolution_add_fusion.11, f32[8192,256]{1,0:T(8,128)} %copy-done.8, f32[8192]{0:T(1024)S(1)} %get-tuple-element.127, f32[256]{0:T(256)S(1)} %bitcast.236), kind=kOutput, calls=%fused_computation.160 | convolution fusion | flops 6471811072 | bytes 17073152 | tf_op jit(solution)/shard_map/transpose(jvp())/dot_general | solution.py:31
  410.0 24.2 %fusion.133 = f32[1,256,256]{2,1,0:T(8,128)} fusion(f32[8192,256]{1,0:T(8,128)} %copy-done.5, f32[8192,256]{1,0:T(8,128)} %convolution_add_fusion.12, f32[8192]{0:T(1024)S(1)} %get-tuple-element.125, f32[256]{0:T(256)S(1)} %bitcast.240), kind=kOutput, calls=%fused_computation.159 | convolution fusion | flops 6471811072 | bytes 17073152 | tf_op jit(solution)/shard_map/transpose(jvp())/dot_general | solution.py:31
  434.3 17.3 %fusion.292 = (f32[256]{0:T(256)}, f32[256]{0:T(256)}, f32[256]{0:T(256)}, f32[256]{0:T(256)}) fusion(f32[8192,256]{1,0:T(8,128)} %copy-done.8, f32[256]{0:T(256)S(1)} %bitcast.237, f32[8192]{0:T(1024)S(1)} %get-tuple-element.127, f32[8192,256]{1,0:T(8,128)} %convolution_add_fusion, f32[8192]{0:T(1024)S(1)} %get-tuple-element.130, ...), kind=kLoop, calls=%fused_computation.390 | loop fusion | flops 92273664 | bytes 33691648 | tf_op jit(solution)/shard_map/transpose(jvp())/reduce_sum | solution.py:31
  451.5 21.7 %fusion.130 = f32[1,256,256]{2,1,0:T(8,128)} fusion(f32[8192,256]{1,0:T(8,128)S(1)} %bitcast.188, f32[8192,256]{1,0:T(8,128)} %convolution_add_fusion.8, f32[8192]{0:T(1024)S(1)} %get-tuple-element.132, f32[256]{0:T(256)S(1)} %bitcast.242), kind=kOutput, calls=%fused_computation.158 | convolution fusion | flops 6471811072 | bytes 17073152 | tf_op jit(solution)/shard_map/transpose(jvp())/dot_general | solution.py:31
  473.2 15.5 %fusion.316 = (f32[256]{0:T(256)}, f32[8192,256]{1,0:T(8,128)}) fusion(f32[8192,256]{1,0:T(8,128)S(1)} %bitcast.188, f32[2,256,256]{2,1,0:T(8,128)S(1)} %copy-done.66, f32[8192,256]{1,0:T(8,128)} %convolution_add_fusion.8, f32[8192]{0:T(1024)S(1)} %get-tuple-element.132, f32[256]{0:T(256)S(1)} %bitcast.243), kind=kOutput, calls=%fused_computation.407 | convolution fusion | flops 6484393984 | bytes 25462784 | tf_op jit(solution)/shard_map/transpose(jvp())/dot_general | solution.py:31
  488.7 16.4 %fusion.318 = (f32[256]{0:T(256)}, f32[8192,256]{1,0:T(8,128)}) fusion(f32[8192,256]{1,0:T(8,128)} %copy-done.5, f32[2,256,256]{2,1,0:T(8,128)S(1)} %copy-done.66, f32[8192,256]{1,0:T(8,128)} %convolution_add_fusion.12, f32[8192]{0:T(1024)S(1)} %get-tuple-element.125, f32[256]{0:T(256)S(1)} %bitcast.244), kind=kOutput, calls=%fused_computation.409 | convolution fusion | flops 6484393984 | bytes 25462784 | tf_op jit(solution)/shard_map/transpose(jvp())/dot_general | solution.py:31
  505.1 13.9 %fusion.317 = (f32[256]{0:T(256)}, f32[8192,256]{1,0:T(8,128)}) fusion(f32[8192,256]{1,0:T(8,128)S(1)} %convolution_add_fusion.11, f32[2,256,256]{2,1,0:T(8,128)S(1)} %copy-done.66, f32[8192,256]{1,0:T(8,128)S(1)} %bitcast.198, f32[8192]{0:T(1024)S(1)} %get-tuple-element.127, f32[256]{0:T(256)S(1)} %bitcast.238), kind=kOutput, calls=%fused_computation.408 | convolution fusion | flops 6484393984 | bytes 25462784 | tf_op jit(solution)/shard_map/transpose(jvp())/dot_general | solution.py:31
  530.7 13.8 %fusion.8 = f32[8192,256]{1,0:T(8,128)} fusion(f32[8192,256]{1,0:T(8,128)} %copy-done.8, f32[256]{0:T(256)S(1)} %bitcast.239, f32[8192]{0:T(1024)S(1)} %copy-done.42, f32[2,256,256]{2,1,0:T(8,128)S(1)} %copy-done.66), kind=kOutput, calls=%fused_computation.48 | convolution fusion | flops 6463422464 | bytes 17073152 | tf_op jit(solution)/shard_map/transpose(jvp())/dot_general | solution.py:31
  544.6 12.5 %fusion.68 = f32[8192,6]{0,1:T(8,128)S(1)} fusion(f32[8192,256]{1,0:T(8,128)S(1)} %bitcast.190, f32[8192,256]{1,0:T(8,128)} %fusion.3, f32[23,256]{1,0:T(8,128)} %get-tuple-element.164), kind=kOutput, calls=%fused_computation.112 | convolution fusion | flops 169869312 | bytes 16982016 | tf_op jit(solution)/shard_map/transpose(jvp())/dot_general | solution.py:31
  557.1 13.1 %multiply_multiply_fusion.14 = (f32[8192,6]{0,1:T(8,128)S(1)}, f32[8192,6]{0,1:T(8,128)S(1)}) fusion(f32[8192,12]{0,1:T(8,128)S(1)} %copy-done.14, s32[6]{0:T(128)S(1)} %copy-done.64, s32[8192]{0:T(1024)S(1)} %copy-done.28, f32[8192]{0:T(1024)S(1)} %copy-done.40, f32[8192,6]{0,1:T(8,128)S(1)} %copy-done.12, f32[8192,6]{0,1:T(8,128)S(1)} %fusion.68, ...), kind=kOutput, calls=%fused_computation.248 | convolution fusion | flops 172965888 | bytes 17866776 | tf_op jit(solution)/shard_map/transpose(jvp())/dot_general | solution.py:31
  576.3 11.9 %fusion.314 = (f32[256]{0:T(256)S(1)}, f32[8192,256]{1,0:T(8,128)S(1)}) fusion(f32[8192,256]{1,0:T(8,128)} %convolution_add_fusion.14, f32[256,12]{0,1:T(8,128)S(1)} %copy-done.68, f32[8192,6]{0,1:T(8,128)S(1)} %get-tuple-element.150, f32[8192,6]{0,1:T(8,128)S(1)} %get-tuple-element.149), kind=kOutput, calls=%fused_computation.405 | convolution fusion | flops 323059456 | bytes 17183744 | tf_op jit(solution)/shard_map/transpose(jvp())/dot_general | solution.py:31
  588.2 15.4 %fusion.99 = f32[256,256]{1,0:T(8,128)} fusion(f32[8192,256]{1,0:T(8,128)S(1)} %get-tuple-element.152, f32[8192,256]{1,0:T(8,128)S(1)} %bitcast.186), kind=kOutput, calls=%fused_computation.145 | convolution fusion | flops 6450839552 | bytes 17039360 | tf_op jit(solution)/shard_map/transpose(jvp())/dot_general | solution.py:31
  663.2 40.2 %all-reduce.32 = (f32[17,256]{1,0:T(8,128)S(1)}, f32[]{:T(128)}, f32[256]{0:T(256)S(1)}, f32[256]{0:T(256)S(1)}, f32[256,12]{0,1:T(8,128)S(1)}, /*index=5*/f32[1...) all-reduce(f32[17,256]{1,0:T(8,128)S(1)} %fusion.283, ...), channel_id=1, replica_groups=mesh['dp'=32] {'dp'}, use_global_device_ids=true, to_apply=%region_0.1 | all-reduce | flops 21267 | bytes 170136 | tf_op jit(solution)/shard_map/psum | solution.py:240
  721.0 122.5 %all-reduce.31.cloned.1.call-done = (f32[256,256]{1,0:T(8,128)}, f32[2,256,256]{2,1,0:T(8,128)}) async-done(((f32[256,256]{1,0:T(8,128)}, f32[2,256,256]{2,1,0:T(8,128)}), (f32[256,256]{1,0:T(8,128)}, f32[2,256,256]{2,1,0:T(8,128)})) %all-reduce.31.cloned.1.call-update) | async-done | bytes 786448 | tf_op jit(solution)/shard_map/psum | solution.py:240
  (304 shorter events, 295.8 us)
Async XLA Ops:
  7.2 131.5 %copy-start = (f32[256,256]{1,0:T(8,128)S(1)}, f32[256,256]{1,0:T(8,128)}, u32[]{:S(2)}) copy-start(f32[256,256]{1,0:T(8,128)} %param.29) | copy-start | bytes 786436
  8.6 18.0 %all-to-all-start = ((s32[1,32,256]{2,0,1:T(1,128)}), s32[1,32,256]{2,0,1:T(1,128)S(1)}, u32[]{:S(2)}, u32[]{:S(2)}) async-start(s32[1,32,256]{2,0,1:T(1,128)} %copy.56), calls=%async_computation | async-start | bytes 65536 | tf_op jit(solution)/shard_map/all_to_all | solution.py:196
  62.3 46.4 %copy-start.35 = (f32[17,256]{1,0:T(8,128)S(1)}, f32[17,256]{1,0:T(8,128)}, u32[]{:S(2)}) copy-start(f32[17,256]{1,0:T(8,128)} %param.27) | copy-start | bytes 52228
  62.3 46.4 %copy-start.43 = (f32[256]{0:T(256)S(1)}, f32[256]{0:T(256)}, u32[]{:S(2)}) copy-start(f32[256]{0:T(256)} %param.28) | copy-start | bytes 3076
  62.3 43.6 %all-to-all-start.1 = ((f32[42,32,256]{2,0,1:T(8,128)}), f32[42,32,256]{2,0,1:T(8,128)S(1)}, u32[]{:S(2)}, u32[]{:S(2)}) async-start(f32[42,32,256]{2,0,1:T(8,128)} %broadcast_select_fusion), calls=%async_computation.1 | async-start | bytes 3145728 | tf_op jit(solution)/shard_map/all_to_all | solution.py:200
  68.1 775.4 %all-reduce.31.cloned.1.call-start = ((), (), s32[]{:S(2)}) async-start(), calls=%async_computation.2 | async-start | bytes 1572864 | tf_op jit(solution)/shard_map/psum | solution.py:240
  68.2 108.7 %copy-start.63 = (s32[6]{0:T(128)}, s32[6]{0:T(128)S(1)}, u32[]{:S(2)}) copy-start(s32[6]{0:T(128)S(1)} %iota_multiply_fusion) | copy-start | bytes 76
  71.2 105.8 %copy-start.27 = (s32[8192]{0:T(1024)}, s32[8192]{0:T(1024)S(1)}, u32[]{:S(2)}) copy-start(s32[8192]{0:T(1024)S(1)} %fusion.223) | copy-start | bytes 98308
  108.7 79.7 %copy-start.6 = (f32[8192,17]{0,1:T(8,128)}, f32[8192,17]{0,1:T(8,128)S(1)}, u32[]{:S(2)}) copy-start(f32[8192,17]{0,1:T(8,128)S(1)} %get-tuple-element.111) | copy-start | bytes 1671172
  138.7 84.3 %copy-start.4 = (f32[8192,256]{1,0:T(8,128)}, f32[8192,256]{1,0:T(8,128)S(1)}, u32[]{:S(2)}) copy-start(f32[8192,256]{1,0:T(8,128)S(1)} %convolution_add_fusion.9) | copy-start | bytes 25165828
  195.7 108.1 %copy-start.5 = (f32[8192,256]{1,0:T(8,128)}, f32[8192,256]{1,0:T(8,128)S(1)}, u32[]{:S(2)}) copy-start(f32[8192,256]{1,0:T(8,128)S(1)} %convolution_add_fusion.13) | copy-start | bytes 25165828
  314.1 35.5 %slice-start.6 = ((s8[8388608]{0:T(1024)(128)(4,1)}), s8[4194304]{0:T(1024)(128)(4,1)S(1)}, s32[]{:S(2)}) async-start(s8[8388608]{0:T(1024)(128)(4,1)} %bitcast.191), calls=%async_computation.9 | async-start | bytes 8388608
  349.7 84.6 %copy-start.23 = (f32[8192]{0:T(1024)}, f32[8192]{0:T(1024)S(1)}, u32[]{:S(2)}) copy-start(f32[8192]{0:T(1024)S(1)} %get-tuple-element.130) | copy-start | bytes 98308
  349.7 123.5 %copy-start.25 = (f32[8192]{0:T(1024)}, f32[8192]{0:T(1024)S(1)}, u32[]{:S(2)}) copy-start(f32[8192]{0:T(1024)S(1)} %get-tuple-element.132) | copy-start | bytes 98308
  349.7 155.4 %copy-start.21 = (f32[8192]{0:T(1024)}, f32[8192]{0:T(1024)S(1)}, u32[]{:S(2)}) copy-start(f32[8192]{0:T(1024)S(1)} %get-tuple-element.127) | copy-start | bytes 98308
  388.0 100.8 %copy-start.19 = (f32[8192]{0:T(1024)}, f32[8192]{0:T(1024)S(1)}, u32[]{:S(2)}) copy-start(f32[8192]{0:T(1024)S(1)} %get-tuple-element.125) | copy-start | bytes 98308
  388.0 63.6 %slice-start.2 = ((s8[8388608]{0:T(1024)(128)(4,1)}), s8[4194304]{0:T(1024)(128)(4,1)S(1)}, s32[]{:S(2)}) async-start(s8[8388608]{0:T(1024)(128)(4,1)} %bitcast.187), calls=%async_computation.5 | async-start | bytes 8388608
  410.0 41.5 %slice-start.3 = ((s8[8388608]{0:T(1024)(128)(4,1)}), s8[4194304]{0:T(1024)(128)(4,1)S(1)}, s32[]{:S(2)}) async-start(s8[8388608]{0:T(1024)(128)(4,1)} %bitcast.187), calls=%async_computation.6 | async-start | bytes 8388608
  473.2 31.9 %slice-start.12 = ((s8[8388608]{0:T(1024)(128)(4,1)}), s8[4194304]{0:T(1024)(128)(4,1)S(1)}, s32[]{:S(2)}) async-start(s8[8388608]{0:T(1024)(128)(4,1)} %bitcast.197), calls=%async_computation.15 | async-start | bytes 8388608
  488.7 30.3 %slice-start.8 = ((s8[8388608]{0:T(1024)(128)(4,1)}), s8[4194304]{0:T(1024)(128)(4,1)S(1)}, s32[]{:S(2)}) async-start(s8[8388608]{0:T(1024)(128)(4,1)} %bitcast.193), calls=%async_computation.11 | async-start | bytes 8388608
  655.0 57.6 %copy-start.15 = (f32[1,256,256]{2,1,0:T(8,128)S(1)}, f32[1,256,256]{2,1,0:T(8,128)}, u32[]{:S(2)}) copy-start(f32[1,256,256]{2,1,0:T(8,128)} %fusion.127) | copy-start | bytes 786436
  655.0 57.6 %copy-start.16 = (f32[1,256,256]{2,1,0:T(8,128)S(1)}, f32[1,256,256]{2,1,0:T(8,128)}, u32[]{:S(2)}) copy-start(f32[1,256,256]{2,1,0:T(8,128)} %fusion.136) | copy-start | bytes 786436
  655.0 57.6 %copy-start.17 = (f32[1,256,256]{2,1,0:T(8,128)S(1)}, f32[1,256,256]{2,1,0:T(8,128)}, u32[]{:S(2)}) copy-start(f32[1,256,256]{2,1,0:T(8,128)} %fusion.133) | copy-start | bytes 786436
  655.0 57.6 %copy-start.18 = (f32[1,256,256]{2,1,0:T(8,128)S(1)}, f32[1,256,256]{2,1,0:T(8,128)}, u32[]{:S(2)}) copy-start(f32[1,256,256]{2,1,0:T(8,128)} %fusion.130) | copy-start | bytes 786436
  (79 other events, 895.4 us)
Sparse Core Ops, SparseCore 0:
  713.6 129.8 all-reduce.30
where the time goes:
time: 867 us; the launch traced here: 857 us
  matrix products  520 us (60%)
  waiting for transfers between devices  156 us (18%)
  other arithmetic  54.4 us (6%)
  local copies, waits for them, and re-layouts  50.3 us (6%)
  blocking collectives  40.2 us (5%)
  between operations  22.5 us (3%)
  starting transfers between devices  13.2 us (2%)
    dot_general x39, matrix products, linear(): return jnp.dot(inputs, weight, precision=PRECISE) + offset  426 us
    psum x1, waiting for transfers between devices, body(): lax.psum((actor_local[0], actor_local[1], actor_local[2], actor_local[3],...  122 us
    dot_general x10, matrix products, critic_forward(): return jnp.dot(hidden, third_w[member], precision=PRECISE) + third_b[member]  94 us
    psum x1, blocking collectives, body(): lax.psum((actor_local[0], actor_local[1], actor_local[2], actor_local[3],...  40.2 us
    gather x2, local copies, waits for them, and re-layouts, body(): jnp.take(experience_buffer, asked_rows.reshape(-1), axis=1)  34.1 us
    all_to_all x1, waiting for transfers between devices, body(): lax.all_to_all(picked, 'dp', split_axis=1, concat_axis=1, tiled=True)  33.3 us
    reduce_sum x2, other arithmetic, linear(): return jnp.dot(inputs, weight, precision=PRECISE) + offset  17.5 us
  transfers between devices with their start and end apart: 3, of which 2 were waited for; matrix products, arithmetic and copies ran while one was open for 2% of the time, Pallas kernels for 0%

commit v1 on v0

v1 whole, which is shorter than its diff:
```python
import functools
import math

import jax
import jax.numpy as jnp
from jax import lax
from jax.experimental import pallas as pl
from jax.experimental.pallas import tpu as pltpu
from jax.sharding import PartitionSpec as P

OBS = 17
ACT = 6
HID = 256
GAMMA = 0.99
PRIME = 65521
TILE = 1024
BF = jnp.bfloat16
F32 = jnp.float32


def dot(a, b):
    return jnp.dot(a, b, preferred_element_type=F32)


def dot_t(a, b):
    return lax.dot_general(a, b, (((1,), (1,)), ((), ())), preferred_element_type=F32)


def split(x):
    hi = x.astype(BF).astype(F32)
    return hi, x - hi


def mod_prime(x):
    y = ((x >> 16) * 15) + (x & 65535)
    y = ((y >> 16) * 15) + (y & 65535)
    return jnp.where(y >= PRIME, y - PRIME, y)


def noise(seeds, rows):
    comp = jnp.where(rows >= 8, rows - 2, rows)
    z = mod_prime(seeds)
    h0 = mod_prime(z * 257 + comp * 7919 + 1)
    h1 = mod_prime(h0 * 32749 + 12345)
    h2 = mod_prime(h1 * 32749 + 54321)
    u1 = (h1.astype(F32) + 0.5) / float(PRIME)
    u2 = (h2.astype(F32) + 0.5) / float(PRIME)
    return jnp.sqrt(-2.0 * jnp.log(u1)) * jnp.cos(2.0 * math.pi * u2)


def fold(x):
    return functools.reduce(lambda a, b: a + b, [x[:, k * 128 : (k + 1) * 128] for k in range(x.shape[1] // 128)])


def net_kernel(
    idx_s, cnt_s, alpha_s, hb3_s, jb3_s, lb3_s,
    buf, seeds,
    aw1, ab1, aw2, ab2, aw3,
    jw1, jb1, jw2, jb2, jw3,
    lw1, lb1, lw2, lb2, lw3,
    gw2, gaw1, gcw1, gaw3, gcol, gmisc,
    tab, xrow, w1all, f2, b2, head, headb, da_w, col, tmp, rowbuf,
    *, cap, width, slots,
):
    T = min(TILE, slots)
    nt = slots // T
    lists = T // cap

    @pl.loop(0, width // 128)
    def _(c):
        blk = buf[:, pl.ds(pl.multiple_of(c * 128, 128), 128)]
        tab[pl.ds(pl.multiple_of(c * 128, 128), 128), 0:42] = blk.T

    rowbuf[...] = jnp.zeros_like(rowbuf)
    for l, (w1, b1, k) in enumerate(((aw1, ab1, None), (jw1, jb1, 0), (jw1, jb1, 1), (lw1, lb1, 0), (lw1, lb1, 1))):
        if k is None:
            tmp[0:6, :] = jnp.zeros((6, HID), F32)
            tmp[6:7, :] = b1[...]
            tmp[7:8, :] = w1[16:17, :]
            tmp[8:24, :] = w1[0:16, :]
        else:
            tmp[0:6, :] = w1[k, 17:23, :]
            tmp[6:7, :] = b1[k : k + 1, :]
            tmp[7:8, :] = w1[k, 16:17, :]
            tmp[8:24, :] = w1[k, 0:16, :]
        hi, lo = split(0.5 * tmp[0:24, :])
        w1all[l * HID : (l + 1) * HID, :] = jnp.concatenate([hi, hi, lo], axis=0).T.astype(BF)
        if l in (1, 2):
            hi, lo = split(tmp[0:8, :])
            da_w[l - 1] = jnp.concatenate([hi, lo], axis=0).astype(BF)
    for l, w in enumerate((aw2[...], jw2[0], jw2[1], lw2[0], lw2[1])):
        hi, lo = split(0.5 * w)
        if l < 3:
            b2[l, 0:HID, :] = hi.astype(BF)
            b2[l, HID:, :] = lo.astype(BF)
        f2[l, 0:HID, :] = hi.T.astype(BF)
        f2[l, HID:, :] = lo.T.astype(BF)
    tmp[0:12, :] = aw3[...].T
    w_mean = tmp[0:8, :]
    w_ls = tmp[6:14, :]
    r8 = lax.broadcasted_iota(jnp.int32, (8, HID), 0)
    w_head = jnp.concatenate([jnp.where(r8 < 6, w_mean, 0.0), jnp.where(r8 < 6, w_ls, 0.0)], axis=0)
    hi, lo = split(w_head)
    head[...] = jnp.concatenate([hi, lo], axis=0).astype(BF)
    headb[...] = (0.5 * jnp.concatenate([hi, lo], axis=0)).T.astype(BF)
    rowbuf[0:1, :] = 0.5 * ab2[...]
    rowbuf[1:3, :] = 0.5 * jb2[...]
    rowbuf[3:5, :] = 0.5 * lb2[...]
    rowbuf[5:7, :] = jw3[...]
    rowbuf[7:9, :] = lw3[...]
    col[:, 0:16] = rowbuf[...].T
    rows16 = lax.broadcasted_iota(jnp.int32, (16, 1), 0)
    hb = jnp.zeros((16, 1), F32)
    for k in range(12):
        hb = jnp.where(rows16 == (k if k < 6 else k + 2), hb3_s[k], hb)

    gw2[...] = jnp.zeros_like(gw2)
    gaw1[...] = jnp.zeros_like(gaw1)
    gcw1[...] = jnp.zeros_like(gcw1)
    gaw3[...] = jnp.zeros_like(gaw3)
    gcol[...] = jnp.zeros_like(gcol)
    gmisc[...] = jnp.zeros_like(gmisc)
    level = alpha_s[0]

    def act(u):
        t = jnp.tanh(u)
        p = 1.0 + t
        h = u * p
        return h, p + h * (2.0 - p)

    def layer2(l, h):
        r = dot(f2[l], h.astype(BF))
        return act(r[:HID] + r[HID:] + col[:, l : l + 1])

    def first(l0, l1, x24):
        hi, lo = split(x24)
        xs = jnp.concatenate([hi, lo, hi], axis=0).astype(BF)
        return dot(w1all[l0 * HID : l1 * HID, :], xs)

    def back2(l, g):
        r = dot(b2[l], g)
        return r[:HID] + r[HID:]

    def head_out(h2):
        r = dot(head[...], h2.astype(BF))
        o = r[0:16] + r[16:32] + hb
        mean = o[0:8]
        t = jnp.tanh(o[8:16])
        ls = -5.0 + 3.5 * (t + 1.0)
        return mean, t, ls

    def sample(mean, ls, e, live):
        sg = jnp.exp(ls)
        u = mean + sg * e
        a = jnp.tanh(u)
        au = jnp.abs(u)
        sq = 2.0 * (math.log(2.0) - au - jnp.log1p(jnp.exp(-2.0 * au)))
        lp = -0.5 * e * e - ls - 0.5 * math.log(2.0 * math.pi) - sq
        return a, sg, jnp.sum(jnp.where(live, lp, 0.0), axis=0, keepdims=True)

    def q_of(h2, wcol, b):
        return jnp.sum(h2 * wcol, axis=0, keepdims=True) + b

    def softmin(q, w):
        a, b = -4.0 * q, -4.0 * w
        m = jnp.maximum(a, b)
        return -0.25 * (m + jnp.log1p(jnp.exp(-jnp.abs(a - b))))

    @pl.loop(0, nt)
    def _(i):
        @pl.loop(0, T, unroll=8)
        def _(j):
            xrow[pl.ds(j, 1), :] = tab[pl.ds(idx_s[i * T + j], 1), :]

        xt = xrow[...].T
        row8 = lax.broadcasted_iota(jnp.int32, (8, T), 0)
        row16 = lax.broadcasted_iota(jnp.int32, (16, T), 0)
        live = row8 < ACT
        eps = noise(seeds[pl.ds(i, 1), :], row16)
        lane = lax.broadcasted_iota(jnp.int32, (1, cap), 1)
        mask = jnp.concatenate(
            [jnp.where(lane < cnt_s[i * lists + k], 1.0, 0.0).astype(F32) for k in range(lists)], axis=1
        )
        alpha = jnp.exp(jnp.full((1, T), level, F32))
        b1 = pltpu.roll(xt[16:24], 7, 0)
        reward = b1[6:7]
        xa = jnp.concatenate([jnp.where(row8 == 6, 1.0, b1), xt[0:16]], axis=0)
        b2_ = pltpu.roll(xt[40:48], 7, 0)
        done = b2_[0:1]
        n_lo = jnp.where(row8 == 7, b2_, jnp.where(row8 == 6, 1.0, 0.0))
        xn = jnp.concatenate([n_lo, xt[24:40]], axis=0)

        h1, _ = act(first(0, 1, xn))
        h2, _ = layer2(0, h1)
        mean, _, ls = head_out(h2)
        a2, _, lp2 = sample(mean, ls, eps[8:16], live)
        xn = jnp.concatenate([jnp.where(live, a2, n_lo), xt[24:40]], axis=0)
        r = first(3, 5, xn)
        qs = []
        for k in range(2):
            h1, _ = act(r[k * HID : (k + 1) * HID])
            h2, _ = layer2(3 + k, h1)
            qs.append(q_of(h2, col[:, 7 + k : 8 + k], lb3_s[k]))
        y = reward + GAMMA * (1.0 - done) * (softmin(qs[0], qs[1]) - alpha * lp2)

        hi, lo = split(xa)
        xs = jnp.concatenate([hi, lo, hi], axis=0).astype(BF)
        xw = jnp.concatenate([hi, lo], axis=0).astype(BF)
        r = dot(w1all[0 : 3 * HID, :], xs)
        closs = jnp.zeros((1, T), F32)
        for k in range(2):
            h1, d1 = act(r[(1 + k) * HID : (2 + k) * HID])
            h1b = h1.astype(BF)
            h2, d2 = layer2(1 + k, h1b)
            w3 = col[:, 5 + k : 6 + k]
            dq = q_of(h2, w3, jb3_s[k]) - y
            mdq = dq * mask
            closs = closs + 0.5 * (mdq * dq)
            gcol[2 + k] += fold(h2 * mdq)
            g2 = (0.5 * w3) * mdq * d2
            gcol[k] += fold(g2)
            g2 = g2.astype(BF)
            gw2[1 + k] += dot_t(h1b, g2)
            g1 = (back2(1 + k, g2) * d1).astype(BF)
            w = dot_t(xw, g1)
            gcw1[k] += w[0:24] + w[24:48]
            gmisc[k : k + 1, :] += fold(mdq)

        h1a, d1a = act(r[0:HID])
        h1ab = h1a.astype(BF)
        h2a, d2a = layer2(0, h1ab)
        h2ab = h2a.astype(BF)
        mean, t, ls = head_out(h2ab)
        e = eps[0:8]
        a1, sg, lp = sample(mean, ls, e, live)
        xq = jnp.concatenate([jnp.where(live, a1, xa[0:8]), xt[0:16]], axis=0)
        r = first(1, 3, xq)
        qs, d1s, d2s = [], [], []
        for k in range(2):
            h1, d1 = act(r[k * HID : (k + 1) * HID])
            h2, d2 = layer2(1 + k, h1)
            qs.append(q_of(h2, col[:, 5 + k : 6 + k], jb3_s[k]))
            d1s.append(d1)
            d2s.append(d2)
        sm = softmin(qs[0], qs[1])
        p0 = 1.0 / (1.0 + jnp.exp(4.0 * (qs[0] - qs[1])))
        da = jnp.zeros((8, T), F32)
        for k, pk in enumerate((p0, 1.0 - p0)):
            g2 = ((0.5 * col[:, 5 + k : 6 + k]) * (-pk * mask) * d2s[k]).astype(BF)
            g1 = (back2(1 + k, g2) * d1s[k]).astype(BF)
            w = dot(da_w[k], g1)
            da = da + w[0:8] + w[8:16]
        ma = mask * alpha
        du = da * (1.0 - a1 * a1) + ma * (2.0 * a1)
        dls = (du * sg * e - ma) * (3.5 * (1.0 - t * t))
        do = jnp.concatenate([jnp.where(live, du, 0.0), jnp.where(live, dls, 0.0)], axis=0)
        gcol[5] += jnp.concatenate([fold(do), jnp.zeros((HID - 16, 128), F32)], axis=0)
        dob = do.astype(BF)
        gaw3[...] += dot_t(dob, h2ab)
        g2 = dot(headb[...], jnp.concatenate([dob, dob], axis=0)) * d2a
        gcol[4] += fold(g2)
        g2 = g2.astype(BF)
        gw2[0] += dot_t(h1ab, g2)
        g1 = (back2(0, g2) * d1a).astype(BF)
        w = dot_t(xw, g1)
        gaw1[...] += w[0:24] + w[24:48]
        gmisc[2:3, :] += fold(closs)
        gmisc[3:4, :] += fold(mask * (alpha * lp - sm))
        gmisc[4:5, :] += fold(mask * (lp - 6.0))
        gmisc[5:6, :] += fold(mask)


def local_grads(experience_buffer, idx, counts, seeds, params):
    (aw1, ab1, aw2, ab2, aw3, ab3, jw1, jb1, jw2, jb2, jw3, jb3, lw1, lb1, lw2, lb2, lw3, lb3, level) = params
    feats, width = experience_buffer.shape
    peers, cap = idx.shape
    slots = peers * cap
    T = min(TILE, slots)
    vm = pl.BlockSpec(memory_space=pltpu.VMEM)
    sm = pl.BlockSpec(memory_space=pltpu.SMEM)
    out = [
        jax.ShapeDtypeStruct((3, HID, HID), F32),
        jax.ShapeDtypeStruct((24, HID), F32),
        jax.ShapeDtypeStruct((2, 24, HID), F32),
        jax.ShapeDtypeStruct((16, HID), F32),
        jax.ShapeDtypeStruct((6, HID, 128), F32),
        jax.ShapeDtypeStruct((8, 128), F32),
    ]
    return pl.pallas_call(
        functools.partial(net_kernel, cap=cap, width=width, slots=slots),
        out_shape=out,
        in_specs=[sm] * 6 + [vm] * 17,
        out_specs=[vm] * 6,
        scratch_shapes=[
            pltpu.VMEM((width, 128), F32),
            pltpu.VMEM((T, 128), F32),
            pltpu.VMEM((5 * HID, 72), BF),
            pltpu.VMEM((5, 2 * HID, HID), BF),
            pltpu.VMEM((3, 2 * HID, HID), BF),
            pltpu.VMEM((32, HID), BF),
            pltpu.VMEM((HID, 32), BF),
            pltpu.VMEM((2, 16, HID), BF),
            pltpu.VMEM((HID, 128), F32),
            pltpu.VMEM((32, HID), F32),
            pltpu.VMEM((16, HID), F32),
        ],
        compiler_params=pltpu.CompilerParams(vmem_limit_bytes=60 << 20),
        name="networks",
    )(
        idx.reshape(-1), counts, level.reshape(1), ab3, jb3, lb3,
        experience_buffer, seeds.reshape(slots // T, T),
        aw1, ab1.reshape(1, HID), aw2, ab2.reshape(1, HID), aw3,
        jw1, jb1, jw2, jb2, jw3,
        lw1, lb1, lw2, lb2, lw3,
    )


def body(experience_buffer, sampled_indices, filled_lengths, randomizer_numbers, *params):
    peers, cap = sampled_indices.shape[1:]
    level = params[-1]
    message = jnp.concatenate(
        [sampled_indices[0], randomizer_numbers[0], jnp.broadcast_to(filled_lengths[0][:, None], (peers, 128))], axis=1
    )
    got = lax.all_to_all(message, "dp", split_axis=0, concat_axis=0, tiled=True)
    idx, seeds, counts = got[:, :cap], got[:, cap : 2 * cap], got[:, 2 * cap]
    gw2, gaw1, gcw1, gaw3, gcol, gmisc = local_grads(experience_buffer, idx, counts, seeds, params)
    cols = jnp.sum(gcol, axis=2)
    misc = jnp.sum(gmisc, axis=1)
    gw2, gaw1, gcw1, gaw3, cols, misc = lax.psum((gw2, gaw1, gcw1, gaw3, cols, misc), "dp")
    n = misc[5]
    inv = 1.0 / n

    def w1_of(g):
        return jnp.concatenate([g[8:24], g[7:8]], axis=0), g[0:6], g[6]

    s, _, b1 = w1_of(gaw1)
    c = [w1_of(gcw1[k]) for k in range(2)]
    outs = (
        s, b1, gw2[0], cols[4], jnp.concatenate([gaw3[0:6], gaw3[8:14]], axis=0).T, jnp.concatenate([cols[5, 0:6], cols[5, 8:14]]),
        jnp.stack([jnp.concatenate([x[0], x[1]], axis=0) for x in c]), jnp.stack([x[2] for x in c]),
        gw2[1:3], cols[0:2], cols[2:4], misc[0:2],
    )
    outs = tuple(o / n for o in outs)
    losses = jnp.stack([misc[2], misc[3], -level * misc[4]]) / n
    return outs + (-misc[4] / n, losses)


def solution(mesh):
    in_specs = (P(None, "dp"), P("dp", None, None), P("dp", None), P("dp", None, None)) + (P(),) * 19
    return jax.shard_map(body, mesh=mesh, in_specs=in_specs, out_specs=(P(),) * 14, check_vma=False)
```

time: 867 us -> 400 us (0.46)
  matrix products: 520 us -> 0 us
  Pallas kernels: 0 us -> 98.9 us
  waiting for transfers between devices: 156 us -> 238 us
  blocking collectives: 40.2 us -> 0 us
  local copies, waits for them, and re-layouts: 50.3 us -> 14 us
  other arithmetic: 54.4 us -> 22.2 us
    dot_general x49 -> x0, matrix products: 520 us -> none  [the longest x39 426 us: linear(): return jnp.dot(inputs, weight, precision=PRECISE) + offset]
    psum x1 -> x2, waiting for transfers between devices: 122 us -> 235 us  [body(): lax.psum((gw2, gaw1, gcw1, gaw3, cols, misc), 'dp')]
    pallas_call x0 -> x1, Pallas kernels: none -> 98.9 us  [local_grads(): pl.pallas_call(functools.partial(net_kernel, cap=cap, width=width, slots=...]
    psum x1 -> x0, blocking collectives: 40.2 us -> none  [body(): lax.psum((actor_local[0], actor_local[1], actor_local[2], actor_local[3],...]
    gather x2 -> x0, local copies, waits for them, and re-layouts: 34.1 us -> none  [body(): jnp.take(experience_buffer, asked_rows.reshape(-1), axis=1)]
    all_to_all x2 -> x1, waiting for transfers between devices: 33.3 us -> 2.6 us  [body(): got = lax.all_to_all(message, 'dp', split_axis=0, concat_axis=0, tiled=True)]
    reduce_sum x5 -> x2, other arithmetic: 26.7 us -> 3.31 us  [the longest x1 2.01 us: body(): cols = jnp.sum(gcol, axis=2)]
    div x13 -> x10, other arithmetic: 19.4 us -> 16.3 us  [the longest x9 15.1 us: body(): outs = tuple((o / n for o in outs))]
  transfers between devices with their start and end apart: 3 -> 3, of which waited for: 2 -> 3; matrix products, arithmetic and copies ran while one was open for 2% -> 6% of each run, Pallas kernels for 0% -> 0%
where the time goes in v1:
time: 400 us; the launch traced here: 398 us
  waiting for transfers between devices  238 us (60%)
  Pallas kernels  98.9 us (25%)
  other arithmetic  22.2 us (6%)
  between operations  17.8 us (4%)
  local copies, waits for them, and re-layouts  14 us (4%)
  starting transfers between devices  7.38 us (2%)
    psum x2, waiting for transfers between devices, body(): lax.psum((gw2, gaw1, gcw1, gaw3, cols, misc), 'dp')  235 us
    pallas_call x1, Pallas kernels, local_grads(): pl.pallas_call(functools.partial(net_kernel, cap=cap, width=width, slots=...  98.9 us
    div x9, other arithmetic, body(): outs = tuple((o / n for o in outs))  15.1 us
  transfers between devices with their start and end apart: 3, of which 3 were waited for; matrix products, arithmetic and copies ran while one was open for 6% of the time, Pallas kernels for 0%

profile of v1, /device:TPU:0, one launch (start us, length us, event | category | flops | bytes accessed | tf_op | source)
XLA Modules:
  0.0 398.2 jit_solution(8086663912336826204)
XLA Ops:
  7.9 0.8 pad_add_fusion
  9.4 7.3 %all-to-all-start = ((s32[32,1,640]{2,1,0:T(1,128)}), s32[32,1,640]{2,1,0:T(1,128)S(1)}, u32[]{:S(2)}, u32[]{:S(2)}) async-start(s32[32,1,640]{2,1,0:T(1,128)} %all_to_all.8), calls=%async_computation | async-start | bytes 163840 | tf_op jit(solution)/shard_map/all_to_all | solution.py:324
  17.4 1.5 copy.45.aw3
  18.9 1.4 copy.46.jw1
  20.3 1.4 copy.47.lw1
  21.7 2.6 all-to-all-done
  26.2 98.9 %networks.1 = (f32[3,256,256]{2,1,0:T(8,128)}, f32[24,256]{1,0:T(8,128)}, f32[2,24,256]{2,1,0:T(8,128)}, f32[16,256]{1,0:T(8,128)}, f32[6,256,128]{2,1,0:T(8,128)}, /*index=5*/f32[8,128]{1,0:T(8,128)}) custom-call(s32[8192]{0:T(1024)} %bitcast.48, s32[32]{0:T(128)} %slice_reduce_fusion.cnt_s, f32[1]{0:T(128)} %bitcast.45.alpha_s, f32[12]{0:T(128)} %hb3_s.1, ...), custom_call_target="tpu_custom_call" | custom-call | tf_op jit(solution)/shard_map/networks/pallas_call | solution.py:289
  125.1 2.0 reduce_sum.19
  127.1 1.3 reduce_sum.18
  129.2 121.0 %all-reduce.6.cloned.1.call-done = (f32[24,256]{1,0:T(8,128)}, f32[8]{0:T(128)}, f32[6,256]{1,0:T(8,128)}, f32[16,256]{1,0:T(8,128)}, f32[2,24,256]{2,1,0:T(8,128)}) async-done(((f32[24,256]{1,0:T(8,128)}, f32[8]{0:T(128)}, f32[6,256]{1,0:T(8,128)}, f32[16,256]{1,0:T(8,128)}, f32[2,24,256]{2,1,0:T(8,128)}), (f32[24,256]{1,0:T(8,128)}, f32[8]{0:T(128)}, f32[6,256]{1,0:T(8,128)}, f32[16,256]{1,0:T(8,128)}, ...) | async-done | bytes 96304 | tf_op jit(solution)/shard_map/psum | solution.py:329
  250.1 0.8 slice_bitcast_fusion.6
  252.4 1.3 fusion.5
  253.7 1.8 fusion.4
  255.5 2.0 slice_divide_fusion.5
  261.5 0.8 slice_bitcast_fusion.10
  263.0 1.2 maximum_divide_fusion.5
  264.3 1.2 maximum_divide_fusion.4
  265.5 1.2 fusion.1
  266.7 1.2 maximum_divide_fusion.1
  268.0 1.9 slice_divide_fusion.4
  269.9 2.0 slice_divide_fusion.2
  271.9 113.6 %all-reduce.4.cloned.1.call-done = f32[3,256,256]{2,1,0:T(8,128)} async-done(((f32[3,256,256]{2,1,0:T(8,128)}), f32[3,256,256]{2,1,0:T(8,128)}) %all-reduce.4.cloned.1.call-update) | async-done | bytes 786448 | tf_op jit(solution)/shard_map/psum | solution.py:329
  385.4 2.5 slice_divide_fusion
  388.0 2.3 fusion
  (18 shorter events, 8.3 us)
Async XLA Ops:
  9.4 14.9 %all-to-all-start = ((s32[32,1,640]{2,1,0:T(1,128)}), s32[32,1,640]{2,1,0:T(1,128)S(1)}, u32[]{:S(2)}, u32[]{:S(2)}) async-start(s32[32,1,640]{2,1,0:T(1,128)} %all_to_all.8), calls=%async_computation | async-start | bytes 163840 | tf_op jit(solution)/shard_map/all_to_all | solution.py:324
  16.7 233.5 %all-reduce.6.cloned.1.call-start = ((), (), s32[]{:S(2)}) async-start(), calls=%async_computation.2 | async-start | bytes 197632 | tf_op jit(solution)/shard_map/psum | solution.py:329
  128.4 257.0 %all-reduce.4.cloned.1.call-start = ((), (), s32[]{:S(2)}) async-start(), calls=%async_computation.1 | async-start | bytes 1572864 | tf_op jit(solution)/shard_map/psum | solution.py:329
Sparse Core Ops, SparseCore 0:
  128.5 121.5 all-reduce.5
  255.3 130.0 all-reduce.3

commit v2 on v1

--- a/solution.py
+++ b/solution.py
@@ -14,6 +14,12 @@
 GAMMA = 0.99
 PRIME = 65521
 TILE = 1024
+R_AW1 = 6 * HID
+R_CW1 = R_AW1 + 48
+R_AW3 = R_CW1 + 96
+R_COL = R_AW3 + 32
+R_MISC = R_COL + 16
+R_END = R_MISC + 8
 BF = jnp.bfloat16
 F32 = jnp.float32
 
@@ -58,8 +64,8 @@
     aw1, ab1, aw2, ab2, aw3,
     jw1, jb1, jw2, jb2, jw3,
     lw1, lb1, lw2, lb2, lw3,
-    gw2, gaw1, gcw1, gaw3, gcol, gmisc,
-    tab, xrow, w1all, f2, b2, head, headb, da_w, col, tmp, rowbuf,
+    packed,
+    gw2, gaw1, gcw1, gaw3, gcol, gmisc, tab, xrow, w1all, f2, b2, head, headb, da_w, col, tmp, rowbuf,
     *, cap, width, slots,
 ):
     T = min(TILE, slots)
@@ -269,8 +275,180 @@
         gmisc[4:5, :] += fold(mask * (lp - 6.0))
         gmisc[5:6, :] += fold(mask)
 
-
-def local_grads(experience_buffer, idx, counts, seeds, params):
+    for m in range(3):
+        for h in range(2):
+            packed[(2 * m + h) * HID : (2 * m + h + 1) * HID, :] = gw2[m, :, h * 128 : (h + 1) * 128]
+    lane = lax.broadcasted_iota(jnp.int32, (HID, 128), 1)
+    cols = jnp.zeros((HID, 128), F32)
+    for k in range(6):
+        cols = jnp.where(lane == k, jnp.sum(gcol[k], axis=1, keepdims=True), cols)
+    for h in range(2):
+        packed[R_AW1 + 24 * h : R_AW1 + 24 * (h + 1), :] = gaw1[:, h * 128 : (h + 1) * 128]
+        for k in range(2):
+            at = R_CW1 + 48 * k + 24 * h
+            packed[at : at + 24, :] = gcw1[k, :, h * 128 : (h + 1) * 128]
+        packed[R_AW3 + 16 * h : R_AW3 + 16 * (h + 1), :] = gaw3[:, h * 128 : (h + 1) * 128]
+        packed[R_COL + 8 * h : R_COL + 8 * (h + 1), :] = cols[h * 128 : (h + 1) * 128].T[0:8]
+    packed[R_MISC : R_MISC + 8, :] = gmisc[...]
+    packed[R_END:, :] = jnp.zeros((packed.shape[0] - R_END, 128), F32)
+
+
+def split_sizes(n):
+    sizes = [2]
+    n //= 2
+    while n > 1:
+        f = 4 if n % 4 == 0 else n if n < 4 else 2
+        sizes.append(f)
+        n //= f
+    return sizes
+
+
+def sum_kernel(sizes, mine, out, full, *rest):
+    ns = len(sizes)
+    got, part, sems = rest[:ns], rest[ns : 2 * ns], rest[2 * ns]
+    me = lax.axis_index("dp")
+    digits, strides, st = [], [], 1
+    for f in sizes:
+        digits.append(lax.rem(me // st, f))
+        strides.append(st)
+        st *= f
+
+    def member(s, k):
+        d = lax.rem(digits[s] + k, sizes[s])
+        return d, me + (d - digits[s]) * strides[s]
+
+    barrier = pltpu.get_barrier_semaphore()
+    count = 0
+    for s in range(ns):
+        for k in range(1, sizes[s]):
+            pl.semaphore_signal(barrier, inc=1, device_id=(member(s, k)[1],), device_id_type=pl.DeviceIdType.MESH)
+            count += 1
+    pl.semaphore_wait(barrier, count)
+
+    def send(src, dst, s, k, phase):
+        return pltpu.make_async_remote_copy(
+            src_ref=src, dst_ref=dst, send_sem=sems.at[phase, s, k, 0], recv_sem=sems.at[phase, s, k, 1],
+            device_id=(member(s, k)[1],), device_id_type=pl.DeviceIdType.MESH,
+        )
+
+    done = []
+    cur, size = mine, mine.shape[0]
+    for s in range(ns):
+        f = sizes[s]
+        blk = size // f
+        copies = []
+        for k in range(1, f):
+            d, _ = member(s, k)
+            c = send(cur.at[pl.ds(d * blk, blk)], got[s].at[k - 1], s, k, 0)
+            c.start()
+            copies.append(c)
+        acc = cur[pl.ds(digits[s] * blk, blk)]
+        for k in range(1, f):
+            copies[k - 1].wait_recv()
+            acc = acc + got[s][k - 1]
+        part[s][...] = acc
+        done += copies
+        cur, size = part[s], blk
+    at = 0
+    span = mine.shape[0]
+    for s in range(ns):
+        span //= sizes[s]
+        at = at + digits[s] * span
+    full[pl.ds(at, 1)] = part[ns - 1][...]
+    span = 1
+    for s in reversed(range(ns)):
+        copies = []
+        for k in range(1, sizes[s]):
+            c = send(full.at[pl.ds(at, span)], full.at[pl.ds(at, span)], s, k, 1)
+            c.start()
+            copies.append(c)
+        for c in copies:
+            c.wait_recv()
+        done += copies
+        at = at - digits[s] * span
+        span *= sizes[s]
+    out[...] = full[...]
+    for c in done:
+        c.wait_send()
+
+
+def sum_over_devices(packed, n):
+    sizes = split_sizes(n)
+    rows = packed.shape[0] // n
+    mine = packed.reshape(n, rows, 128)
+    got, part, size = [], [], n
+    for f in sizes:
+        size //= f
+        got.append(pltpu.VMEM((f - 1, size, rows, 128), F32))
+        part.append(pltpu.VMEM((size, rows, 128), F32))
+    vm = pl.BlockSpec(memory_space=pltpu.VMEM)
+    out = pl.pallas_call(
+        functools.partial(sum_kernel, sizes),
+        out_shape=jax.ShapeDtypeStruct((n, rows, 128), F32),
+        in_specs=[vm],
+        out_specs=vm,
+        scratch_shapes=[pltpu.VMEM((n, rows, 128), F32)] + got + part + [pltpu.SemaphoreType.DMA((2, len(sizes), max(sizes), 2))],
+        compiler_params=pltpu.CompilerParams(collective_id=1, has_side_effects=True, vmem_limit_bytes=40 << 20),
+        name="sum_over_devices",
+    )(mine)
+    return out.reshape(packed.shape)
+
+
+def finish_kernel(level_s, g, aw1, ab1, aw2, ab2, aw3, ab3, cw1, cb1, cw2, cb2, cw3, cb3, da, losses, tmp):
+    misc = jnp.sum(g[R_MISC : R_MISC + 8, :], axis=1, keepdims=True)
+    n = misc[5:6]
+    inv = 1.0 / n
+
+    def rows(at, count):
+        return jnp.concatenate([g[at : at + count, :], g[at + count : at + 2 * count, :]], axis=1) * inv
+
+    aw2[...] = rows(0, HID)
+    cw2[0] = rows(2 * HID, HID)
+    cw2[1] = rows(4 * HID, HID)
+    w = rows(R_AW1, 24)
+    aw1[0:16, :] = w[8:24]
+    aw1[16:17, :] = w[7:8]
+    ab1[...] = w[6:7]
+    for k in range(2):
+        w = rows(R_CW1 + 48 * k, 24)
+        cw1[k, 0:16, :] = w[8:24]
+        cw1[k, 16:17, :] = w[7:8]
+        cw1[k, 17:23, :] = w[0:6]
+        cb1[k : k + 1, :] = w[6:7]
+    w = rows(R_AW3, 16)
+    tmp[0:8, :] = w[0:8]
+    tmp[6:12, :] = w[8:14]
+    aw3[...] = tmp[...].T[:, 0:12]
+    c = rows(R_COL, 8)
+    cb2[...] = c[0:2]
+    cw3[...] = c[2:4]
+    ab2[...] = c[4:5]
+    ab3[...] = jnp.concatenate([c[5:6, 0:6], c[5:6, 8:14]], axis=1)
+    m = misc * inv
+    cb3[...] = jnp.concatenate([m[0:1], m[1:2]], axis=1)
+    da[...] = -m[4:5]
+    losses[...] = jnp.concatenate([m[2:3], m[3:4], -level_s[0] * m[4:5]], axis=1)
+
+
+def finish(total, level):
+    vm = pl.BlockSpec(memory_space=pltpu.VMEM)
+    shapes = [
+        (OBS, HID), (1, HID), (HID, HID), (1, HID), (HID, 12), (1, 12),
+        (2, 23, HID), (2, HID), (2, HID, HID), (2, HID), (2, HID), (1, 2), (1, 1), (1, 3),
+    ]
+    outs = pl.pallas_call(
+        finish_kernel,
+        out_shape=[jax.ShapeDtypeStruct(x, F32) for x in shapes],
+        in_specs=[pl.BlockSpec(memory_space=pltpu.SMEM), vm],
+        out_specs=[vm] * len(shapes),
+        scratch_shapes=[pltpu.VMEM((16, HID), F32)],
+        name="finish",
+    )(level.reshape(1), total)
+    final = [(OBS, HID), (HID,), (HID, HID), (HID,), (HID, 12), (12,), (2, 23, HID), (2, HID), (2, HID, HID), (2, HID), (2, HID), (2,), (), (3,)]
+    return tuple(o.reshape(x) for o, x in zip(outs, final))
+
+
+def local_grads(experience_buffer, idx, counts, seeds, params, packed_rows):
     (aw1, ab1, aw2, ab2, aw3, ab3, jw1, jb1, jw2, jb2, jw3, jb3, lw1, lb1, lw2, lb2, lw3, lb3, level) = params
     feats, width = experience_buffer.shape
     peers, cap = idx.shape
@@ -278,20 +456,18 @@
     T = min(TILE, slots)
     vm = pl.BlockSpec(memory_space=pltpu.VMEM)
     sm = pl.BlockSpec(memory_space=pltpu.SMEM)
-    out = [
-        jax.ShapeDtypeStruct((3, HID, HID), F32),
-        jax.ShapeDtypeStruct((24, HID), F32),
-        jax.ShapeDtypeStruct((2, 24, HID), F32),
-        jax.ShapeDtypeStruct((16, HID), F32),
-        jax.ShapeDtypeStruct((6, HID, 128), F32),
-        jax.ShapeDtypeStruct((8, 128), F32),
-    ]
     return pl.pallas_call(
         functools.partial(net_kernel, cap=cap, width=width, slots=slots),
-        out_shape=out,
+        out_shape=jax.ShapeDtypeStruct((packed_rows, 128), F32),
         in_specs=[sm] * 6 + [vm] * 17,
-        out_specs=[vm] * 6,
+        out_specs=vm,
         scratch_shapes=[
+            pltpu.VMEM((3, HID, HID), F32),
+            pltpu.VMEM((24, HID), F32),
+            pltpu.VMEM((2, 24, HID), F32),
+            pltpu.VMEM((16, HID), F32),
+            pltpu.VMEM((6, HID, 128), F32),
+            pltpu.VMEM((8, 128), F32),
             pltpu.VMEM((width, 128), F32),
             pltpu.VMEM((T, 128), F32),
             pltpu.VMEM((5 * HID, 72), BF),
@@ -323,26 +499,8 @@
     )
     got = lax.all_to_all(message, "dp", split_axis=0, concat_axis=0, tiled=True)
     idx, seeds, counts = got[:, :cap], got[:, cap : 2 * cap], got[:, 2 * cap]
-    gw2, gaw1, gcw1, gaw3, gcol, gmisc = local_grads(experience_buffer, idx, counts, seeds, params)
-    cols = jnp.sum(gcol, axis=2)
-    misc = jnp.sum(gmisc, axis=1)
-    gw2, gaw1, gcw1, gaw3, cols, misc = lax.psum((gw2, gaw1, gcw1, gaw3, cols, misc), "dp")
-    n = misc[5]
-    inv = 1.0 / n
-
-    def w1_of(g):
-        return jnp.concatenate([g[8:24], g[7:8]], axis=0), g[0:6], g[6]
-
-    s, _, b1 = w1_of(gaw1)
-    c = [w1_of(gcw1[k]) for k in range(2)]
-    outs = (
-        s, b1, gw2[0], cols[4], jnp.concatenate([gaw3[0:6], gaw3[8:14]], axis=0).T, jnp.concatenate([cols[5, 0:6], cols[5, 8:14]]),
-        jnp.stack([jnp.concatenate([x[0], x[1]], axis=0) for x in c]), jnp.stack([x[2] for x in c]),
-        gw2[1:3], cols[0:2], cols[2:4], misc[0:2],
-    )
-    outs = tuple(o / n for o in outs)
-    losses = jnp.stack([misc[2], misc[3], -level * misc[4]]) / n
-    return outs + (-misc[4] / n, losses)
+    packed = local_grads(experience_buffer, idx, counts, seeds, params, peers * 8 * (-(-R_END // (8 * peers))))
+    return finish(sum_over_devices(packed, peers), level)
 
 
 def solution(mesh):

time: 400 us -> 153 us (0.38)
  waiting for transfers between devices: 238 us -> 2.65 us
  Pallas kernels: 98.9 us -> 128 us
  other arithmetic: 22.2 us -> 0.78 us
  between operations: 17.8 us -> 1.33 us
    psum x2 -> x0, waiting for transfers between devices: 235 us -> none  [body(): lax.psum((gw2, gaw1, gcw1, gaw3, cols, misc), 'dp')]
    pallas_call x0 -> x2, Pallas kernels: none -> 28.4 us  [the longest x1 26.2 us: sum_over_devices(): pl.pallas_call(functools.partial(sum_kernel, sizes), out_shape=jax.ShapeD...]
    div x10 -> x0, other arithmetic: 16.3 us -> none  [the longest x9 15.1 us: body(): outs = tuple((o / n for o in outs))]
    slice x6 -> x0, local copies, waits for them, and re-layouts: 4.96 us -> none  [the longest x4 2.95 us: w1_of(): return (jnp.concatenate([g[8:24], g[7:8]], axis=0), g[0:6], g[6])]
    unnamed x6 -> x11, local copies, waits for them, and re-layouts: 5.59 us -> 10.1 us
  transfers between devices with their start and end apart: 3 -> 1, of which waited for: 3 -> 1; matrix products, arithmetic and copies ran while one was open for 6% -> 3% of each run, Pallas kernels for 0% -> 0%
where the time goes in v2:
time: 153 us
  Pallas kernels  128 us (84%)
  local copies, waits for them, and re-layouts  12.7 us (8%)
  starting transfers between devices  7.3 us (5%)
  waiting for transfers between devices  2.65 us (2%)
    pallas_call x1, Pallas kernels, local_grads(): pl.pallas_call(functools.partial(net_kernel, cap=cap, width=width, slots=...  99.6 us
    pallas_call x1, Pallas kernels, sum_over_devices(): pl.pallas_call(functools.partial(sum_kernel, sizes), out_shape=jax.ShapeD...  26.2 us
    unnamed x11, local copies, waits for them, and re-layouts  10.1 us
    all_to_all x1, starting transfers between devices, body(): got = lax.all_to_all(message, 'dp', split_axis=0, concat_axis=0, tiled=True)  7.3 us
  transfers between devices with their start and end apart: 1, of which 1 were waited for; matrix products, arithmetic and copies ran while one was open for 3% of the time, Pallas kernels for 0%

profile of v2, /device:TPU:0, one launch (start us, length us, event | category | flops | bytes accessed | tf_op | source)
XLA Modules:
  0.0 152.8 jit_solution(6388813041384231222)
XLA Ops:
  0.6 0.7 broadcast_in_dim.8
  1.4 0.8 pad_add_fusion
  2.2 0.7 all_to_all.8
  2.8 7.3 %all-to-all-start = ((s32[32,1,640]{2,1,0:T(1,128)}), s32[32,1,640]{2,1,0:T(1,128)S(1)}, u32[]{:S(2)}, u32[]{:S(2)}) async-start(s32[32,1,640]{2,1,0:T(1,128)} %all_to_all.8), calls=%async_computation | async-start | bytes 163840 | tf_op jit(solution)/shard_map/all_to_all | solution.py:500
  10.8 1.4 copy.48.jw1
  12.2 1.4 copy.49.lw1
  13.6 1.5 copy.47.aw3
  15.1 2.7 %all-to-all-done = s32[32,1,640]{2,1,0:T(1,128)S(1)} async-done(((s32[32,1,640]{2,1,0:T(1,128)}), s32[32,1,640]{2,1,0:T(1,128)S(1)}, u32[]{:S(2)}, u32[]{:S(2)}) %all-to-all-start) | async-done | bytes 81952 | tf_op jit(solution)/shard_map/all_to_all | solution.py:500
  17.8 0.6 slice_reduce_fusion.cnt_s
  18.4 0.6 reshape.73.seeds
  19.0 0.6 copy.53
  19.7 99.6 %networks.1 = f32[1792,128]{1,0:T(8,128)} custom-call(s32[8192]{0:T(1024)} %bitcast.26, s32[32]{0:T(128)} %slice_reduce_fusion.cnt_s, f32[1]{0:T(128)} %bitcast.20.alpha_s, f32[12]{0:T(128)} %hb3_s.1, f32[2]{0:T(128)} %jb3_s.1, f32[2]{0:T(128)} %lb3_s.1, f32[42,16384]{1,0:T(8,128)} %buf.1, s32[8,1024]{1,0:T(8,128)} %reshape.73.seeds, f32[17,256]{1,0:T(8,128)} %aw1.1, ...), custom_call_target="tpu_custom_call" | custom-call | tf_op jit(solution)/shard_map/networks/pallas_call | solution.py:459
  119.3 0.0 copy-start.1
  119.3 1.2 copy-done.1
  120.4 26.2 %sum_over_devices.1 = f32[32,56,128]{2,1,0:T(8,128)S(1)} custom-call(f32[32,56,128]{2,1,0:T(8,128)S(1)} %bitcast.23), custom_call_target="tpu_custom_call" | custom-call | tf_op jit(solution)/shard_map/sum_over_devices/pallas_call | solution.py:385
  146.6 0.0 copy-start
  146.6 0.9 copy-done
  147.5 2.2 %finish.1 = (f32[17,256]{1,0:T(8,128)}, f32[1,256]{1,0:T(1,128)}, f32[256,256]{1,0:T(8,128)}, f32[1,256]{1,0:T(1,128)}, f32[256,12]{1,0:T(8,128)}, /*index=5*/f3...) custom-call(f32[1]{0:T(128)} %bitcast.21.level_s, ...), custom_call_target="tpu_custom_call" | custom-call | tf_op jit(solution)/shard_map/finish/pallas_call | solution.py:439
  149.8 1.6 %copy.50 = f32[256,12]{0,1:T(8,128)} copy(f32[256,12]{1,0:T(8,128)} %get-tuple-element.74) | data formatting | bytes 24576
  151.4 1.4 copy.51
  (2 shorter events, 0.0 us)
Async XLA Ops:
  2.8 14.9 %all-to-all-start = ((s32[32,1,640]{2,1,0:T(1,128)}), s32[32,1,640]{2,1,0:T(1,128)S(1)}, u32[]{:S(2)}, u32[]{:S(2)}) async-start(s32[32,1,640]{2,1,0:T(1,128)} %all_to_all.8), calls=%async_computation | async-start | bytes 163840 | tf_op jit(solution)/shard_map/all_to_all | solution.py:500
  119.3 1.2 copy-start.1
  146.6 0.9 copy-start

commit v3 on v2

v3 whole, which is shorter than its diff:
```python
import functools
import math

import jax
import jax.numpy as jnp
from jax import lax
from jax.experimental import pallas as pl
from jax.experimental.pallas import tpu as pltpu
from jax.sharding import PartitionSpec as P

OBS = 17
ACT = 6
HID = 256
GAMMA = 0.99
PRIME = 65521
TILE = 1024
R_AW1 = 6 * HID
R_CW1 = R_AW1 + 48
R_AW3 = R_CW1 + 96
R_COL = R_AW3 + 32
R_AB3 = R_COL + 16
R_MISC = R_AB3 + 16
R_END = R_MISC + 8
BF = jnp.bfloat16
F32 = jnp.float32


def dot(a, b):
    return jnp.dot(a, b, preferred_element_type=F32)


def dot_t(a, b):
    return lax.dot_general(a, b, (((1,), (1,)), ((), ())), preferred_element_type=F32)


def split(x):
    hi = x.astype(BF).astype(F32)
    return hi, x - hi


def fold_prime(x):
    return (x >> 16) * 15 + (x & 65535)


def below_prime(x):
    return jnp.where(x >= PRIME, x - PRIME, x)


def noise(seeds, rows):
    comp = jnp.where(rows >= 8, rows - 2, rows)
    z = below_prime(fold_prime(seeds))
    h0 = below_prime(fold_prime(z * 257 + comp * 7919 + 1))
    h1 = below_prime(fold_prime(fold_prime(h0 * 32749 + 12345)))
    h2 = below_prime(fold_prime(fold_prime(h1 * 32749 + 54321)))
    u1 = (h1.astype(F32) + 0.5) * (1.0 / PRIME)
    x = jnp.abs((2 * h2 + (1 - PRIME)).astype(F32)) * (math.pi / PRIME) - 0.5 * math.pi
    x2 = x * x
    p = -1.0 / 39916800.0
    for c in (1.0 / 362880.0, -1.0 / 5040.0, 1.0 / 120.0, -1.0 / 6.0, 1.0):
        p = p * x2 + c
    return jnp.sqrt(-2.0 * jnp.log(u1)) * (p * x)


def fold(x):
    return functools.reduce(lambda a, b: a + b, [x[:, k * 128 : (k + 1) * 128] for k in range(x.shape[1] // 128)])


def message_rows(cap):
    return -(-cap // 128)


def prepare_kernel(
    idx_h, seed_h, cnt_h, buf_h, aw2_h, jw2_h, lw2_h,
    aw1, ab1, ab2, aw3, ab3, jw1, jb1, jb2, jw3, jb3, lw1, lb1, lb2, lw3, lb3, level,
    tab, got, idx_s, w1all, f2, b2, head, headb, da_w, qw, col, scale,
    idx_v, seed_v, cnt_v, buf, w2, msg, land, flat, tmp, rowbuf, in_sems, sems,
    *, n, cap,
):
    me = lax.axis_index("dp")
    rows = message_rows(cap)
    part = min(cap, 128)
    width = buf.shape[1]
    loads = [
        pltpu.make_async_copy(src, dst, in_sems.at[k])
        for k, (src, dst) in enumerate(
            ((idx_h, idx_v), (seed_h, seed_v), (cnt_h, cnt_v), (buf_h, buf), (aw2_h, w2.at[0]), (jw2_h, w2.at[pl.ds(1, 2)]), (lw2_h, w2.at[pl.ds(3, 2)]))
        )
    ]
    for c in loads:
        c.start()
    barrier = pltpu.get_barrier_semaphore()

    @pl.loop(1, n)
    def _(k):
        pl.semaphore_signal(barrier, inc=1, device_id=(lax.rem(me + k, n),), device_id_type=pl.DeviceIdType.MESH)

    for c in loads[:3]:
        c.wait()
    msg[...] = jnp.zeros_like(msg)
    for r in range(rows):
        msg[:, r, 0:part] = idx_v[0, :, r * part : (r + 1) * part]
        msg[:, rows + r, 0:part] = seed_v[0, :, r * part : (r + 1) * part]
    diag = lax.broadcasted_iota(jnp.int32, (n, n), 0) == lax.broadcasted_iota(jnp.int32, (n, n), 1)
    counts = jnp.sum(jnp.where(diag, cnt_v[...].astype(F32), 0.0), axis=1, keepdims=True)
    msg[:, 2 * rows, :] = jnp.broadcast_to(counts, (n, 128)).astype(jnp.int32)
    pl.semaphore_wait(barrier, n - 1)

    def copy(k):
        return pltpu.make_async_remote_copy(
            src_ref=msg.at[lax.rem(me + k, n)], dst_ref=land.at[k], send_sem=sems.at[0, k], recv_sem=sems.at[1, k],
            device_id=(lax.rem(me + k, n),), device_id_type=pl.DeviceIdType.MESH,
        )

    @pl.loop(1, n)
    def _(k):
        copy(k).start()

    loads[3].wait()

    @pl.loop(0, width // 128, unroll=4)
    def _(c):
        blk = buf[:, pl.ds(pl.multiple_of(c * 128, 128), 128)]
        tab[pl.ds(pl.multiple_of(c * 128, 128), 128), 0:42] = blk.T

    for c in loads[4:]:
        c.wait()
    for l, (w1, b1, k) in enumerate(((aw1, ab1, None), (jw1, jb1, 0), (jw1, jb1, 1), (lw1, lb1, 0), (lw1, lb1, 1))):
        if k is None:
            tmp[0:6, :] = jnp.zeros((6, HID), F32)
            tmp[6:7, :] = b1[...]
            tmp[7:8, :] = w1[16:17, :]
            tmp[8:24, :] = w1[0:16, :]
        else:
            tmp[0:6, :] = w1[17:23, k, :]
            tmp[6:7, :] = b1[k : k + 1, :]
            tmp[7:8, :] = w1[16:17, k, :]
            tmp[8:24, :] = w1[0:16, k, :]
        hi, lo = split(0.5 * tmp[0:24, :])
        w1all[l * HID : (l + 1) * HID, :] = jnp.concatenate([hi, hi, lo], axis=0).T.astype(BF)
        if l in (1, 2):
            hi, lo = split(tmp[0:8, :])
            da_w[l - 1] = jnp.concatenate([hi, lo], axis=0).astype(BF)
    for l in range(5):
        w = 0.5 * w2[l]
        hi, lo = split(w)
        f2[l, 0:HID, :] = hi.T.astype(BF)
        f2[l, HID:, :] = lo.T.astype(BF)
        if l < 3:
            if l > 0:
                hi, lo = split(w * (0.5 * jw3[l - 1 : l, :]))
            b2[l, 0:HID, :] = hi.astype(BF)
            b2[l, HID:, :] = lo.astype(BF)
    tmp[0:12, :] = aw3[...]
    r8 = lax.broadcasted_iota(jnp.int32, (8, HID), 0)
    w_head = jnp.concatenate([jnp.where(r8 < 6, tmp[0:8, :], 0.0), jnp.where(r8 < 6, tmp[6:14, :], 0.0)], axis=0)
    hi, lo = split(w_head)
    head[...] = jnp.concatenate([hi, lo], axis=0).astype(BF)
    headb[...] = (0.5 * jnp.concatenate([hi, lo], axis=0)).T.astype(BF)
    for k in range(4):
        w3 = jw3[k : k + 1, :] if k < 2 else lw3[k - 2 : k - 1, :]
        hi, lo = split(w3)
        qw[k] = jnp.concatenate([jnp.where(r8 == 0, hi, 0.0), jnp.where(r8 == 0, lo, 0.0)], axis=0).astype(BF)
    rowbuf[...] = jnp.zeros_like(rowbuf)
    rowbuf[0:1, :] = 0.5 * ab2[...]
    rowbuf[1:3, :] = 0.5 * jb2[...]
    rowbuf[3:5, :] = 0.5 * lb2[...]
    lane12 = lax.broadcasted_iota(jnp.int32, (1, HID), 1)
    hb = jnp.zeros((1, HID), F32)
    for k in range(12):
        hb = jnp.where(lane12 == (k if k < 6 else k + 2), ab3[k], hb)
    rowbuf[5:6, :] = hb
    col[...] = rowbuf[...].T
    scale[...] = jnp.zeros_like(scale)
    scale[0:2, :] = 0.5 * jw3[...]

    land[0] = msg[me]

    @pl.loop(1, n)
    def _(k):
        copy(k).wait()

    @pl.loop(0, n)
    def _(k):
        got[lax.rem(me - k + n, n)] = land[k]

    for r in range(rows):
        flat[:, r, :] = got[:, r, :]
    c = pltpu.make_async_copy(flat, idx_s, in_sems.at[0])
    c.start()
    c.wait()


def prepare(experience_buffer, sampled, seeds, counts, params):
    (aw1, ab1, aw2, ab2, aw3, ab3, jw1, jb1, jw2, jb2, jw3, jb3, lw1, lb1, lw2, lb2, lw3, lb3, level) = params
    feats, width = experience_buffer.shape
    _, n, cap = sampled.shape
    rows = message_rows(cap)
    vm = pl.BlockSpec(memory_space=pltpu.VMEM)
    sm = pl.BlockSpec(memory_space=pltpu.SMEM)
    hbm = pl.BlockSpec(memory_space=pl.ANY)
    out = [
        pltpu.VMEM((width, 128), F32),
        pltpu.VMEM((n, 8, 128), jnp.int32),
        pltpu.SMEM((n, rows, 128), jnp.int32),
        pltpu.VMEM((5 * HID, 72), BF),
        pltpu.VMEM((5, 2 * HID, HID), BF),
        pltpu.VMEM((3, 2 * HID, HID), BF),
        pltpu.VMEM((32, HID), BF),
        pltpu.VMEM((HID, 32), BF),
        pltpu.VMEM((2, 16, HID), BF),
        pltpu.VMEM((4, 16, HID), BF),
        pltpu.VMEM((HID, 8), F32),
        pltpu.VMEM((8, HID), F32),
    ]
    return pl.pallas_call(
        functools.partial(prepare_kernel, n=n, cap=cap),
        out_shape=out,
        in_specs=[hbm] * 7 + [vm] * 4 + [sm] + [vm] * 4 + [sm] + [vm] * 4 + [sm] * 2,
        out_specs=[vm, vm, sm] + [vm] * 9,
        scratch_shapes=[
            pltpu.VMEM((1, n, cap), jnp.int32),
            pltpu.VMEM((1, n, cap), jnp.int32),
            pltpu.VMEM((1, n), jnp.int32),
            pltpu.VMEM((feats, width), F32),
            pltpu.VMEM((5, HID, HID), F32),
            pltpu.VMEM((n, 8, 128), jnp.int32),
            pltpu.VMEM((n, 8, 128), jnp.int32),
            pltpu.VMEM((n, rows, 128), jnp.int32),
            pltpu.VMEM((24, HID), F32),
            pltpu.VMEM((8, HID), F32),
            pltpu.SemaphoreType.DMA((7,)),
            pltpu.SemaphoreType.DMA((2, n)),
        ],
        compiler_params=pltpu.CompilerParams(collective_id=2, has_side_effects=True, vmem_limit_bytes=24 << 20),
        name="exchange_and_prepare",
    )(
        sampled, seeds, counts, experience_buffer, aw2, jw2, lw2,
        aw1, ab1.reshape(1, HID), ab2.reshape(1, HID), aw3.T, ab3,
        jw1.transpose(1, 0, 2), jb1, jb2, jw3, jb3, lw1.transpose(1, 0, 2), lb1, lb2, lw3, lb3, level.reshape(1),
    )


def net_kernel(
    idx_s, level_s, jb3_s, lb3_s,
    tab, got, w1all, f2, b2, head, headb, da_w, qw, col, scale,
    packed,
    xrow, gw2, gw2b, gaw1, gcw1, gaw3, gcw3, gcol, gmisc,
    *, cap, slots,
):
    T = min(TILE, slots)
    nt = slots // T
    lists = T // cap
    rows = message_rows(cap)
    part = min(cap, 128)

    def gather(i):
        for t in range(T):
            r = idx_s[i * lists + t // cap, (t % cap) // 128, t % 128]
            xrow[t : t + 1, :] = tab[pl.ds(r, 1), :]

    gather(0)
    for ref in (gw2, gw2b, gaw1, gcw1, gaw3, gcw3, gcol, gmisc):
        ref[...] = jnp.zeros_like(ref)
    level = level_s[0]

    def act(u):
        t = jnp.tanh(u)
        p = 1.0 + t
        h = u * p
        return h.astype(BF), p + h * (2.0 - p)

    def layer2(l, h):
        r = dot(f2[l], h)
        return act(r[:HID] + r[HID:] + col[:, l : l + 1])

    def first(l0, l1, x24):
        hi, lo = split(x24)
        xs = jnp.concatenate([hi, lo, hi], axis=0).astype(BF)
        return dot(w1all[l0 * HID : l1 * HID, :], xs)

    def back2(l, g):
        r = dot(b2[l], g)
        return r[:HID] + r[HID:]

    def head_out(h2):
        r = dot(head[...], h2)
        o = r[0:16] + r[16:32] + col[0:16, 5:6]
        mean = o[0:8]
        t = jnp.tanh(o[8:16])
        ls = -5.0 + 3.5 * (t + 1.0)
        return mean, t, ls

    def sample(mean, ls, e, live):
        sg = jnp.exp(ls)
        u = mean + sg * e
        a = jnp.tanh(u)
        au = jnp.abs(u)
        sq = 2.0 * (math.log(2.0) - au - jnp.log(1.0 + jnp.exp(-2.0 * au)))
        lp = -0.5 * e * e - ls - 0.5 * math.log(2.0 * math.pi) - sq
        return a, sg, jnp.sum(jnp.where(live, lp, 0.0), axis=0, keepdims=True)

    def q_of(k, h2, b):
        r = dot(qw[k], h2)
        return r[0:1] + r[8:9] + b

    def softmin(q, w):
        a, b = -4.0 * q, -4.0 * w
        return -0.25 * (jnp.maximum(a, b) + jnp.log(1.0 + jnp.exp(-jnp.abs(a - b))))

    ones = jnp.ones((16, T), BF)

    @pl.loop(0, nt)
    def _(i):
        xt = xrow[...].T
        gather(jnp.minimum(i + 1, nt - 1))
        row8 = lax.broadcasted_iota(jnp.int32, (8, T), 0)
        row16 = lax.broadcasted_iota(jnp.int32, (16, T), 0)
        live = row8 < ACT
        seeds = jnp.concatenate([got[i * lists + k, rows + r : rows + r + 1, 0:part] for k in range(lists) for r in range(rows)], axis=1)
        lane = lax.broadcasted_iota(jnp.int32, (1, cap), 1)
        mask = jnp.concatenate(
            [jnp.where(lane < got[i * lists + k, 2 * rows : 2 * rows + 1, 0:1], 1.0, 0.0).astype(F32) for k in range(lists)], axis=1
        )
        alpha = jnp.exp(jnp.full((1, T), level, F32))
        b1 = pltpu.roll(xt[16:24], 7, 0)
        reward = b1[6:7]
        xa = jnp.concatenate([jnp.where(row8 == 6, 1.0, b1), xt[0:16]], axis=0)
        b2_ = pltpu.roll(xt[40:48], 7, 0)
        done = b2_[0:1]
        n_lo = jnp.where(row8 == 7, b2_, jnp.where(row8 == 6, 1.0, 0.0))
        xn = jnp.concatenate([n_lo, xt[24:40]], axis=0)

        un = first(0, 1, xn)
        hi, lo = split(xa)
        xw = jnp.concatenate([hi, lo], axis=0).astype(BF)
        ua = dot(w1all[0 : 3 * HID, :], jnp.concatenate([hi, lo, hi], axis=0).astype(BF))
        eps = noise(seeds, row16)
        e = eps[0:8]
        hn, _ = act(un)
        h1a, d1a = act(ua[0:HID])
        h1c, d1c = zip(*[act(ua[(1 + k) * HID : (2 + k) * HID]) for k in range(2)])
        hn, _ = layer2(0, hn)
        mean, _, ls = head_out(hn)
        a2, _, lp2 = sample(mean, ls, eps[8:16], live)
        h2a, d2a = layer2(0, h1a)
        mean, t, ls = head_out(h2a)
        a1, sg, lp = sample(mean, ls, e, live)
        un = first(3, 5, jnp.concatenate([jnp.where(live, a2, n_lo), xt[24:40]], axis=0))
        h2c, d2c = zip(*[layer2(1 + k, h1c[k]) for k in range(2)])
        qc = [q_of(k, h2c[k], jb3_s[k]) for k in range(2)]
        uq = first(1, 3, jnp.concatenate([jnp.where(live, a1, xa[0:8]), xt[0:16]], axis=0))
        ht = [act(un[k * HID : (k + 1) * HID])[0] for k in range(2)]
        ht = [layer2(3 + k, ht[k])[0] for k in range(2)]
        qt = [q_of(2 + k, ht[k], lb3_s[k]) for k in range(2)]
        h1q, d1q = zip(*[act(uq[k * HID : (k + 1) * HID]) for k in range(2)])
        y = reward + GAMMA * (1.0 - done) * (softmin(qt[0], qt[1]) - alpha * lp2)
        h2q, d2q = zip(*[layer2(1 + k, h1q[k]) for k in range(2)])
        qq = [q_of(k, h2q[k], jb3_s[k]) for k in range(2)]

        closs = jnp.zeros((1, T), F32)
        g2c = []
        for k in range(2):
            dq = qc[k] - y
            mdq = dq * mask
            closs = closs + 0.5 * (mdq * dq)
            g2 = (mdq * d2c[k]).astype(BF)
            g2c.append(g2)
            mhi, mlo = split(mdq)
            m16 = jnp.where(row16 == 0, mhi, jnp.where(row16 == 1, mlo, 0.0)).astype(BF)
            gcw3[k] += dot_t(m16, h2c[k])
            r = dot_t(jnp.concatenate([h1c[k], ones], axis=0), g2)
            gw2[1 + k] += r[0:HID]
            gw2b[1 + k] += r[HID : HID + 8]
            gmisc[k : k + 1, :] += fold(mdq)
        sm = softmin(qq[0], qq[1])
        p0 = 1.0 / (1.0 + jnp.exp(4.0 * (qq[0] - qq[1])))
        da = jnp.zeros((8, T), F32)
        for k, pk in enumerate((p0, 1.0 - p0)):
            g2 = ((-pk * mask) * d2q[k]).astype(BF)
            g1 = (back2(1 + k, g2) * d1q[k]).astype(BF)
            w = dot(da_w[k], g1)
            da = da + w[0:8] + w[8:16]
        for k in range(2):
            g1 = (back2(1 + k, g2c[k]) * d1c[k]).astype(BF)
            w = dot_t(xw, g1)
            gcw1[k] += w[0:24] + w[24:48]
        ma = mask * alpha
        du = da * (1.0 - a1 * a1) + ma * (2.0 * a1)
        dls = (du * sg * e - ma) * (3.5 * (1.0 - t * t))
        do = jnp.concatenate([jnp.where(live, du, 0.0), jnp.where(live, dls, 0.0)], axis=0)
        gcol[...] += fold(do)
        dob = do.astype(BF)
        gaw3[...] += dot_t(dob, h2a)
        g2 = (dot(headb[...], jnp.concatenate([dob, dob], axis=0)) * d2a).astype(BF)
        r = dot_t(jnp.concatenate([h1a, ones], axis=0), g2)
        gw2[0] += r[0:HID]
        gw2b[0] += r[HID : HID + 8]
        g1 = (back2(0, g2) * d1a).astype(BF)
        w = dot_t(xw, g1)
        gaw1[...] += w[0:24] + w[24:48]
        gmisc[2:3, :] += fold(closs)
        gmisc[3:4, :] += fold(mask * (alpha * lp - sm))
        gmisc[4:5, :] += fold(mask * (lp - 6.0))
        gmisc[5:6, :] += fold(mask)

    row8 = lax.broadcasted_iota(jnp.int32, (8, HID), 0)
    cols = jnp.zeros((8, HID), F32)
    for k in range(2):
        s = scale[k : k + 1, :]
        cols = jnp.where(row8 == k, gw2b[1 + k] * s, cols)
        cols = jnp.where(row8 == 2 + k, gcw3[k, 0:1, :] + gcw3[k, 1:2, :], cols)
    cols = jnp.where(row8 == 4, gw2b[0], cols)
    for m in range(3):
        for h in range(2):
            w = gw2[m, :, h * 128 : (h + 1) * 128]
            if m > 0:
                w = w * scale[m - 1 : m, h * 128 : (h + 1) * 128]
            packed[(2 * m + h) * HID : (2 * m + h + 1) * HID, :] = w
    for h in range(2):
        packed[R_AW1 + 24 * h : R_AW1 + 24 * (h + 1), :] = gaw1[:, h * 128 : (h + 1) * 128]
        for k in range(2):
            at = R_CW1 + 48 * k + 24 * h
            packed[at : at + 24, :] = gcw1[k, :, h * 128 : (h + 1) * 128]
        packed[R_AW3 + 16 * h : R_AW3 + 16 * (h + 1), :] = gaw3[:, h * 128 : (h + 1) * 128]
        packed[R_COL + 8 * h : R_COL + 8 * (h + 1), :] = cols[:, h * 128 : (h + 1) * 128]
    packed[R_AB3 : R_AB3 + 16, :] = gcol[...]
    packed[R_MISC : R_MISC + 8, :] = gmisc[...]
    packed[R_END:, :] = jnp.zeros((packed.shape[0] - R_END, 128), F32)


def local_grads(ready, params, n, cap, packed_rows):
    tab, got, idx_s, *weights = ready
    jb3, lb3, level = params[11], params[17], params[18]
    slots = n * cap
    T = min(TILE, slots)
    vm = pl.BlockSpec(memory_space=pltpu.VMEM)
    sm = pl.BlockSpec(memory_space=pltpu.SMEM)
    return pl.pallas_call(
        functools.partial(net_kernel, cap=cap, slots=slots),
        out_shape=pltpu.VMEM((packed_rows, 128), F32),
        in_specs=[sm] * 4 + [vm] * (2 + len(weights)),
        out_specs=vm,
        scratch_shapes=[
            pltpu.VMEM((T, 128), F32),
            pltpu.VMEM((3, HID, HID), F32),
            pltpu.VMEM((3, 8, HID), F32),
            pltpu.VMEM((24, HID), F32),
            pltpu.VMEM((2, 24, HID), F32),
            pltpu.VMEM((16, HID), F32),
            pltpu.VMEM((2, 16, HID), F32),
            pltpu.VMEM((16, 128), F32),
            pltpu.VMEM((8, 128), F32),
        ],
        compiler_params=pltpu.CompilerParams(vmem_limit_bytes=40 << 20),
        name="networks",
    )(idx_s, level.reshape(1), jb3, lb3, tab, got, *weights)


def split_sizes(n):
    sizes = [2]
    n //= 2
    while n > 1:
        f = 4 if n % 4 == 0 else n if n < 4 else 2
        sizes.append(f)
        n //= f
    return sizes


def sum_kernel(sizes, mine, out, full, *rest):
    ns = len(sizes)
    got, part, sems = rest[:ns], rest[ns : 2 * ns], rest[2 * ns]
    me = lax.axis_index("dp")
    digits, strides, st = [], [], 1
    for f in sizes:
        digits.append(lax.rem(me // st, f))
        strides.append(st)
        st *= f

    def member(s, k):
        d = lax.rem(digits[s] + k, sizes[s])
        return d, me + (d - digits[s]) * strides[s]

    barrier = pltpu.get_barrier_semaphore()
    count = 0
    for s in range(ns):
        for k in range(1, sizes[s]):
            pl.semaphore_signal(barrier, inc=1, device_id=(member(s, k)[1],), device_id_type=pl.DeviceIdType.MESH)
            count += 1
    pl.semaphore_wait(barrier, count)

    def send(src, dst, s, k, phase):
        return pltpu.make_async_remote_copy(
            src_ref=src, dst_ref=dst, send_sem=sems.at[phase, s, k, 0], recv_sem=sems.at[phase, s, k, 1],
            device_id=(member(s, k)[1],), device_id_type=pl.DeviceIdType.MESH,
        )

    done = []
    cur, size = mine, mine.shape[0]
    for s in range(ns):
        f = sizes[s]
        blk = size // f
        copies = []
        for k in range(1, f):
            d, _ = member(s, k)
            c = send(cur.at[pl.ds(d * blk, blk)], got[s].at[k - 1], s, k, 0)
            c.start()
            copies.append(c)
        acc = cur[pl.ds(digits[s] * blk, blk)]
        for k in range(1, f):
            copies[k - 1].wait_recv()
            acc = acc + got[s][k - 1]
        part[s][...] = acc
        done += copies
        cur, size = part[s], blk
    at = 0
    span = mine.shape[0]
    for s in range(ns):
        span //= sizes[s]
        at = at + digits[s] * span
    full[pl.ds(at, 1)] = part[ns - 1][...]
    span = 1
    for s in reversed(range(ns)):
        copies = []
        for k in range(1, sizes[s]):
            c = send(full.at[pl.ds(at, span)], full.at[pl.ds(at, span)], s, k, 1)
            c.start()
            copies.append(c)
        for c in copies:
            c.wait_recv()
        done += copies
        at = at - digits[s] * span
        span *= sizes[s]
    out[...] = full[...]
    for c in done:
        c.wait_send()


def sum_over_devices(packed, n):
    sizes = split_sizes(n)
    rows = packed.shape[0] // n
    mine = packed.reshape(n, rows, 128)
    got, part, size = [], [], n
    for f in sizes:
        size //= f
        got.append(pltpu.VMEM((f - 1, size, rows, 128), F32))
        part.append(pltpu.VMEM((size, rows, 128), F32))
    vm = pl.BlockSpec(memory_space=pltpu.VMEM)
    out = pl.pallas_call(
        functools.partial(sum_kernel, sizes),
        out_shape=pltpu.VMEM((n, rows, 128), F32),
        in_specs=[vm],
        out_specs=vm,
        scratch_shapes=[pltpu.VMEM((n, rows, 128), F32)] + got + part + [pltpu.SemaphoreType.DMA((2, len(sizes), max(sizes), 2))],
        compiler_params=pltpu.CompilerParams(collective_id=1, has_side_effects=True, vmem_limit_bytes=24 << 20),
        name="sum_over_devices",
    )(mine)
    return out.reshape(packed.shape)


def finish_kernel(level_s, g, aw1, ab1, aw2, ab2, aw3, ab3, cw1, cb1, cw2, cb2, cw3, cb3, da, losses):
    misc = jnp.sum(g[R_MISC : R_MISC + 8, :], axis=1, keepdims=True)
    n = misc[5:6]
    inv = 1.0 / n

    def rows(at, count):
        return jnp.concatenate([g[at : at + count, :], g[at + count : at + 2 * count, :]], axis=1) * inv

    aw2[...] = rows(0, HID)
    cw2[0] = rows(2 * HID, HID)
    cw2[1] = rows(4 * HID, HID)
    w = rows(R_AW1, 24)
    aw1[0:16, :] = w[8:24]
    aw1[16:17, :] = w[7:8]
    ab1[...] = w[6:7]
    for k in range(2):
        w = rows(R_CW1 + 48 * k, 24)
        cw1[0:16, k, :] = w[8:24]
        cw1[16:17, k, :] = w[7:8]
        cw1[17:23, k, :] = w[0:6]
        cb1[k : k + 1, :] = w[6:7]
    w = rows(R_AW3, 16)
    aw3[0:6, :] = w[0:6]
    aw3[6:12, :] = w[8:14]
    c = rows(R_COL, 8)
    cb2[...] = c[0:2]
    cw3[...] = c[2:4]
    ab2[...] = c[4:5]
    b = jnp.sum(g[R_AB3 : R_AB3 + 16, :], axis=1, keepdims=True) * inv
    diag = lax.broadcasted_iota(jnp.int32, (16, 128), 0) == lax.broadcasted_iota(jnp.int32, (16, 128), 1)
    b = jnp.sum(jnp.where(diag, b, 0.0), axis=0, keepdims=True)
    ab3[...] = jnp.concatenate([b[:, 0:6], b[:, 8:14]], axis=1)
    m = misc * inv
    cb3[...] = jnp.concatenate([m[0:1], m[1:2]], axis=1)
    da[...] = -m[4:5]
    losses[...] = jnp.concatenate([m[2:3], m[3:4], -level_s[0] * m[4:5]], axis=1)


def finish(total, level):
    vm = pl.BlockSpec(memory_space=pltpu.VMEM)
    shapes = [
        (OBS, HID), (1, HID), (HID, HID), (1, HID), (12, HID), (1, 12),
        (23, 2, HID), (2, HID), (2, HID, HID), (2, HID), (2, HID), (1, 2), (1, 1), (1, 3),
    ]
    outs = list(pl.pallas_call(
        finish_kernel,
        out_shape=[jax.ShapeDtypeStruct(x, F32) for x in shapes],
        in_specs=[pl.BlockSpec(memory_space=pltpu.SMEM), vm],
        out_specs=[vm] * len(shapes),
        name="finish",
    )(level.reshape(1), total))
    outs[4] = outs[4].T
    outs[6] = outs[6].transpose(1, 0, 2)
    for k, shape in ((1, (HID,)), (3, (HID,)), (5, (12,)), (11, (2,)), (12, ()), (13, (3,))):
        outs[k] = outs[k].reshape(shape)
    return tuple(outs)


def body(experience_buffer, sampled_indices, filled_lengths, randomizer_numbers, *params):
    n, cap = sampled_indices.shape[1:]
    ready = prepare(experience_buffer, sampled_indices, randomizer_numbers, filled_lengths, params)
    packed = local_grads(ready, params, n, cap, n * 8 * (-(-R_END // (8 * n))))
    return finish(sum_over_devices(packed, n), params[-1])


def solution(mesh):
    in_specs = (P(None, "dp"), P("dp", None, None), P("dp", None), P("dp", None, None)) + (P(),) * 19
    return jax.shard_map(body, mesh=mesh, in_specs=in_specs, out_specs=(P(),) * 14, check_vma=False)
```

time: 153 us -> 137 us (0.90)
  Pallas kernels: 128 us -> 116 us
  starting transfers between devices: 7.3 us -> 0 us
  local copies, waits for them, and re-layouts: 12.7 us -> 18.5 us
  waiting for transfers between devices: 2.65 us -> 0 us
    pallas_call x2 -> x3, Pallas kernels: 126 us -> 114 us  [the longest x1 72.1 us: local_grads(): pl.pallas_call(functools.partial(net_kernel, cap=cap, slots=slots), out_s...]
    unnamed x11 -> x50, local copies, waits for them, and re-layouts: 10.1 us -> 18.5 us
    all_to_all x1 -> x0, starting transfers between devices: 7.3 us -> none  [body(): got = lax.all_to_all(message, 'dp', split_axis=0, concat_axis=0, tiled=True)]
    all_to_all x1 -> x0, waiting for transfers between devices: 2.65 us -> none  [body(): got = lax.all_to_all(message, 'dp', split_axis=0, concat_axis=0, tiled=True)]
  transfers between devices with their start and end apart: 1 -> 0, of which waited for: 1 -> 0; matrix products, arithmetic and copies ran while one was open for 3% -> 0% of each run, Pallas kernels for 0% -> 0%
where the time goes in v3:
time: 137 us; the launch traced here: 136 us
  Pallas kernels  116 us (85%)
  local copies, waits for them, and re-layouts  18.5 us (14%)
  between operations  1.41 us (1%)
    pallas_call x1, Pallas kernels, local_grads(): pl.pallas_call(functools.partial(net_kernel, cap=cap, slots=slots), out_s...  72.1 us
    pallas_call x1, Pallas kernels, sum_over_devices(): pl.pallas_call(functools.partial(sum_kernel, sizes), out_shape=pltpu.VMEM...  26.6 us
    unnamed x50, local copies, waits for them, and re-layouts  18.5 us
    pallas_call x1, Pallas kernels, prepare(): pl.pallas_call(functools.partial(prepare_kernel, n=n, cap=cap), out_shape...  15.3 us

profile of v3, /device:TPU:0, one launch (start us, length us, event | category | flops | bytes accessed | tf_op | source)
XLA Modules:
  0.0 136.1 jit_solution(7794270304948957491)
XLA Ops:
  1.3 1.9 %copy-done.1 = f32[42,16384]{1,0:T(8,128)S(1)} copy-done((f32[42,16384]{1,0:T(8,128)S(1)}, f32[42,16384]{1,0:T(8,128)}, u32[]{:S(2)}) %copy-start.1) | copy-done | bytes 2752536
  3.2 1.0 copy-done.2
  4.3 1.0 copy-done.3
  5.3 0.9 copy-done.4
  6.3 0.8 copy-done.5
  7.1 0.8 copy-done.6
  7.9 0.8 copy-done.7
  8.6 0.8 copy-done.8
  9.4 0.7 copy-done.9
  10.1 0.7 copy-done.10
  10.8 0.7 copy-done.11
  11.5 0.7 copy-done.12
  12.2 0.7 copy-done.13
  12.9 0.7 copy-done.14
  13.6 0.7 copy-done.15
  14.2 0.7 copy-done.16
  14.9 0.7 copy-done.17
  16.2 0.7 copy-done.21
  16.9 0.7 copy-done.22
  18.9 15.3 %exchange_and_prepare.1 = (f32[16384,128]{1,0:T(8,128)S(1)}, s32[32,8,128]{2,1,0:T(8,128)S(1)}, s32[32,2,128]{2,1,0:T(2,128)S(4)}, bf16[1280,72]{1,0:T(8,128)(2,...) custom-call(s32[1,32,256]{2,1,0:T(8,128)S(1)} %copy-done.7, ...), custom_call_target="tpu_custom_call" | custom-call | tf_op jit(solution)/shard_map/exchange_and_prepare/pallas_call | solution.py:215
  34.2 72.1 %networks.1 = f32[1792,128]{1,0:T(8,128)S(1)} custom-call(s32[32,2,128]{2,1,0:T(2,128)S(4)} %get-tuple-element.40.idx_s, f32[1]{0:T(128)} %bitcast.17.level_s, f32[2]{0:T(128)S(1)} %copy-done.18, f32[2]{0:T(128)S(1)} %copy-done.20, f32[16384,128]{1,0:T(8,128)S(1)} %get-tuple-element.41.tab, s32[32,8,128]{2,1,0:T(8,128)S(1)} %get-tuple-element.42.got, ...), custom_call_target="tpu_custom_call" | custom-call | tf_op jit(solution)/shard_map/networks/pallas_call | solution.py:438
  106.3 26.6 %sum_over_devices.1 = f32[32,56,128]{2,1,0:T(8,128)S(1)} custom-call(f32[32,56,128]{2,1,0:T(8,128)S(1)} %bitcast.20), custom_call_target="tpu_custom_call" | custom-call | tf_op jit(solution)/shard_map/sum_over_devices/pallas_call | solution.py:548
  133.0 0.9 copy-done
  133.9 2.2 %finish.1 = (f32[17,256]{1,0:T(8,128)}, f32[1,256]{1,0:T(1,128)}, f32[256,256]{1,0:T(8,128)}, f32[1,256]{1,0:T(1,128)}, f32[12,256]{1,0:T(8,128)}, /*index=5*/f3...) custom-call(f32[1]{0:T(128)} %bitcast.18.level_s, ...), custom_call_target="tpu_custom_call" | custom-call | tf_op jit(solution)/shard_map/finish/pallas_call | solution.py:604
  (30 shorter events, 2.0 us)
Async XLA Ops:
  0.7 33.6 %copy-start.20 = (f32[2]{0:T(128)S(1)}, f32[2]{0:T(128)}, u32[]{:S(2)}) copy-start(f32[2]{0:T(128)} %lb3_s.1) | copy-start | bytes 28
  0.7 33.6 %copy-start.18 = (f32[2]{0:T(128)S(1)}, f32[2]{0:T(128)}, u32[]{:S(2)}) copy-start(f32[2]{0:T(128)} %jb3_s.1) | copy-start | bytes 28
  1.3 1.9 %copy-start.1 = (f32[42,16384]{1,0:T(8,128)S(1)}, f32[42,16384]{1,0:T(8,128)}, u32[]{:S(2)}) copy-start(f32[42,16384]{1,0:T(8,128)} %buf_h.1) | copy-start | bytes 8257540
  3.2 1.0 copy-start.2
  4.3 1.0 copy-start.3
  5.3 0.9 copy-start.4
  6.3 0.8 copy-start.5
  7.1 0.8 copy-start.6
  7.9 0.8 copy-start.7
  8.6 0.8 copy-start.8
  9.4 0.7 copy-start.9
  10.1 0.7 copy-start.10
  10.8 0.7 copy-start.11
  11.5 0.7 copy-start.12
  12.2 0.7 copy-start.13
  12.9 0.7 copy-start.14
  13.6 0.7 copy-start.15
  14.2 0.7 copy-start.16
  14.9 0.7 copy-start.17
  15.6 0.7 copy-start.19
  16.2 0.7 copy-start.21
  16.9 0.7 copy-start.22
  17.6 0.7 copy-start.23
  133.0 0.9 copy-start
  (1 other events, 0.7 us)

commit v4 on v3

--- a/solution.py
+++ b/solution.py
@@ -14,6 +14,7 @@
 GAMMA = 0.99
 PRIME = 65521
 TILE = 1024
+CHUNKS = 4
 R_AW1 = 6 * HID
 R_CW1 = R_AW1 + 48
 R_AW3 = R_CW1 + 96
@@ -71,21 +72,25 @@
 
 def prepare_kernel(
     idx_h, seed_h, cnt_h, buf_h, aw2_h, jw2_h, lw2_h,
-    aw1, ab1, ab2, aw3, ab3, jw1, jb1, jb2, jw3, jb3, lw1, lb1, lb2, lw3, lb3, level,
-    tab, got, idx_s, w1all, f2, b2, head, headb, da_w, qw, col, scale,
-    idx_v, seed_v, cnt_v, buf, w2, msg, land, flat, tmp, rowbuf, in_sems, sems,
+    aw1_h, ab1_h, ab2_h, aw3_h, jw1_h, jb1_h, jb2_h, jw3_h, lw1_h, lb1_h, lb2_h, lw3_h,
+    ab3_h, jb3_h, lb3_h, level,
+    tab, got, idx_s, w1all, f2, b2, head, headb, da_w, qw, col, scale, scal,
+    idx_v, seed_v, cnt_v, buf, w2, aw1, ab1, ab2, aw3, jw1, jb1, jb2, jw3, lw1, lb1, lb2, lw3,
+    ab3, jb3, lb3, msg, land, flat, tmp, rowbuf, in_sems, sems,
     *, n, cap,
 ):
     me = lax.axis_index("dp")
     rows = message_rows(cap)
     part = min(cap, 128)
     width = buf.shape[1]
-    loads = [
-        pltpu.make_async_copy(src, dst, in_sems.at[k])
-        for k, (src, dst) in enumerate(
-            ((idx_h, idx_v), (seed_h, seed_v), (cnt_h, cnt_v), (buf_h, buf), (aw2_h, w2.at[0]), (jw2_h, w2.at[pl.ds(1, 2)]), (lw2_h, w2.at[pl.ds(3, 2)]))
-        )
-    ]
+    pairs = (
+        (idx_h, idx_v), (seed_h, seed_v), (cnt_h, cnt_v), (buf_h, buf),
+        (aw2_h, w2.at[0]), (jw2_h, w2.at[pl.ds(1, 2)]), (lw2_h, w2.at[pl.ds(3, 2)]),
+        (aw1_h, aw1), (ab1_h, ab1), (ab2_h, ab2), (aw3_h, aw3), (jw1_h, jw1), (jb1_h, jb1), (jb2_h, jb2),
+        (jw3_h, jw3), (lw1_h, lw1), (lb1_h, lb1), (lb2_h, lb2), (lw3_h, lw3),
+        (ab3_h, ab3), (jb3_h, jb3), (lb3_h, lb3),
+    )
+    loads = [pltpu.make_async_copy(src, dst, in_sems.at[k]) for k, (src, dst) in enumerate(pairs)]
     for c in loads:
         c.start()
     barrier = pltpu.get_barrier_semaphore()
@@ -172,6 +177,10 @@
     col[...] = rowbuf[...].T
     scale[...] = jnp.zeros_like(scale)
     scale[0:2, :] = 0.5 * jw3[...]
+    for k in range(2):
+        scal[k] = jb3[k]
+        scal[2 + k] = lb3[k]
+    scal[4] = level[0]
 
     land[0] = msg[me]
 
@@ -211,38 +220,60 @@
         pltpu.VMEM((4, 16, HID), BF),
         pltpu.VMEM((HID, 8), F32),
         pltpu.VMEM((8, HID), F32),
+        pltpu.SMEM((8,), F32),
     ]
     return pl.pallas_call(
         functools.partial(prepare_kernel, n=n, cap=cap),
         out_shape=out,
-        in_specs=[hbm] * 7 + [vm] * 4 + [sm] + [vm] * 4 + [sm] + [vm] * 4 + [sm] * 2,
-        out_specs=[vm, vm, sm] + [vm] * 9,
+        in_specs=[hbm] * 22 + [sm],
+        out_specs=[vm, vm, sm] + [vm] * 9 + [sm],
         scratch_shapes=[
             pltpu.VMEM((1, n, cap), jnp.int32),
             pltpu.VMEM((1, n, cap), jnp.int32),
             pltpu.VMEM((1, n), jnp.int32),
             pltpu.VMEM((feats, width), F32),
             pltpu.VMEM((5, HID, HID), F32),
+            pltpu.VMEM((OBS, HID), F32),
+            pltpu.VMEM((1, HID), F32),
+            pltpu.VMEM((1, HID), F32),
+            pltpu.VMEM((12, HID), F32),
+            pltpu.VMEM((23, 2, HID), F32),
+            pltpu.VMEM((2, HID), F32),
+            pltpu.VMEM((2, HID), F32),
+            pltpu.VMEM((2, HID), F32),
+            pltpu.VMEM((23, 2, HID), F32),
+            pltpu.VMEM((2, HID), F32),
+            pltpu.VMEM((2, HID), F32),
+            pltpu.VMEM((2, HID), F32),
+            pltpu.SMEM((12,), F32),
+            pltpu.SMEM((2,), F32),
+            pltpu.SMEM((2,), F32),
             pltpu.VMEM((n, 8, 128), jnp.int32),
             pltpu.VMEM((n, 8, 128), jnp.int32),
             pltpu.VMEM((n, rows, 128), jnp.int32),
             pltpu.VMEM((24, HID), F32),
             pltpu.VMEM((8, HID), F32),
-            pltpu.SemaphoreType.DMA((7,)),
+            pltpu.SemaphoreType.DMA((22,)),
             pltpu.SemaphoreType.DMA((2, n)),
         ],
         compiler_params=pltpu.CompilerParams(collective_id=2, has_side_effects=True, vmem_limit_bytes=24 << 20),
         name="exchange_and_prepare",
     )(
-        sampled, seeds, counts, experience_buffer, aw2, jw2, lw2,
-        aw1, ab1.reshape(1, HID), ab2.reshape(1, HID), aw3.T, ab3,
-        jw1.transpose(1, 0, 2), jb1, jb2, jw3, jb3, lw1.transpose(1, 0, 2), lb1, lb2, lw3, lb3, level.reshape(1),
+        *[
+            pltpu.with_memory_space_constraint(x, pltpu.HBM)
+            for x in (
+                sampled, seeds, counts, experience_buffer, aw2, jw2, lw2,
+                aw1, ab1.reshape(1, HID), ab2.reshape(1, HID), aw3.T,
+                jw1.transpose(1, 0, 2), jb1, jb2, jw3, lw1.transpose(1, 0, 2), lb1, lb2, lw3,
+                ab3, jb3, lb3,
+            )
+        ],
+        level.reshape(1),
     )
 
 
 def net_kernel(
-    idx_s, level_s, jb3_s, lb3_s,
-    tab, got, w1all, f2, b2, head, headb, da_w, qw, col, scale,
+    idx_s, scal, tab, got, w1all, f2, b2, head, headb, da_w, qw, col, scale,
     packed,
     xrow, gw2, gw2b, gaw1, gcw1, gaw3, gcw3, gcol, gmisc,
     *, cap, slots,
@@ -261,7 +292,9 @@
     gather(0)
     for ref in (gw2, gw2b, gaw1, gcw1, gaw3, gcw3, gcol, gmisc):
         ref[...] = jnp.zeros_like(ref)
-    level = level_s[0]
+    level = scal[4]
+    jb3_s = (scal[0], scal[1])
+    lb3_s = (scal[2], scal[3])
 
     def act(u):
         t = jnp.tanh(u)
@@ -428,9 +461,8 @@
     packed[R_END:, :] = jnp.zeros((packed.shape[0] - R_END, 128), F32)
 
 
-def local_grads(ready, params, n, cap, packed_rows):
-    tab, got, idx_s, *weights = ready
-    jb3, lb3, level = params[11], params[17], params[18]
+def local_grads(ready, n, cap, packed_rows):
+    tab, got, idx_s, *weights, scal = ready
     slots = n * cap
     T = min(TILE, slots)
     vm = pl.BlockSpec(memory_space=pltpu.VMEM)
@@ -438,7 +470,7 @@
     return pl.pallas_call(
         functools.partial(net_kernel, cap=cap, slots=slots),
         out_shape=pltpu.VMEM((packed_rows, 128), F32),
-        in_specs=[sm] * 4 + [vm] * (2 + len(weights)),
+        in_specs=[sm] * 2 + [vm] * (2 + len(weights)),
         out_specs=vm,
         scratch_shapes=[
             pltpu.VMEM((T, 128), F32),
@@ -453,7 +485,7 @@
         ],
         compiler_params=pltpu.CompilerParams(vmem_limit_bytes=40 << 20),
         name="networks",
-    )(idx_s, level.reshape(1), jb3, lb3, tab, got, *weights)
+    )(idx_s, scal, tab, got, *weights)
 
 
 def split_sizes(n):
@@ -466,9 +498,18 @@
     return sizes
 
 
-def sum_kernel(sizes, mine, out, full, *rest):
+def chunk_rows(rows):
+    units = rows // 8
+    k = min(CHUNKS, units)
+    cuts = [8 * (units * j // k) for j in range(k + 1)]
+    return list(zip(cuts[:-1], cuts[1:]))
+
+
+def sum_kernel(sizes, mine, out, *rest):
     ns = len(sizes)
     got, part, sems = rest[:ns], rest[ns : 2 * ns], rest[2 * ns]
+    n = mine.shape[0]
+    parts = chunk_rows(mine.shape[1])
     me = lax.axis_index("dp")
     digits, strides, st = [], [], 1
     for f in sizes:
@@ -488,51 +529,67 @@
             count += 1
     pl.semaphore_wait(barrier, count)
 
-    def send(src, dst, s, k, phase):
-        return pltpu.make_async_remote_copy(
-            src_ref=src, dst_ref=dst, send_sem=sems.at[phase, s, k, 0], recv_sem=sems.at[phase, s, k, 1],
+    def send(src, dst, s, k, phase, c):
+        copy = pltpu.make_async_remote_copy(
+            src_ref=src, dst_ref=dst, send_sem=sems.at[phase, c, s, k, 0], recv_sem=sems.at[phase, c, s, k, 1],
             device_id=(member(s, k)[1],), device_id_type=pl.DeviceIdType.MESH,
         )
-
-    done = []
-    cur, size = mine, mine.shape[0]
+        copy.start()
+        return copy
+
+    spans, starts = [n], [0]
     for s in range(ns):
-        f = sizes[s]
-        blk = size // f
-        copies = []
-        for k in range(1, f):
-            d, _ = member(s, k)
-            c = send(cur.at[pl.ds(d * blk, blk)], got[s].at[k - 1], s, k, 0)
-            c.start()
-            copies.append(c)
-        acc = cur[pl.ds(digits[s] * blk, blk)]
-        for k in range(1, f):
-            copies[k - 1].wait_recv()
-            acc = acc + got[s][k - 1]
-        part[s][...] = acc
-        done += copies
-        cur, size = part[s], blk
-    at = 0
-    span = mine.shape[0]
-    for s in range(ns):
-        span //= sizes[s]
-        at = at + digits[s] * span
-    full[pl.ds(at, 1)] = part[ns - 1][...]
-    span = 1
-    for s in reversed(range(ns)):
-        copies = []
-        for k in range(1, sizes[s]):
-            c = send(full.at[pl.ds(at, span)], full.at[pl.ds(at, span)], s, k, 1)
-            c.start()
-            copies.append(c)
-        for c in copies:
-            c.wait_recv()
-        done += copies
-        at = at - digits[s] * span
-        span *= sizes[s]
-    out[...] = full[...]
-    for c in done:
-        c.wait_send()
+        spans.append(spans[s] // sizes[s])
+        starts.append(starts[s] + digits[s] * spans[s + 1])
+    done, flying = [], {}
+
+    def scatter(s, c):
+        lo, hi = parts[c]
+        src = mine if s == 0 else part[s - 1]
+        flying[0, s, c] = [
+            send(src.at[pl.ds(member(s, k)[0] * spans[s + 1], spans[s + 1]), lo:hi], got[s].at[k - 1, :, lo:hi], s, k, 0, c)
+            for k in range(1, sizes[s])
+        ]
+
+    def add(s, c):
+        lo, hi = parts[c]
+        src = mine if s == 0 else part[s - 1]
+        acc = src[pl.ds(digits[s] * spans[s + 1], spans[s + 1]), lo:hi]
+        for k, copy in enumerate(flying[0, s, c]):
+            copy.wait_recv()
+            acc = acc + got[s][k, :, lo:hi]
+            done.append(copy)
+        if s == ns - 1:
+            out[pl.ds(starts[ns], 1), lo:hi] = acc
+        else:
+            part[s][:, lo:hi] = acc
+
+    def spread(s, c):
+        lo, hi = parts[c]
+        at = out.at[pl.ds(starts[s + 1], spans[s + 1]), lo:hi]
+        flying[1, s, c] = [send(at, at, s, k, 1, c) for k in range(1, sizes[s])]
+
+    def arrive(s, c):
+        for copy in flying[1, s, c]:
+            copy.wait_recv()
+            done.append(copy)
+
+    def step(j, c):
+        if 1 <= j <= ns:
+            add(j - 1, c)
+        if j > ns:
+            arrive(2 * ns - j, c)
+        if j < ns:
+            scatter(j, c)
+        elif j < 2 * ns:
+            spread(2 * ns - 1 - j, c)
+
+    for t in range(2 * ns + len(parts)):
+        for j in reversed(range(2 * ns + 1)):
+            if 0 <= t - j < len(parts):
+                step(j, t - j)
+    for copy in done:
+        copy.wait_send()
 
 
 def sum_over_devices(packed, n):
@@ -550,14 +607,14 @@
         out_shape=pltpu.VMEM((n, rows, 128), F32),
         in_specs=[vm],
         out_specs=vm,
-        scratch_shapes=[pltpu.VMEM((n, rows, 128), F32)] + got + part + [pltpu.SemaphoreType.DMA((2, len(sizes), max(sizes), 2))],
+        scratch_shapes=got + part + [pltpu.SemaphoreType.DMA((2, len(chunk_rows(rows)), len(sizes), max(sizes), 2))],
         compiler_params=pltpu.CompilerParams(collective_id=1, has_side_effects=True, vmem_limit_bytes=24 << 20),
         name="sum_over_devices",
     )(mine)
     return out.reshape(packed.shape)
 
 
-def finish_kernel(level_s, g, aw1, ab1, aw2, ab2, aw3, ab3, cw1, cb1, cw2, cb2, cw3, cb3, da, losses):
+def finish_kernel(scal, g, aw1, ab1, aw2, ab2, aw3, ab3, cw1, cb1, cw2, cb2, cw3, cb3, da, losses):
     misc = jnp.sum(g[R_MISC : R_MISC + 8, :], axis=1, keepdims=True)
     n = misc[5:6]
     inv = 1.0 / n
@@ -592,10 +649,10 @@
     m = misc * inv
     cb3[...] = jnp.concatenate([m[0:1], m[1:2]], axis=1)
     da[...] = -m[4:5]
-    losses[...] = jnp.concatenate([m[2:3], m[3:4], -level_s[0] * m[4:5]], axis=1)
-
-
-def finish(total, level):
+    losses[...] = jnp.concatenate([m[2:3], m[3:4], -scal[4] * m[4:5]], axis=1)
+
+
+def finish(total, scal):
     vm = pl.BlockSpec(memory_space=pltpu.VMEM)
     shapes = [
         (OBS, HID), (1, HID), (HID, HID), (1, HID), (12, HID), (1, 12),
@@ -607,7 +664,7 @@
         in_specs=[pl.BlockSpec(memory_space=pltpu.SMEM), vm],
         out_specs=[vm] * len(shapes),
         name="finish",
-    )(level.reshape(1), total))
+    )(scal, total))
     outs[4] = outs[4].T
     outs[6] = outs[6].transpose(1, 0, 2)
     for k, shape in ((1, (HID,)), (3, (HID,)), (5, (12,)), (11, (2,)), (12, ()), (13, (3,))):
@@ -618,8 +675,8 @@
 def body(experience_buffer, sampled_indices, filled_lengths, randomizer_numbers, *params):
     n, cap = sampled_indices.shape[1:]
     ready = prepare(experience_buffer, sampled_indices, randomizer_numbers, filled_lengths, params)
-    packed = local_grads(ready, params, n, cap, n * 8 * (-(-R_END // (8 * n))))
-    return finish(sum_over_devices(packed, n), params[-1])
+    packed = local_grads(ready, n, cap, n * 8 * (-(-R_END // (8 * n))))
+    return finish(sum_over_devices(packed, n), ready[-1])
 
 
 def solution(mesh):

time: 137 us -> 118 us (0.86)
  local copies, waits for them, and re-layouts: 18.5 us -> 0.91 us
    unnamed x50 -> x2, local copies, waits for them, and re-layouts: 18.5 us -> 0.91 us
    pallas_call x1, Pallas kernels: 26.6 us -> 31.4 us  [sum_over_devices(): pl.pallas_call(functools.partial(sum_kernel, sizes), out_shape=pltpu.VMEM...]
    pallas_call x1, Pallas kernels: 72.1 us -> 67.5 us  [local_grads(): pl.pallas_call(functools.partial(net_kernel, cap=cap, slots=slots), out_s...]
where the time goes in v4:
time: 118 us
  Pallas kernels  116 us (98%)
  between operations  1.33 us (1%)
    pallas_call x1, Pallas kernels, local_grads(): pl.pallas_call(functools.partial(net_kernel, cap=cap, slots=slots), out_s...  67.5 us
    pallas_call x1, Pallas kernels, sum_over_devices(): pl.pallas_call(functools.partial(sum_kernel, sizes), out_shape=pltpu.VMEM...  31.4 us
    pallas_call x1, Pallas kernels, prepare(): pl.pallas_call(functools.partial(prepare_kernel, n=n, cap=cap), out_shape...  14.6 us

profile of v4, /device:TPU:0, one launch (start us, length us, event | category | flops | bytes accessed | tf_op | source)
XLA Modules:
  0.0 118.0 jit_solution(1235940237622701310)
XLA Ops:
  1.3 14.6 %exchange_and_prepare.1 = (f32[16384,128]{1,0:T(8,128)S(1)}, s32[32,8,128]{2,1,0:T(8,128)S(1)}, s32[32,2,128]{2,1,0:T(2,128)S(4)}, bf16[1280,72]{1,0:T(8,128)(2,...) custom-call(s32[1,32,256]{2,1,0:T(8,128)} %idx_h.1, ...), custom_call_target="tpu_custom_call" | custom-call | tf_op jit(solution)/shard_map/exchange_and_prepare/pallas_call | solution.py:225
  15.9 67.5 %networks.1 = f32[1792,128]{1,0:T(8,128)S(1)} custom-call(s32[32,2,128]{2,1,0:T(2,128)S(4)} %get-tuple-element.42.idx_s, f32[8]{0:T(128)S(4)} %get-tuple-element.41.scal, f32[16384,128]{1,0:T(8,128)S(1)} %get-tuple-element.43.tab, s32[32,8,128]{2,1,0:T(8,128)S(1)} %get-tuple-element.44.got, bf16[1280,72]{1,0:T(8,128)(2,1)S(1)} %get-tuple-element.45.w1all, ...), custom_call_target="tpu_custom_call" | custom-call | tf_op jit(solution)/shard_map/networks/pallas_call | solution.py:470
  83.4 31.4 %sum_over_devices.1 = f32[32,56,128]{2,1,0:T(8,128)S(1)} custom-call(f32[32,56,128]{2,1,0:T(8,128)S(1)} %bitcast.18), custom_call_target="tpu_custom_call" | custom-call | tf_op jit(solution)/shard_map/sum_over_devices/pallas_call | solution.py:605
  114.9 0.0 copy-start
  114.9 0.9 copy-done
  115.8 2.2 %finish.1 = (f32[17,256]{1,0:T(8,128)}, f32[1,256]{1,0:T(1,128)}, f32[256,256]{1,0:T(8,128)}, f32[1,256]{1,0:T(1,128)}, f32[12,256]{1,0:T(8,128)}, /*index=5*/f3...) custom-call(f32[8]{0:T(128)S(4)} %get-tuple-element.41.scal, ...), custom_call_target="tpu_custom_call" | custom-call | tf_op jit(solution)/shard_map/finish/pallas_call | solution.py:661
Async XLA Ops:
  114.9 0.9 copy-start

commit v5 on v4

--- a/solution.py
+++ b/solution.py
@@ -15,6 +15,7 @@
 PRIME = 65521
 TILE = 1024
 CHUNKS = 4
+VARIANTS = 8
 R_AW1 = 6 * HID
 R_CW1 = R_AW1 + 48
 R_AW3 = R_CW1 + 96
@@ -108,25 +109,6 @@
     diag = lax.broadcasted_iota(jnp.int32, (n, n), 0) == lax.broadcasted_iota(jnp.int32, (n, n), 1)
     counts = jnp.sum(jnp.where(diag, cnt_v[...].astype(F32), 0.0), axis=1, keepdims=True)
     msg[:, 2 * rows, :] = jnp.broadcast_to(counts, (n, 128)).astype(jnp.int32)
-    pl.semaphore_wait(barrier, n - 1)
-
-    def copy(k):
-        return pltpu.make_async_remote_copy(
-            src_ref=msg.at[lax.rem(me + k, n)], dst_ref=land.at[k], send_sem=sems.at[0, k], recv_sem=sems.at[1, k],
-            device_id=(lax.rem(me + k, n),), device_id_type=pl.DeviceIdType.MESH,
-        )
-
-    @pl.loop(1, n)
-    def _(k):
-        copy(k).start()
-
-    loads[3].wait()
-
-    @pl.loop(0, width // 128, unroll=4)
-    def _(c):
-        blk = buf[:, pl.ds(pl.multiple_of(c * 128, 128), 128)]
-        tab[pl.ds(pl.multiple_of(c * 128, 128), 128), 0:42] = blk.T
-
     for c in loads[4:]:
         c.wait()
     for l, (w1, b1, k) in enumerate(((aw1, ab1, None), (jw1, jb1, 0), (jw1, jb1, 1), (lw1, lb1, 0), (lw1, lb1, 1))):
@@ -145,16 +127,23 @@
         if l in (1, 2):
             hi, lo = split(tmp[0:8, :])
             da_w[l - 1] = jnp.concatenate([hi, lo], axis=0).astype(BF)
+    start = ((2 * me + 1).astype(F32) / n - 1.0) * 2.0**-8
+
+    def roundings(ref, l, w):
+        left = w.astype(BF).astype(F32) * start
+        for v in range(VARIANTS):
+            want = w + left
+            got_ = want.astype(BF)
+            ref[l, v] = got_
+            left = want - got_.astype(F32)
+
     for l in range(5):
         w = 0.5 * w2[l]
-        hi, lo = split(w)
-        f2[l, 0:HID, :] = hi.T.astype(BF)
-        f2[l, HID:, :] = lo.T.astype(BF)
-        if l < 3:
-            if l > 0:
-                hi, lo = split(w * (0.5 * jw3[l - 1 : l, :]))
-            b2[l, 0:HID, :] = hi.astype(BF)
-            b2[l, HID:, :] = lo.astype(BF)
+        roundings(f2, l, w.T)
+        if l == 0:
+            roundings(b2, l, w)
+        elif l < 3:
+            roundings(b2, l, w * (0.5 * jw3[l - 1 : l, :]))
     tmp[0:12, :] = aw3[...]
     r8 = lax.broadcasted_iota(jnp.int32, (8, HID), 0)
     w_head = jnp.concatenate([jnp.where(r8 < 6, tmp[0:8, :], 0.0), jnp.where(r8 < 6, tmp[6:14, :], 0.0)], axis=0)
@@ -182,6 +171,25 @@
         scal[2 + k] = lb3[k]
     scal[4] = level[0]
 
+    pl.semaphore_wait(barrier, n - 1)
+
+    def copy(k):
+        return pltpu.make_async_remote_copy(
+            src_ref=msg.at[lax.rem(me + k, n)], dst_ref=land.at[k], send_sem=sems.at[0, k], recv_sem=sems.at[1, k],
+            device_id=(lax.rem(me + k, n),), device_id_type=pl.DeviceIdType.MESH,
+        )
+
+    @pl.loop(1, n)
+    def _(k):
+        copy(k).start()
+
+    loads[3].wait()
+
+    @pl.loop(0, width // 128, unroll=4)
+    def _(c):
+        blk = buf[:, pl.ds(pl.multiple_of(c * 128, 128), 128)]
+        tab[pl.ds(pl.multiple_of(c * 128, 128), 128), 0:42] = blk.T
+
     land[0] = msg[me]
 
     @pl.loop(1, n)
@@ -212,8 +220,8 @@
         pltpu.VMEM((n, 8, 128), jnp.int32),
         pltpu.SMEM((n, rows, 128), jnp.int32),
         pltpu.VMEM((5 * HID, 72), BF),
-        pltpu.VMEM((5, 2 * HID, HID), BF),
-        pltpu.VMEM((3, 2 * HID, HID), BF),
+        pltpu.VMEM((5, VARIANTS, HID, HID), BF),
+        pltpu.VMEM((3, VARIANTS, HID, HID), BF),
         pltpu.VMEM((32, HID), BF),
         pltpu.VMEM((HID, 32), BF),
         pltpu.VMEM((2, 16, HID), BF),
@@ -302,18 +310,19 @@
         h = u * p
         return h.astype(BF), p + h * (2.0 - p)
 
-    def layer2(l, h):
-        r = dot(f2[l], h)
-        return act(r[:HID] + r[HID:] + col[:, l : l + 1])
+    def layer2(i, l, h):
+        return act(by_chunk(f2, l, i, h) + col[:, l : l + 1])
 
     def first(l0, l1, x24):
         hi, lo = split(x24)
         xs = jnp.concatenate([hi, lo, hi], axis=0).astype(BF)
         return dot(w1all[l0 * HID : l1 * HID, :], xs)
 
-    def back2(l, g):
-        r = dot(b2[l], g)
-        return r[:HID] + r[HID:]
+    def by_chunk(w, l, i, x):
+        nq = T // HID
+        return jnp.concatenate(
+            [dot(w[l, lax.rem(i * nq + q, VARIANTS)], x[:, q * HID : (q + 1) * HID]) for q in range(nq)], axis=1
+        )
 
     def head_out(h2):
         r = dot(head[...], h2)
@@ -372,22 +381,22 @@
         hn, _ = act(un)
         h1a, d1a = act(ua[0:HID])
         h1c, d1c = zip(*[act(ua[(1 + k) * HID : (2 + k) * HID]) for k in range(2)])
-        hn, _ = layer2(0, hn)
+        hn, _ = layer2(i, 0, hn)
         mean, _, ls = head_out(hn)
         a2, _, lp2 = sample(mean, ls, eps[8:16], live)
-        h2a, d2a = layer2(0, h1a)
+        h2a, d2a = layer2(i, 0, h1a)
         mean, t, ls = head_out(h2a)
         a1, sg, lp = sample(mean, ls, e, live)
         un = first(3, 5, jnp.concatenate([jnp.where(live, a2, n_lo), xt[24:40]], axis=0))
-        h2c, d2c = zip(*[layer2(1 + k, h1c[k]) for k in range(2)])
+        h2c, d2c = zip(*[layer2(i, 1 + k, h1c[k]) for k in range(2)])
         qc = [q_of(k, h2c[k], jb3_s[k]) for k in range(2)]
         uq = first(1, 3, jnp.concatenate([jnp.where(live, a1, xa[0:8]), xt[0:16]], axis=0))
         ht = [act(un[k * HID : (k + 1) * HID])[0] for k in range(2)]
-        ht = [layer2(3 + k, ht[k])[0] for k in range(2)]
+        ht = [layer2(i, 3 + k, ht[k])[0] for k in range(2)]
         qt = [q_of(2 + k, ht[k], lb3_s[k]) for k in range(2)]
         h1q, d1q = zip(*[act(uq[k * HID : (k + 1) * HID]) for k in range(2)])
         y = reward + GAMMA * (1.0 - done) * (softmin(qt[0], qt[1]) - alpha * lp2)
-        h2q, d2q = zip(*[layer2(1 + k, h1q[k]) for k in range(2)])
+        h2q, d2q = zip(*[layer2(i, 1 + k, h1q[k]) for k in range(2)])
         qq = [q_of(k, h2q[k], jb3_s[k]) for k in range(2)]
 
         closs = jnp.zeros((1, T), F32)
@@ -410,11 +419,11 @@
         da = jnp.zeros((8, T), F32)
         for k, pk in enumerate((p0, 1.0 - p0)):
             g2 = ((-pk * mask) * d2q[k]).astype(BF)
-            g1 = (back2(1 + k, g2) * d1q[k]).astype(BF)
+            g1 = (by_chunk(b2, 1 + k, i, g2) * d1q[k]).astype(BF)
             w = dot(da_w[k], g1)
             da = da + w[0:8] + w[8:16]
         for k in range(2):
-            g1 = (back2(1 + k, g2c[k]) * d1c[k]).astype(BF)
+            g1 = (by_chunk(b2, 1 + k, i, g2c[k]) * d1c[k]).astype(BF)
             w = dot_t(xw, g1)
             gcw1[k] += w[0:24] + w[24:48]
         ma = mask * alpha
@@ -428,7 +437,7 @@
         r = dot_t(jnp.concatenate([h1a, ones], axis=0), g2)
         gw2[0] += r[0:HID]
         gw2b[0] += r[HID : HID + 8]
-        g1 = (back2(0, g2) * d1a).astype(BF)
+        g1 = (by_chunk(b2, 0, i, g2) * d1a).astype(BF)
         w = dot_t(xw, g1)
         gaw1[...] += w[0:24] + w[24:48]
         gmisc[2:3, :] += fold(closs)
@@ -574,20 +583,21 @@
             copy.wait_recv()
             done.append(copy)
 
-    def step(j, c):
-        if 1 <= j <= ns:
-            add(j - 1, c)
-        if j > ns:
-            arrive(2 * ns - j, c)
-        if j < ns:
-            scatter(j, c)
-        elif j < 2 * ns:
-            spread(2 * ns - 1 - j, c)
-
-    for t in range(2 * ns + len(parts)):
-        for j in reversed(range(2 * ns + 1)):
-            if 0 <= t - j < len(parts):
-                step(j, t - j)
+    chunks = range(len(parts))
+    for c in chunks:
+        scatter(0, c)
+    for s in range(ns):
+        for c in chunks:
+            add(s, c)
+            if s < ns - 1:
+                scatter(s + 1, c)
+            else:
+                spread(ns - 1, c)
+    for s in reversed(range(ns)):
+        for c in chunks:
+            arrive(s, c)
+            if s > 0:
+                spread(s - 1, c)
     for copy in done:
         copy.wait_send()
 

time: 118 us -> 113 us (0.958)
  Pallas kernels: 116 us -> 107 us
  local copies, waits for them, and re-layouts: 0.91 us -> 4.14 us
    pallas_call x1, Pallas kernels: 31.4 us -> 23.8 us  [sum_over_devices(): pl.pallas_call(functools.partial(sum_kernel, sizes), out_shape=pltpu.VMEM...]
    unnamed x2 -> x4, local copies, waits for them, and re-layouts: 0.91 us -> 4.14 us
    pallas_call x1, Pallas kernels: 67.5 us -> 65.7 us  [local_grads(): pl.pallas_call(functools.partial(net_kernel, cap=cap, slots=slots), out_s...]
where the time goes in v5:
time: 113 us
  Pallas kernels  107 us (95%)
  local copies, waits for them, and re-layouts  4.14 us (4%)
  between operations  1.34 us (1%)
    pallas_call x1, Pallas kernels, local_grads(): pl.pallas_call(functools.partial(net_kernel, cap=cap, slots=slots), out_s...  65.7 us
    pallas_call x1, Pallas kernels, sum_over_devices(): pl.pallas_call(functools.partial(sum_kernel, sizes), out_shape=pltpu.VMEM...  23.8 us
    pallas_call x1, Pallas kernels, prepare(): pl.pallas_call(functools.partial(prepare_kernel, n=n, cap=cap), out_shape...  15.7 us
    unnamed x4, local copies, waits for them, and re-layouts  4.14 us

profile of v5, /device:TPU:0, one launch (start us, length us, event | category | flops | bytes accessed | tf_op | source)
XLA Modules:
  0.0 112.8 jit_solution(12692700530753450243)
XLA Ops:
  1.3 15.7 %exchange_and_prepare.1 = (f32[16384,128]{1,0:T(8,128)S(1)}, s32[32,8,128]{2,1,0:T(8,128)S(1)}, s32[32,2,128]{2,1,0:T(2,128)S(4)}, bf16[1280,72]{1,0:T(8,128)(2,...) custom-call(s32[1,32,256]{2,1,0:T(8,128)} %idx_h.1, ...), custom_call_target="tpu_custom_call" | custom-call | tf_op jit(solution)/shard_map/exchange_and_prepare/pallas_call | solution.py:233
  17.0 0.0 copy-start
  17.0 3.2 %copy-done = f32[16384,128]{1,0:T(8,128)} copy-done((f32[16384,128]{1,0:T(8,128)}, f32[16384,128]{1,0:T(8,128)S(1)}, u32[]{:S(2)}) %copy-start) | copy-done | bytes 8388632
  20.2 65.7 %networks.1 = f32[1792,128]{1,0:T(8,128)S(1)} custom-call(s32[32,2,128]{2,1,0:T(2,128)S(4)} %get-tuple-element.42.idx_s, f32[8]{0:T(128)S(4)} %get-tuple-element.41.scal, f32[16384,128]{1,0:T(8,128)} %copy-done, s32[32,8,128]{2,1,0:T(8,128)S(1)} %get-tuple-element.44.got, bf16[1280,72]{1,0:T(8,128)(2,1)S(1)} %get-tuple-element.45.w1all, ...), custom_call_target="tpu_custom_call" | custom-call | tf_op jit(solution)/shard_map/networks/pallas_call | solution.py:479
  85.9 23.8 %sum_over_devices.1 = f32[32,56,128]{2,1,0:T(8,128)S(1)} custom-call(f32[32,56,128]{2,1,0:T(8,128)S(1)} %bitcast.18), custom_call_target="tpu_custom_call" | custom-call | tf_op jit(solution)/shard_map/sum_over_devices/pallas_call | solution.py:615
  109.7 0.0 copy-start.1
  109.7 0.9 copy-done.1
  110.6 2.2 %finish.1 = (f32[17,256]{1,0:T(8,128)}, f32[1,256]{1,0:T(1,128)}, f32[256,256]{1,0:T(8,128)}, f32[1,256]{1,0:T(1,128)}, f32[12,256]{1,0:T(8,128)}, /*index=5*/f3...) custom-call(f32[8]{0:T(128)S(4)} %get-tuple-element.41.scal, ...), custom_call_target="tpu_custom_call" | custom-call | tf_op jit(solution)/shard_map/finish/pallas_call | solution.py:671
Async XLA Ops:
  17.0 3.2 %copy-start = (f32[16384,128]{1,0:T(8,128)}, f32[16384,128]{1,0:T(8,128)S(1)}, u32[]{:S(2)}) copy-start(f32[16384,128]{1,0:T(8,128)S(1)} %get-tuple-element.43.tab) | copy-start | bytes 25165828
  109.7 0.9 copy-start.1

commit v6 on v5

--- a/solution.py
+++ b/solution.py
@@ -75,7 +75,7 @@
     idx_h, seed_h, cnt_h, buf_h, aw2_h, jw2_h, lw2_h,
     aw1_h, ab1_h, ab2_h, aw3_h, jw1_h, jb1_h, jb2_h, jw3_h, lw1_h, lb1_h, lb2_h, lw3_h,
     ab3_h, jb3_h, lb3_h, level,
-    tab, got, idx_s, w1all, f2, b2, head, headb, da_w, qw, col, scale, scal,
+    tab, got, idx_s, w1all, fa, f2, b2, head, headb, da_w, qw, col, scale, scal,
     idx_v, seed_v, cnt_v, buf, w2, aw1, ab1, ab2, aw3, jw1, jb1, jb2, jw3, lw1, lb1, lb2, lw3,
     ab3, jb3, lb3, msg, land, flat, tmp, rowbuf, in_sems, sems,
     *, n, cap,
@@ -139,7 +139,12 @@
 
     for l in range(5):
         w = 0.5 * w2[l]
-        roundings(f2, l, w.T)
+        wt = w.T
+        roundings(f2, l, wt)
+        if l == 0:
+            hi, lo = split(wt)
+            fa[0:HID, :] = hi.astype(BF)
+            fa[HID:, :] = lo.astype(BF)
         if l == 0:
             roundings(b2, l, w)
         elif l < 3:
@@ -220,6 +225,7 @@
         pltpu.VMEM((n, 8, 128), jnp.int32),
         pltpu.SMEM((n, rows, 128), jnp.int32),
         pltpu.VMEM((5 * HID, 72), BF),
+        pltpu.VMEM((2 * HID, HID), BF),
         pltpu.VMEM((5, VARIANTS, HID, HID), BF),
         pltpu.VMEM((3, VARIANTS, HID, HID), BF),
         pltpu.VMEM((32, HID), BF),
@@ -234,7 +240,7 @@
         functools.partial(prepare_kernel, n=n, cap=cap),
         out_shape=out,
         in_specs=[hbm] * 22 + [sm],
-        out_specs=[vm, vm, sm] + [vm] * 9 + [sm],
+        out_specs=[vm, vm, sm] + [vm] * 10 + [sm],
         scratch_shapes=[
             pltpu.VMEM((1, n, cap), jnp.int32),
             pltpu.VMEM((1, n, cap), jnp.int32),
@@ -281,7 +287,7 @@
 
 
 def net_kernel(
-    idx_s, scal, tab, got, w1all, f2, b2, head, headb, da_w, qw, col, scale,
+    idx_s, scal, tab, got, w1all, fa, f2, b2, head, headb, da_w, qw, col, scale,
     packed,
     xrow, gw2, gw2b, gaw1, gcw1, gaw3, gcw3, gcol, gmisc,
     *, cap, slots,
@@ -304,11 +310,15 @@
     jb3_s = (scal[0], scal[1])
     lb3_s = (scal[2], scal[3])
 
-    def act(u):
+    def act32(u):
         t = jnp.tanh(u)
         p = 1.0 + t
         h = u * p
-        return h.astype(BF), p + h * (2.0 - p)
+        return h, p + h * (2.0 - p)
+
+    def act(u):
+        h, d = act32(u)
+        return h.astype(BF), d
 
     def layer2(i, l, h):
         return act(by_chunk(f2, l, i, h) + col[:, l : l + 1])
@@ -324,9 +334,15 @@
             [dot(w[l, lax.rem(i * nq + q, VARIANTS)], x[:, q * HID : (q + 1) * HID]) for q in range(nq)], axis=1
         )
 
-    def head_out(h2):
-        r = dot(head[...], h2)
-        o = r[0:16] + r[16:32] + col[0:16, 5:6]
+    def exact(w, h):
+        hb = h.astype(BF)
+        r = dot(w[...], hb)
+        half = r.shape[0] // 2
+        lo = dot(w[0:half, :], (h - hb.astype(F32)).astype(BF))
+        return hb, r[:half] + (r[half:] + lo)
+
+    def head_out(o):
+        o = o + col[0:16, 5:6]
         mean = o[0:8]
         t = jnp.tanh(o[8:16])
         ls = -5.0 + 3.5 * (t + 1.0)
@@ -379,13 +395,16 @@
         eps = noise(seeds, row16)
         e = eps[0:8]
         hn, _ = act(un)
-        h1a, d1a = act(ua[0:HID])
+        h1a, d1a = act32(ua[0:HID])
         h1c, d1c = zip(*[act(ua[(1 + k) * HID : (2 + k) * HID]) for k in range(2)])
         hn, _ = layer2(i, 0, hn)
-        mean, _, ls = head_out(hn)
+        r = dot(head[...], hn)
+        mean, _, ls = head_out(r[0:16] + r[16:32])
         a2, _, lp2 = sample(mean, ls, eps[8:16], live)
-        h2a, d2a = layer2(i, 0, h1a)
-        mean, t, ls = head_out(h2a)
+        h1a, r = exact(fa, h1a)
+        h2a, d2a = act32(r + col[:, 0:1])
+        h2a, r = exact(head, h2a)
+        mean, t, ls = head_out(r)
         a1, sg, lp = sample(mean, ls, e, live)
         un = first(3, 5, jnp.concatenate([jnp.where(live, a2, n_lo), xt[24:40]], axis=0))
         h2c, d2c = zip(*[layer2(i, 1 + k, h1c[k]) for k in range(2)])
@@ -418,10 +437,9 @@
         p0 = 1.0 / (1.0 + jnp.exp(4.0 * (qq[0] - qq[1])))
         da = jnp.zeros((8, T), F32)
         for k, pk in enumerate((p0, 1.0 - p0)):
-            g2 = ((-pk * mask) * d2q[k]).astype(BF)
-            g1 = (by_chunk(b2, 1 + k, i, g2) * d1q[k]).astype(BF)
+            g1 = (by_chunk(b2, 1 + k, i, d2q[k].astype(BF)) * d1q[k]).astype(BF)
             w = dot(da_w[k], g1)
-            da = da + w[0:8] + w[8:16]
+            da = da - (pk * mask) * (w[0:8] + w[8:16])
         for k in range(2):
             g1 = (by_chunk(b2, 1 + k, i, g2c[k]) * d1c[k]).astype(BF)
             w = dot_t(xw, g1)
@@ -492,7 +510,7 @@
             pltpu.VMEM((16, 128), F32),
             pltpu.VMEM((8, 128), F32),
         ],
-        compiler_params=pltpu.CompilerParams(vmem_limit_bytes=40 << 20),
+        compiler_params=pltpu.CompilerParams(vmem_limit_bytes=34 << 20),
         name="networks",
     )(idx_s, scal, tab, got, *weights)
 

time: 113 us -> 105 us (0.929)
  Pallas kernels: 107 us -> 103 us
  local copies, waits for them, and re-layouts: 4.14 us -> 0.91 us
    pallas_call x1, Pallas kernels: 65.7 us -> 61.1 us  [local_grads(): pl.pallas_call(functools.partial(net_kernel, cap=cap, slots=slots), out_s...]
    unnamed x4 -> x2, local copies, waits for them, and re-layouts: 4.14 us -> 0.91 us
where the time goes in v6:
time: 105 us
  Pallas kernels  103 us (98%)
  between operations  1.33 us (1%)
    pallas_call x1, Pallas kernels, local_grads(): pl.pallas_call(functools.partial(net_kernel, cap=cap, slots=slots), out_s...  61.1 us
    pallas_call x1, Pallas kernels, sum_over_devices(): pl.pallas_call(functools.partial(sum_kernel, sizes), out_shape=pltpu.VMEM...  23.8 us
    pallas_call x1, Pallas kernels, prepare(): pl.pallas_call(functools.partial(prepare_kernel, n=n, cap=cap), out_shape...  15.7 us
    pallas_call x1, Pallas kernels, finish(): pl.pallas_call(finish_kernel, out_shape=[jax.ShapeDtypeStruct(x, F32) for...  2.2 us

profile of v6, /device:TPU:0, one launch (start us, length us, event | category | flops | bytes accessed | tf_op | source)
XLA Modules:
  0.0 105.0 jit_solution(4093060159741681297)
XLA Ops:
  1.3 15.7 %exchange_and_prepare.1 = (f32[16384,128]{1,0:T(8,128)S(1)}, s32[32,8,128]{2,1,0:T(8,128)S(1)}, s32[32,2,128]{2,1,0:T(2,128)S(4)}, bf16[1280,72]{1,0:T(8,128)(2,...) custom-call(s32[1,32,256]{2,1,0:T(8,128)} %idx_h.1, ...), custom_call_target="tpu_custom_call" | custom-call | tf_op jit(solution)/shard_map/exchange_and_prepare/pallas_call | solution.py:239
  17.0 61.1 %networks.1 = f32[1792,128]{1,0:T(8,128)S(1)} custom-call(s32[32,2,128]{2,1,0:T(2,128)S(4)} %get-tuple-element.43.idx_s, f32[8]{0:T(128)S(4)} %get-tuple-element.42.scal, f32[16384,128]{1,0:T(8,128)S(1)} %get-tuple-element.44.tab, s32[32,8,128]{2,1,0:T(8,128)S(1)} %get-tuple-element.45.got, bf16[1280,72]{1,0:T(8,128)(2,1)S(1)} %get-tuple-element.46.w1all, ...), custom_call_target="tpu_custom_call" | custom-call | tf_op jit(solution)/shard_map/networks/pallas_call | solution.py:497
  78.1 23.8 %sum_over_devices.1 = f32[32,56,128]{2,1,0:T(8,128)S(1)} custom-call(f32[32,56,128]{2,1,0:T(8,128)S(1)} %bitcast.18), custom_call_target="tpu_custom_call" | custom-call | tf_op jit(solution)/shard_map/sum_over_devices/pallas_call | solution.py:633
  101.9 0.0 copy-start
  101.9 0.9 copy-done
  102.8 2.2 %finish.1 = (f32[17,256]{1,0:T(8,128)}, f32[1,256]{1,0:T(1,128)}, f32[256,256]{1,0:T(8,128)}, f32[1,256]{1,0:T(1,128)}, f32[12,256]{1,0:T(8,128)}, /*index=5*/f3...) custom-call(f32[8]{0:T(128)S(4)} %get-tuple-element.42.scal, ...), custom_call_target="tpu_custom_call" | custom-call | tf_op jit(solution)/shard_map/finish/pallas_call | solution.py:689
Async XLA Ops:
  101.9 0.9 copy-start

commit v7 on v6

--- a/solution.py
+++ b/solution.py
@@ -16,13 +16,15 @@
 TILE = 1024
 CHUNKS = 4
 VARIANTS = 8
-R_AW1 = 6 * HID
-R_CW1 = R_AW1 + 48
-R_AW3 = R_CW1 + 96
-R_COL = R_AW3 + 32
-R_AB3 = R_COL + 16
+R_CW1 = 4 * HID
+R_CCOL = R_CW1 + 96
+R_CEND = R_CCOL + 16
+R_AW1 = 2 * HID
+R_AW3 = R_AW1 + 48
+R_ACOL = R_AW3 + 32
+R_AB3 = R_ACOL + 16
 R_MISC = R_AB3 + 16
-R_END = R_MISC + 8
+R_AEND = R_MISC + 8
 BF = jnp.bfloat16
 F32 = jnp.float32
 
@@ -286,17 +288,146 @@
     )
 
 
+def split_sizes(n):
+    sizes = [2]
+    n //= 2
+    while n > 1:
+        f = 4 if n % 4 == 0 else n if n < 4 else 2
+        sizes.append(f)
+        n //= f
+    return sizes
+
+
+def chunk_rows(rows, chunks):
+    units = rows // 8
+    k = min(chunks, units)
+    cuts = [8 * (units * j // k) for j in range(k + 1)]
+    return list(zip(cuts[:-1], cuts[1:]))
+
+
+def piece_rows(end, n):
+    return 8 * (-(-end // (8 * n)))
+
+
+class DeviceSum:
+    def __init__(self, sizes, parts, mine, out, got, part, sems):
+        self.sizes, self.parts, self.mine, self.out, self.got, self.part, self.sems = sizes, parts, mine, out, got, part, sems
+        self.me = lax.axis_index("dp")
+        self.digits, self.strides, st = [], [], 1
+        for f in sizes:
+            self.digits.append(lax.rem(self.me // st, f))
+            self.strides.append(st)
+            st *= f
+        self.spans, self.starts = [mine.shape[0]], [0]
+        for s, f in enumerate(sizes):
+            self.spans.append(self.spans[s] // f)
+            self.starts.append(self.starts[s] + self.digits[s] * self.spans[s + 1])
+
+    def member(self, s, k):
+        d = lax.rem(self.digits[s] + k, self.sizes[s])
+        return d, self.me + (d - self.digits[s]) * self.strides[s]
+
+    def partners(self):
+        return [self.member(s, k)[1] for s in range(len(self.sizes)) for k in range(1, self.sizes[s])]
+
+    def copy(self, phase, s, k, c):
+        lo, hi = self.parts[c]
+        d, to = self.member(s, k)
+        if phase == 0:
+            src = self.source(s).at[pl.ds(d * self.spans[s + 1], self.spans[s + 1]), lo:hi]
+            dst = self.got[s].at[k - 1, :, lo:hi]
+        else:
+            src = dst = self.out.at[pl.ds(self.starts[s + 1], self.spans[s + 1]), lo:hi]
+        return pltpu.make_async_remote_copy(
+            src_ref=src, dst_ref=dst, send_sem=self.sems.at[phase, c, s, k, 0], recv_sem=self.sems.at[phase, c, s, k, 1],
+            device_id=(to,), device_id_type=pl.DeviceIdType.MESH,
+        )
+
+    def source(self, s):
+        return self.mine if s == 0 else self.part[s - 1]
+
+    def start(self, phase, s, c):
+        for k in range(1, self.sizes[s]):
+            self.copy(phase, s, k, c).start()
+
+    def add(self, s, c):
+        lo, hi = self.parts[c]
+        span = self.spans[s + 1]
+        acc = self.source(s)[pl.ds(self.digits[s] * span, span), lo:hi]
+        for k in range(1, self.sizes[s]):
+            self.copy(0, s, k, c).wait_recv()
+            acc = acc + self.got[s][k - 1, :, lo:hi]
+        if s == len(self.sizes) - 1:
+            self.out[pl.ds(self.starts[s + 1], 1), lo:hi] = acc
+        else:
+            self.part[s][:, lo:hi] = acc
+
+    def step(self, j, c):
+        ns = len(self.sizes)
+        if 1 <= j <= ns:
+            self.add(j - 1, c)
+        if j > ns:
+            for k in range(1, self.sizes[2 * ns - j]):
+                self.copy(1, 2 * ns - j, k, c).wait_recv()
+        if j < ns:
+            self.start(0, j, c)
+        elif j < 2 * ns:
+            self.start(1, 2 * ns - 1 - j, c)
+
+    def steps(self):
+        return 2 * len(self.sizes)
+
+    def all_sent(self):
+        for phase in range(2):
+            for s in range(len(self.sizes)):
+                for k in range(1, self.sizes[s]):
+                    for c in range(len(self.parts)):
+                        self.copy(phase, s, k, c).wait_send()
+
+
+def sum_scratch(n, rows, chunks):
+    sizes = split_sizes(n)
+    got, part, size = [], [], n
+    for f in sizes:
+        size //= f
+        got.append(pltpu.VMEM((f - 1, size, rows, 128), F32))
+        part.append(pltpu.VMEM((size, rows, 128), F32))
+    sems = pltpu.SemaphoreType.DMA((2, len(chunk_rows(rows, chunks)), len(sizes), max(sizes), 2))
+    return [pltpu.VMEM((n, rows, 128), F32)] + got + part + [sems]
+
+
+def put(dst, at, value):
+    rows = dst.shape[1]
+    r = 0
+    while r < value.shape[0]:
+        p, o = divmod(at + r, rows)
+        k = min(rows - o, value.shape[0] - r)
+        dst[p, o : o + k, :] = value[r : r + k]
+        r += k
+
+
 def net_kernel(
     idx_s, scal, tab, got, w1all, fa, f2, b2, head, headb, da_w, qw, col, scale,
-    packed,
-    xrow, gw2, gw2b, gaw1, gcw1, gaw3, gcw3, gcol, gmisc,
-    *, cap, slots,
+    sum_c, sum_a,
+    xrow, xkeep, ekeep, gw2, gw2b, gaw1, gcw1, gaw3, gcw3, gcol, gmisc, *rest,
+    n, cap, slots,
 ):
     T = min(TILE, slots)
     nt = slots // T
     lists = T // cap
     rows = message_rows(cap)
     part = min(cap, 128)
+    sizes = split_sizes(n)
+    ns = len(sizes)
+    per = 2 * ns + 2
+    critic_sum, actor_sum = (
+        DeviceSum(sizes, chunk_rows(r[0].shape[1], k), r[0], out, r[1 : 1 + ns], r[1 + ns : 1 + 2 * ns], r[1 + 2 * ns])
+        for r, out, k in ((rest[:per], sum_c, 1), (rest[per:], sum_a, CHUNKS))
+    )
+    barrier = pltpu.get_barrier_semaphore()
+    partners = critic_sum.partners()
+    for to in partners:
+        pl.semaphore_signal(barrier, inc=1, device_id=(to,), device_id_type=pl.DeviceIdType.MESH)
 
     def gather(i):
         for t in range(T):
@@ -367,18 +498,22 @@
 
     ones = jnp.ones((16, T), BF)
 
+    row8 = lax.broadcasted_iota(jnp.int32, (8, T), 0)
+    row16 = lax.broadcasted_iota(jnp.int32, (16, T), 0)
+    live = row8 < ACT
+
+    def mask_of(i):
+        lane = lax.broadcasted_iota(jnp.int32, (1, cap), 1)
+        return jnp.concatenate(
+            [jnp.where(lane < got[i * lists + k, 2 * rows : 2 * rows + 1, 0:1], 1.0, 0.0).astype(F32) for k in range(lists)], axis=1
+        )
+
     @pl.loop(0, nt)
     def _(i):
         xt = xrow[...].T
         gather(jnp.minimum(i + 1, nt - 1))
-        row8 = lax.broadcasted_iota(jnp.int32, (8, T), 0)
-        row16 = lax.broadcasted_iota(jnp.int32, (16, T), 0)
-        live = row8 < ACT
         seeds = jnp.concatenate([got[i * lists + k, rows + r : rows + r + 1, 0:part] for k in range(lists) for r in range(rows)], axis=1)
-        lane = lax.broadcasted_iota(jnp.int32, (1, cap), 1)
-        mask = jnp.concatenate(
-            [jnp.where(lane < got[i * lists + k, 2 * rows : 2 * rows + 1, 0:1], 1.0, 0.0).astype(F32) for k in range(lists)], axis=1
-        )
+        mask = mask_of(i)
         alpha = jnp.exp(jnp.full((1, T), level, F32))
         b1 = pltpu.roll(xt[16:24], 7, 0)
         reward = b1[6:7]
@@ -387,52 +522,85 @@
         done = b2_[0:1]
         n_lo = jnp.where(row8 == 7, b2_, jnp.where(row8 == 6, 1.0, 0.0))
         xn = jnp.concatenate([n_lo, xt[24:40]], axis=0)
+        eps = noise(seeds, row16)
+        xkeep[i] = xa
+        ekeep[i] = eps[0:8]
 
         un = first(0, 1, xn)
         hi, lo = split(xa)
         xw = jnp.concatenate([hi, lo], axis=0).astype(BF)
-        ua = dot(w1all[0 : 3 * HID, :], jnp.concatenate([hi, lo, hi], axis=0).astype(BF))
-        eps = noise(seeds, row16)
-        e = eps[0:8]
+        ua = dot(w1all[HID : 3 * HID, :], jnp.concatenate([hi, lo, hi], axis=0).astype(BF))
         hn, _ = act(un)
-        h1a, d1a = act32(ua[0:HID])
-        h1c, d1c = zip(*[act(ua[(1 + k) * HID : (2 + k) * HID]) for k in range(2)])
+        h1c, d1c = zip(*[act(ua[k * HID : (1 + k) * HID]) for k in range(2)])
         hn, _ = layer2(i, 0, hn)
         r = dot(head[...], hn)
         mean, _, ls = head_out(r[0:16] + r[16:32])
         a2, _, lp2 = sample(mean, ls, eps[8:16], live)
-        h1a, r = exact(fa, h1a)
-        h2a, d2a = act32(r + col[:, 0:1])
-        h2a, r = exact(head, h2a)
-        mean, t, ls = head_out(r)
-        a1, sg, lp = sample(mean, ls, e, live)
         un = first(3, 5, jnp.concatenate([jnp.where(live, a2, n_lo), xt[24:40]], axis=0))
         h2c, d2c = zip(*[layer2(i, 1 + k, h1c[k]) for k in range(2)])
         qc = [q_of(k, h2c[k], jb3_s[k]) for k in range(2)]
-        uq = first(1, 3, jnp.concatenate([jnp.where(live, a1, xa[0:8]), xt[0:16]], axis=0))
         ht = [act(un[k * HID : (k + 1) * HID])[0] for k in range(2)]
         ht = [layer2(i, 3 + k, ht[k])[0] for k in range(2)]
         qt = [q_of(2 + k, ht[k], lb3_s[k]) for k in range(2)]
-        h1q, d1q = zip(*[act(uq[k * HID : (k + 1) * HID]) for k in range(2)])
         y = reward + GAMMA * (1.0 - done) * (softmin(qt[0], qt[1]) - alpha * lp2)
-        h2q, d2q = zip(*[layer2(i, 1 + k, h1q[k]) for k in range(2)])
-        qq = [q_of(k, h2q[k], jb3_s[k]) for k in range(2)]
-
         closs = jnp.zeros((1, T), F32)
-        g2c = []
         for k in range(2):
             dq = qc[k] - y
             mdq = dq * mask
             closs = closs + 0.5 * (mdq * dq)
             g2 = (mdq * d2c[k]).astype(BF)
-            g2c.append(g2)
             mhi, mlo = split(mdq)
             m16 = jnp.where(row16 == 0, mhi, jnp.where(row16 == 1, mlo, 0.0)).astype(BF)
             gcw3[k] += dot_t(m16, h2c[k])
             r = dot_t(jnp.concatenate([h1c[k], ones], axis=0), g2)
             gw2[1 + k] += r[0:HID]
             gw2b[1 + k] += r[HID : HID + 8]
+            g1 = (by_chunk(b2, 1 + k, i, g2) * d1c[k]).astype(BF)
+            w = dot_t(xw, g1)
+            gcw1[k] += w[0:24] + w[24:48]
             gmisc[k : k + 1, :] += fold(mdq)
+        gmisc[2:3, :] += fold(closs)
+
+    mine = critic_sum.mine
+    mine[...] = jnp.zeros_like(mine)
+    row8h = lax.broadcasted_iota(jnp.int32, (8, HID), 0)
+    cols = jnp.zeros((8, HID), F32)
+    for k in range(2):
+        s = scale[k : k + 1, :]
+        cols = jnp.where(row8h == k, gw2b[1 + k] * s, cols)
+        cols = jnp.where(row8h == 2 + k, gcw3[k, 0:1, :] + gcw3[k, 1:2, :], cols)
+        for h in range(2):
+            at = slice(h * 128, (h + 1) * 128)
+            put(mine, (2 * k + h) * HID, gw2[1 + k, :, at] * s[:, at])
+            put(mine, R_CW1 + 48 * k + 24 * h, gcw1[k, :, at])
+    for h in range(2):
+        put(mine, R_CCOL + 8 * h, cols[:, h * 128 : (h + 1) * 128])
+    pl.semaphore_wait(barrier, len(partners))
+    critic_sum.step(0, 0)
+    last = critic_sum.steps()
+    when = (0, 1, 3, 4, 5, 7, 8) if (last, nt) == (6, 8) else tuple(j * nt // last for j in range(last + 1))
+
+    @pl.loop(0, nt)
+    def _(i):
+        for j in range(1, last + 1):
+            if when[j] < nt:
+                pl.when(i == when[j])(functools.partial(critic_sum.step, j, 0))
+        mask = mask_of(i)
+        alpha = jnp.exp(jnp.full((1, T), level, F32))
+        xa = xkeep[i]
+        e = ekeep[i]
+        hi, lo = split(xa)
+        xw = jnp.concatenate([hi, lo], axis=0).astype(BF)
+        h1a, d1a = act32(dot(w1all[0:HID, :], jnp.concatenate([hi, lo, hi], axis=0).astype(BF)))
+        h1a, r = exact(fa, h1a)
+        h2a, d2a = act32(r + col[:, 0:1])
+        h2a, r = exact(head, h2a)
+        mean, t, ls = head_out(r)
+        a1, sg, lp = sample(mean, ls, e, live)
+        uq = first(1, 3, jnp.concatenate([jnp.where(live, a1, xa[0:8]), xa[8:24]], axis=0))
+        h1q, d1q = zip(*[act(uq[k * HID : (k + 1) * HID]) for k in range(2)])
+        h2q, d2q = zip(*[layer2(i, 1 + k, h1q[k]) for k in range(2)])
+        qq = [q_of(k, h2q[k], jb3_s[k]) for k in range(2)]
         sm = softmin(qq[0], qq[1])
         p0 = 1.0 / (1.0 + jnp.exp(4.0 * (qq[0] - qq[1])))
         da = jnp.zeros((8, T), F32)
@@ -440,10 +608,6 @@
             g1 = (by_chunk(b2, 1 + k, i, d2q[k].astype(BF)) * d1q[k]).astype(BF)
             w = dot(da_w[k], g1)
             da = da - (pk * mask) * (w[0:8] + w[8:16])
-        for k in range(2):
-            g1 = (by_chunk(b2, 1 + k, i, g2c[k]) * d1c[k]).astype(BF)
-            w = dot_t(xw, g1)
-            gcw1[k] += w[0:24] + w[24:48]
         ma = mask * alpha
         du = da * (1.0 - a1 * a1) + ma * (2.0 * a1)
         dls = (du * sg * e - ma) * (3.5 * (1.0 - t * t))
@@ -458,49 +622,48 @@
         g1 = (by_chunk(b2, 0, i, g2) * d1a).astype(BF)
         w = dot_t(xw, g1)
         gaw1[...] += w[0:24] + w[24:48]
-        gmisc[2:3, :] += fold(closs)
         gmisc[3:4, :] += fold(mask * (alpha * lp - sm))
         gmisc[4:5, :] += fold(mask * (lp - 6.0))
         gmisc[5:6, :] += fold(mask)
 
-    row8 = lax.broadcasted_iota(jnp.int32, (8, HID), 0)
-    cols = jnp.zeros((8, HID), F32)
-    for k in range(2):
-        s = scale[k : k + 1, :]
-        cols = jnp.where(row8 == k, gw2b[1 + k] * s, cols)
-        cols = jnp.where(row8 == 2 + k, gcw3[k, 0:1, :] + gcw3[k, 1:2, :], cols)
-    cols = jnp.where(row8 == 4, gw2b[0], cols)
-    for m in range(3):
-        for h in range(2):
-            w = gw2[m, :, h * 128 : (h + 1) * 128]
-            if m > 0:
-                w = w * scale[m - 1 : m, h * 128 : (h + 1) * 128]
-            packed[(2 * m + h) * HID : (2 * m + h + 1) * HID, :] = w
+    mine = actor_sum.mine
+    mine[...] = jnp.zeros_like(mine)
     for h in range(2):
-        packed[R_AW1 + 24 * h : R_AW1 + 24 * (h + 1), :] = gaw1[:, h * 128 : (h + 1) * 128]
-        for k in range(2):
-            at = R_CW1 + 48 * k + 24 * h
-            packed[at : at + 24, :] = gcw1[k, :, h * 128 : (h + 1) * 128]
-        packed[R_AW3 + 16 * h : R_AW3 + 16 * (h + 1), :] = gaw3[:, h * 128 : (h + 1) * 128]
-        packed[R_COL + 8 * h : R_COL + 8 * (h + 1), :] = cols[:, h * 128 : (h + 1) * 128]
-    packed[R_AB3 : R_AB3 + 16, :] = gcol[...]
-    packed[R_MISC : R_MISC + 8, :] = gmisc[...]
-    packed[R_END:, :] = jnp.zeros((packed.shape[0] - R_END, 128), F32)
-
-
-def local_grads(ready, n, cap, packed_rows):
+        at = slice(h * 128, (h + 1) * 128)
+        put(mine, h * HID, gw2[0, :, at])
+        put(mine, R_AW1 + 24 * h, gaw1[:, at])
+        put(mine, R_AW3 + 16 * h, gaw3[:, at])
+        put(mine, R_ACOL + 8 * h, gw2b[0, :, at])
+    put(mine, R_AB3, gcol[...])
+    put(mine, R_MISC, gmisc[...])
+    for c in range(len(actor_sum.parts)):
+        actor_sum.step(0, c)
+    for j in range(1, last + 1):
+        if when[j] >= nt:
+            critic_sum.step(j, 0)
+    for j in range(1, last + 1):
+        for c in range(len(actor_sum.parts)):
+            actor_sum.step(j, c)
+    critic_sum.all_sent()
+    actor_sum.all_sent()
+
+
+def summed_grads(ready, n, cap):
     tab, got, idx_s, *weights, scal = ready
     slots = n * cap
     T = min(TILE, slots)
+    rows_c, rows_a = piece_rows(R_CEND, n), piece_rows(R_AEND, n)
     vm = pl.BlockSpec(memory_space=pltpu.VMEM)
     sm = pl.BlockSpec(memory_space=pltpu.SMEM)
     return pl.pallas_call(
-        functools.partial(net_kernel, cap=cap, slots=slots),
-        out_shape=pltpu.VMEM((packed_rows, 128), F32),
+        functools.partial(net_kernel, n=n, cap=cap, slots=slots),
+        out_shape=[pltpu.VMEM((n, rows_c, 128), F32), pltpu.VMEM((n, rows_a, 128), F32)],
         in_specs=[sm] * 2 + [vm] * (2 + len(weights)),
-        out_specs=vm,
+        out_specs=[vm, vm],
         scratch_shapes=[
             pltpu.VMEM((T, 128), F32),
+            pltpu.VMEM((slots // T, 24, T), F32),
+            pltpu.VMEM((slots // T, 8, T), F32),
             pltpu.VMEM((3, HID, HID), F32),
             pltpu.VMEM((3, 8, HID), F32),
             pltpu.VMEM((24, HID), F32),
@@ -509,168 +672,42 @@
             pltpu.VMEM((2, 16, HID), F32),
             pltpu.VMEM((16, 128), F32),
             pltpu.VMEM((8, 128), F32),
-        ],
-        compiler_params=pltpu.CompilerParams(vmem_limit_bytes=34 << 20),
+        ]
+        + sum_scratch(n, rows_c, 1)
+        + sum_scratch(n, rows_a, CHUNKS),
+        compiler_params=pltpu.CompilerParams(collective_id=1, has_side_effects=True, vmem_limit_bytes=34 << 20),
         name="networks",
     )(idx_s, scal, tab, got, *weights)
 
 
-def split_sizes(n):
-    sizes = [2]
-    n //= 2
-    while n > 1:
-        f = 4 if n % 4 == 0 else n if n < 4 else 2
-        sizes.append(f)
-        n //= f
-    return sizes
-
-
-def chunk_rows(rows):
-    units = rows // 8
-    k = min(CHUNKS, units)
-    cuts = [8 * (units * j // k) for j in range(k + 1)]
-    return list(zip(cuts[:-1], cuts[1:]))
-
-
-def sum_kernel(sizes, mine, out, *rest):
-    ns = len(sizes)
-    got, part, sems = rest[:ns], rest[ns : 2 * ns], rest[2 * ns]
-    n = mine.shape[0]
-    parts = chunk_rows(mine.shape[1])
-    me = lax.axis_index("dp")
-    digits, strides, st = [], [], 1
-    for f in sizes:
-        digits.append(lax.rem(me // st, f))
-        strides.append(st)
-        st *= f
-
-    def member(s, k):
-        d = lax.rem(digits[s] + k, sizes[s])
-        return d, me + (d - digits[s]) * strides[s]
-
-    barrier = pltpu.get_barrier_semaphore()
-    count = 0
-    for s in range(ns):
-        for k in range(1, sizes[s]):
-            pl.semaphore_signal(barrier, inc=1, device_id=(member(s, k)[1],), device_id_type=pl.DeviceIdType.MESH)
-            count += 1
-    pl.semaphore_wait(barrier, count)
-
-    def send(src, dst, s, k, phase, c):
-        copy = pltpu.make_async_remote_copy(
-            src_ref=src, dst_ref=dst, send_sem=sems.at[phase, c, s, k, 0], recv_sem=sems.at[phase, c, s, k, 1],
-            device_id=(member(s, k)[1],), device_id_type=pl.DeviceIdType.MESH,
-        )
-        copy.start()
-        return copy
-
-    spans, starts = [n], [0]
-    for s in range(ns):
-        spans.append(spans[s] // sizes[s])
-        starts.append(starts[s] + digits[s] * spans[s + 1])
-    done, flying = [], {}
-
-    def scatter(s, c):
-        lo, hi = parts[c]
-        src = mine if s == 0 else part[s - 1]
-        flying[0, s, c] = [
-            send(src.at[pl.ds(member(s, k)[0] * spans[s + 1], spans[s + 1]), lo:hi], got[s].at[k - 1, :, lo:hi], s, k, 0, c)
-            for k in range(1, sizes[s])
-        ]
-
-    def add(s, c):
-        lo, hi = parts[c]
-        src = mine if s == 0 else part[s - 1]
-        acc = src[pl.ds(digits[s] * spans[s + 1], spans[s + 1]), lo:hi]
-        for k, copy in enumerate(flying[0, s, c]):
-            copy.wait_recv()
-            acc = acc + got[s][k, :, lo:hi]
-            done.append(copy)
-        if s == ns - 1:
-            out[pl.ds(starts[ns], 1), lo:hi] = acc
-        else:
-            part[s][:, lo:hi] = acc
-
-    def spread(s, c):
-        lo, hi = parts[c]
-        at = out.at[pl.ds(starts[s + 1], spans[s + 1]), lo:hi]
-        flying[1, s, c] = [send(at, at, s, k, 1, c) for k in range(1, sizes[s])]
-
-    def arrive(s, c):
-        for copy in flying[1, s, c]:
-            copy.wait_recv()
-            done.append(copy)
-
-    chunks = range(len(parts))
-    for c in chunks:
-        scatter(0, c)
-    for s in range(ns):
-        for c in chunks:
-            add(s, c)
-            if s < ns - 1:
-                scatter(s + 1, c)
-            else:
-                spread(ns - 1, c)
-    for s in reversed(range(ns)):
-        for c in chunks:
-            arrive(s, c)
-            if s > 0:
-                spread(s - 1, c)
-    for copy in done:
-        copy.wait_send()
-
-
-def sum_over_devices(packed, n):
-    sizes = split_sizes(n)
-    rows = packed.shape[0] // n
-    mine = packed.reshape(n, rows, 128)
-    got, part, size = [], [], n
-    for f in sizes:
-        size //= f
-        got.append(pltpu.VMEM((f - 1, size, rows, 128), F32))
-        part.append(pltpu.VMEM((size, rows, 128), F32))
-    vm = pl.BlockSpec(memory_space=pltpu.VMEM)
-    out = pl.pallas_call(
-        functools.partial(sum_kernel, sizes),
-        out_shape=pltpu.VMEM((n, rows, 128), F32),
-        in_specs=[vm],
-        out_specs=vm,
-        scratch_shapes=got + part + [pltpu.SemaphoreType.DMA((2, len(chunk_rows(rows)), len(sizes), max(sizes), 2))],
-        compiler_params=pltpu.CompilerParams(collective_id=1, has_side_effects=True, vmem_limit_bytes=24 << 20),
-        name="sum_over_devices",
-    )(mine)
-    return out.reshape(packed.shape)
-
-
-def finish_kernel(scal, g, aw1, ab1, aw2, ab2, aw3, ab3, cw1, cb1, cw2, cb2, cw3, cb3, da, losses):
-    misc = jnp.sum(g[R_MISC : R_MISC + 8, :], axis=1, keepdims=True)
-    n = misc[5:6]
-    inv = 1.0 / n
-
-    def rows(at, count):
+def finish_kernel(scal, gc, ga, aw1, ab1, aw2, ab2, aw3, ab3, cw1, cb1, cw2, cb2, cw3, cb3, da, losses):
+    misc = jnp.sum(ga[R_MISC : R_MISC + 8, :], axis=1, keepdims=True)
+    inv = 1.0 / misc[5:6]
+
+    def rows(g, at, count):
         return jnp.concatenate([g[at : at + count, :], g[at + count : at + 2 * count, :]], axis=1) * inv
 
-    aw2[...] = rows(0, HID)
-    cw2[0] = rows(2 * HID, HID)
-    cw2[1] = rows(4 * HID, HID)
-    w = rows(R_AW1, 24)
+    aw2[...] = rows(ga, 0, HID)
+    cw2[0] = rows(gc, 0, HID)
+    cw2[1] = rows(gc, 2 * HID, HID)
+    w = rows(ga, R_AW1, 24)
     aw1[0:16, :] = w[8:24]
     aw1[16:17, :] = w[7:8]
     ab1[...] = w[6:7]
     for k in range(2):
-        w = rows(R_CW1 + 48 * k, 24)
+        w = rows(gc, R_CW1 + 48 * k, 24)
         cw1[0:16, k, :] = w[8:24]
         cw1[16:17, k, :] = w[7:8]
         cw1[17:23, k, :] = w[0:6]
         cb1[k : k + 1, :] = w[6:7]
-    w = rows(R_AW3, 16)
+    w = rows(ga, R_AW3, 16)
     aw3[0:6, :] = w[0:6]
     aw3[6:12, :] = w[8:14]
-    c = rows(R_COL, 8)
+    c = rows(gc, R_CCOL, 8)
     cb2[...] = c[0:2]
     cw3[...] = c[2:4]
-    ab2[...] = c[4:5]
-    b = jnp.sum(g[R_AB3 : R_AB3 + 16, :], axis=1, keepdims=True) * inv
+    ab2[...] = rows(ga, R_ACOL, 8)[0:1]
+    b = jnp.sum(ga[R_AB3 : R_AB3 + 16, :], axis=1, keepdims=True) * inv
     diag = lax.broadcasted_iota(jnp.int32, (16, 128), 0) == lax.broadcasted_iota(jnp.int32, (16, 128), 1)
     b = jnp.sum(jnp.where(diag, b, 0.0), axis=0, keepdims=True)
     ab3[...] = jnp.concatenate([b[:, 0:6], b[:, 8:14]], axis=1)
@@ -680,7 +717,7 @@
     losses[...] = jnp.concatenate([m[2:3], m[3:4], -scal[4] * m[4:5]], axis=1)
 
 
-def finish(total, scal):
+def finish(critics, others, scal):
     vm = pl.BlockSpec(memory_space=pltpu.VMEM)
     shapes = [
         (OBS, HID), (1, HID), (HID, HID), (1, HID), (12, HID), (1, 12),
@@ -689,10 +726,11 @@
     outs = list(pl.pallas_call(
         finish_kernel,
         out_shape=[jax.ShapeDtypeStruct(x, F32) for x in shapes],
-        in_specs=[pl.BlockSpec(memory_space=pltpu.SMEM), vm],
+        in_specs=[pl.BlockSpec(memory_space=pltpu.SMEM), vm, vm],
         out_specs=[vm] * len(shapes),
+        compiler_params=pltpu.CompilerParams(vmem_limit_bytes=16 << 20),
         name="finish",
-    )(scal, total))
+    )(scal, critics.reshape(-1, 128), others.reshape(-1, 128)))
     outs[4] = outs[4].T
     outs[6] = outs[6].transpose(1, 0, 2)
     for k, shape in ((1, (HID,)), (3, (HID,)), (5, (12,)), (11, (2,)), (12, ()), (13, (3,))):
@@ -703,8 +741,7 @@
 def body(experience_buffer, sampled_indices, filled_lengths, randomizer_numbers, *params):
     n, cap = sampled_indices.shape[1:]
     ready = prepare(experience_buffer, sampled_indices, randomizer_numbers, filled_lengths, params)
-    packed = local_grads(ready, n, cap, n * 8 * (-(-R_END // (8 * n))))
-    return finish(sum_over_devices(packed, n), ready[-1])
+    return finish(*summed_grads(ready, n, cap), ready[-1])
 
 
 def solution(mesh):

time: 105 us -> 105 us (level)
    pallas_call x2 -> x1, Pallas kernels: 84.8 us -> 86.3 us  [summed_grads(): pl.pallas_call(functools.partial(net_kernel, n=n, cap=cap, slots=slots),...]
    pallas_call x1, Pallas kernels: 2.2 us -> 1.03 us  [finish(): pl.pallas_call(finish_kernel, out_shape=[jax.ShapeDtypeStruct(x, F32) for...]
where the time goes in v7:
time: 105 us; the launch traced here: 104 us
  Pallas kernels  103 us (98%)
  between operations  1.32 us (1%)
    pallas_call x1, Pallas kernels, summed_grads(): pl.pallas_call(functools.partial(net_kernel, n=n, cap=cap, slots=slots),...  86.3 us
    pallas_call x1, Pallas kernels, prepare(): pl.pallas_call(functools.partial(prepare_kernel, n=n, cap=cap), out_shape...  15.7 us

profile of v7, /device:TPU:0, one launch (start us, length us, event | category | flops | bytes accessed | tf_op | source)
XLA Modules:
  0.0 104.4 jit_solution(15085755152423543449)
XLA Ops:
  1.3 15.7 %exchange_and_prepare.1 = (f32[16384,128]{1,0:T(8,128)S(1)}, s32[32,8,128]{2,1,0:T(8,128)S(1)}, s32[32,2,128]{2,1,0:T(2,128)S(4)}, bf16[1280,72]{1,0:T(8,128)(2,...) custom-call(s32[1,32,256]{2,1,0:T(8,128)} %idx_h.1, ...), custom_call_target="tpu_custom_call" | custom-call | tf_op jit(solution)/shard_map/exchange_and_prepare/pallas_call | solution.py:241
  17.0 86.3 %networks.1 = (f32[32,40,128]{2,1,0:T(8,128)S(1)}, f32[32,24,128]{2,1,0:T(8,128)S(1)}) custom-call(s32[32,2,128]{2,1,0:T(2,128)S(4)} %get-tuple-element.45.idx_s, f32[8]{0:T(128)S(4)} %get-tuple-element.44.scal, f32[16384,128]{1,0:T(8,128)S(1)} %get-tuple-element.46.tab, s32[32,8,128]{2,1,0:T(8,128)S(1)} %get-tuple-element.47.got, ...), custom_call_target="tpu_custom_call" | custom-call | tf_op jit(solution)/shard_map/networks/pallas_call | solution.py:658
  103.4 1.0 finish.1

commit v8 on v7

--- a/solution.py
+++ b/solution.py
@@ -14,17 +14,16 @@
 GAMMA = 0.99
 PRIME = 65521
 TILE = 1024
-CHUNKS = 4
+CHUNKS = (2, 1)
 VARIANTS = 8
-R_CW1 = 4 * HID
-R_CCOL = R_CW1 + 96
-R_CEND = R_CCOL + 16
-R_AW1 = 2 * HID
-R_AW3 = R_AW1 + 48
-R_ACOL = R_AW3 + 32
-R_AB3 = R_ACOL + 16
+R_AW1 = 6 * HID
+R_CW1 = R_AW1 + 48
+R_AW3 = R_CW1 + 96
+R_COL = R_AW3 + 32
+R_AB3 = R_COL + 16
 R_MISC = R_AB3 + 16
-R_AEND = R_MISC + 8
+R_END = R_MISC + 8
+R_CUT = 5 * HID
 BF = jnp.bfloat16
 F32 = jnp.float32
 
@@ -288,14 +287,13 @@
     )
 
 
-def split_sizes(n):
-    sizes = [2]
-    n //= 2
-    while n > 1:
-        f = 4 if n % 4 == 0 else n if n < 4 else 2
-        sizes.append(f)
-        n //= f
-    return sizes
+def stage_groups(n):
+    groups, st = [(2, 1)], 2
+    while st < n:
+        f = 4 if (n // st) % 4 == 0 else 2
+        groups.append((f, st))
+        st *= f
+    return groups, groups[:1] + groups[:0:-1]
 
 
 def chunk_rows(rows, chunks):
@@ -310,16 +308,13 @@
 
 
 class DeviceSum:
-    def __init__(self, sizes, parts, mine, out, got, part, sems):
-        self.sizes, self.parts, self.mine, self.out, self.got, self.part, self.sems = sizes, parts, mine, out, got, part, sems
+    def __init__(self, groups, parts, mine, out, got, part, sems):
+        self.sizes, self.strides = [f for f, _ in groups], [st for _, st in groups]
+        self.parts, self.mine, self.out, self.got, self.part, self.sems = parts, mine, out, got, part, sems
         self.me = lax.axis_index("dp")
-        self.digits, self.strides, st = [], [], 1
-        for f in sizes:
-            self.digits.append(lax.rem(self.me // st, f))
-            self.strides.append(st)
-            st *= f
+        self.digits = [lax.rem(self.me // st, f) for f, st in groups]
         self.spans, self.starts = [mine.shape[0]], [0]
-        for s, f in enumerate(sizes):
+        for s, f in enumerate(self.sizes):
             self.spans.append(self.spans[s] // f)
             self.starts.append(self.starts[s] + self.digits[s] * self.spans[s + 1])
 
@@ -385,9 +380,9 @@
                         self.copy(phase, s, k, c).wait_send()
 
 
-def sum_scratch(n, rows, chunks):
-    sizes = split_sizes(n)
+def sum_scratch(groups, n, rows, chunks):
     got, part, size = [], [], n
+    sizes = [f for f, _ in groups]
     for f in sizes:
         size //= f
         got.append(pltpu.VMEM((f - 1, size, rows, 128), F32))
@@ -408,8 +403,8 @@
 
 def net_kernel(
     idx_s, scal, tab, got, w1all, fa, f2, b2, head, headb, da_w, qw, col, scale,
-    sum_c, sum_a,
-    xrow, xkeep, ekeep, gw2, gw2b, gaw1, gcw1, gaw3, gcw3, gcol, gmisc, *rest,
+    sum_q, sum_p,
+    xrow, gw2, gw2b, gaw1, gcw1, gaw3, gcw3, gcol, gmisc, *rest,
     n, cap, slots,
 ):
     T = min(TILE, slots)
@@ -417,15 +412,14 @@
     lists = T // cap
     rows = message_rows(cap)
     part = min(cap, 128)
-    sizes = split_sizes(n)
-    ns = len(sizes)
-    per = 2 * ns + 2
-    critic_sum, actor_sum = (
-        DeviceSum(sizes, chunk_rows(r[0].shape[1], k), r[0], out, r[1 : 1 + ns], r[1 + ns : 1 + 2 * ns], r[1 + 2 * ns])
-        for r, out, k in ((rest[:per], sum_c, 1), (rest[per:], sum_a, CHUNKS))
-    )
+    per = len(rest) // 2
+    ns = (per - 2) // 2
+    sums = [
+        DeviceSum(groups, chunk_rows(r[0].shape[1], k), r[0], out, r[1 : 1 + ns], r[1 + ns : 1 + 2 * ns], r[1 + 2 * ns])
+        for groups, r, out, k in zip(stage_groups(n), (rest[:per], rest[per:]), (sum_q, sum_p), CHUNKS)
+    ]
     barrier = pltpu.get_barrier_semaphore()
-    partners = critic_sum.partners()
+    partners = sums[0].partners()
     for to in partners:
         pl.semaphore_signal(barrier, inc=1, device_id=(to,), device_id_type=pl.DeviceIdType.MESH)
 
@@ -498,22 +492,18 @@
 
     ones = jnp.ones((16, T), BF)
 
-    row8 = lax.broadcasted_iota(jnp.int32, (8, T), 0)
-    row16 = lax.broadcasted_iota(jnp.int32, (16, T), 0)
-    live = row8 < ACT
-
-    def mask_of(i):
-        lane = lax.broadcasted_iota(jnp.int32, (1, cap), 1)
-        return jnp.concatenate(
-            [jnp.where(lane < got[i * lists + k, 2 * rows : 2 * rows + 1, 0:1], 1.0, 0.0).astype(F32) for k in range(lists)], axis=1
-        )
-
     @pl.loop(0, nt)
     def _(i):
         xt = xrow[...].T
         gather(jnp.minimum(i + 1, nt - 1))
+        row8 = lax.broadcasted_iota(jnp.int32, (8, T), 0)
+        row16 = lax.broadcasted_iota(jnp.int32, (16, T), 0)
+        live = row8 < ACT
         seeds = jnp.concatenate([got[i * lists + k, rows + r : rows + r + 1, 0:part] for k in range(lists) for r in range(rows)], axis=1)
-        mask = mask_of(i)
+        lane = lax.broadcasted_iota(jnp.int32, (1, cap), 1)
+        mask = jnp.concatenate(
+            [jnp.where(lane < got[i * lists + k, 2 * rows : 2 * rows + 1, 0:1], 1.0, 0.0).astype(F32) for k in range(lists)], axis=1
+        )
         alpha = jnp.exp(jnp.full((1, T), level, F32))
         b1 = pltpu.roll(xt[16:24], 7, 0)
         reward = b1[6:7]
@@ -522,85 +512,52 @@
         done = b2_[0:1]
         n_lo = jnp.where(row8 == 7, b2_, jnp.where(row8 == 6, 1.0, 0.0))
         xn = jnp.concatenate([n_lo, xt[24:40]], axis=0)
-        eps = noise(seeds, row16)
-        xkeep[i] = xa
-        ekeep[i] = eps[0:8]
 
         un = first(0, 1, xn)
         hi, lo = split(xa)
         xw = jnp.concatenate([hi, lo], axis=0).astype(BF)
-        ua = dot(w1all[HID : 3 * HID, :], jnp.concatenate([hi, lo, hi], axis=0).astype(BF))
+        ua = dot(w1all[0 : 3 * HID, :], jnp.concatenate([hi, lo, hi], axis=0).astype(BF))
+        eps = noise(seeds, row16)
+        e = eps[0:8]
         hn, _ = act(un)
-        h1c, d1c = zip(*[act(ua[k * HID : (1 + k) * HID]) for k in range(2)])
+        h1a, d1a = act32(ua[0:HID])
+        h1c, d1c = zip(*[act(ua[(1 + k) * HID : (2 + k) * HID]) for k in range(2)])
         hn, _ = layer2(i, 0, hn)
         r = dot(head[...], hn)
         mean, _, ls = head_out(r[0:16] + r[16:32])
         a2, _, lp2 = sample(mean, ls, eps[8:16], live)
+        h1a, r = exact(fa, h1a)
+        h2a, d2a = act32(r + col[:, 0:1])
+        h2a, r = exact(head, h2a)
+        mean, t, ls = head_out(r)
+        a1, sg, lp = sample(mean, ls, e, live)
         un = first(3, 5, jnp.concatenate([jnp.where(live, a2, n_lo), xt[24:40]], axis=0))
         h2c, d2c = zip(*[layer2(i, 1 + k, h1c[k]) for k in range(2)])
         qc = [q_of(k, h2c[k], jb3_s[k]) for k in range(2)]
+        uq = first(1, 3, jnp.concatenate([jnp.where(live, a1, xa[0:8]), xt[0:16]], axis=0))
         ht = [act(un[k * HID : (k + 1) * HID])[0] for k in range(2)]
         ht = [layer2(i, 3 + k, ht[k])[0] for k in range(2)]
         qt = [q_of(2 + k, ht[k], lb3_s[k]) for k in range(2)]
+        h1q, d1q = zip(*[act(uq[k * HID : (k + 1) * HID]) for k in range(2)])
         y = reward + GAMMA * (1.0 - done) * (softmin(qt[0], qt[1]) - alpha * lp2)
+        h2q, d2q = zip(*[layer2(i, 1 + k, h1q[k]) for k in range(2)])
+        qq = [q_of(k, h2q[k], jb3_s[k]) for k in range(2)]
+
         closs = jnp.zeros((1, T), F32)
+        g2c = []
         for k in range(2):
             dq = qc[k] - y
             mdq = dq * mask
             closs = closs + 0.5 * (mdq * dq)
             g2 = (mdq * d2c[k]).astype(BF)
+            g2c.append(g2)
             mhi, mlo = split(mdq)
             m16 = jnp.where(row16 == 0, mhi, jnp.where(row16 == 1, mlo, 0.0)).astype(BF)
             gcw3[k] += dot_t(m16, h2c[k])
             r = dot_t(jnp.concatenate([h1c[k], ones], axis=0), g2)
             gw2[1 + k] += r[0:HID]
             gw2b[1 + k] += r[HID : HID + 8]
-            g1 = (by_chunk(b2, 1 + k, i, g2) * d1c[k]).astype(BF)
-            w = dot_t(xw, g1)
-            gcw1[k] += w[0:24] + w[24:48]
             gmisc[k : k + 1, :] += fold(mdq)
-        gmisc[2:3, :] += fold(closs)
-
-    mine = critic_sum.mine
-    mine[...] = jnp.zeros_like(mine)
-    row8h = lax.broadcasted_iota(jnp.int32, (8, HID), 0)
-    cols = jnp.zeros((8, HID), F32)
-    for k in range(2):
-        s = scale[k : k + 1, :]
-        cols = jnp.where(row8h == k, gw2b[1 + k] * s, cols)
-        cols = jnp.where(row8h == 2 + k, gcw3[k, 0:1, :] + gcw3[k, 1:2, :], cols)
-        for h in range(2):
-            at = slice(h * 128, (h + 1) * 128)
-            put(mine, (2 * k + h) * HID, gw2[1 + k, :, at] * s[:, at])
-            put(mine, R_CW1 + 48 * k + 24 * h, gcw1[k, :, at])
-    for h in range(2):
-        put(mine, R_CCOL + 8 * h, cols[:, h * 128 : (h + 1) * 128])
-    pl.semaphore_wait(barrier, len(partners))
-    critic_sum.step(0, 0)
-    last = critic_sum.steps()
-    when = (0, 1, 3, 4, 5, 7, 8) if (last, nt) == (6, 8) else tuple(j * nt // last for j in range(last + 1))
-
-    @pl.loop(0, nt)
-    def _(i):
-        for j in range(1, last + 1):
-            if when[j] < nt:
-                pl.when(i == when[j])(functools.partial(critic_sum.step, j, 0))
-        mask = mask_of(i)
-        alpha = jnp.exp(jnp.full((1, T), level, F32))
-        xa = xkeep[i]
-        e = ekeep[i]
-        hi, lo = split(xa)
-        xw = jnp.concatenate([hi, lo], axis=0).astype(BF)
-        h1a, d1a = act32(dot(w1all[0:HID, :], jnp.concatenate([hi, lo, hi], axis=0).astype(BF)))
-        h1a, r = exact(fa, h1a)
-        h2a, d2a = act32(r + col[:, 0:1])
-        h2a, r = exact(head, h2a)
-        mean, t, ls = head_out(r)
-        a1, sg, lp = sample(mean, ls, e, live)
-        uq = first(1, 3, jnp.concatenate([jnp.where(live, a1, xa[0:8]), xa[8:24]], axis=0))
-        h1q, d1q = zip(*[act(uq[k * HID : (k + 1) * HID]) for k in range(2)])
-        h2q, d2q = zip(*[layer2(i, 1 + k, h1q[k]) for k in range(2)])
-        qq = [q_of(k, h2q[k], jb3_s[k]) for k in range(2)]
         sm = softmin(qq[0], qq[1])
         p0 = 1.0 / (1.0 + jnp.exp(4.0 * (qq[0] - qq[1])))
         da = jnp.zeros((8, T), F32)
@@ -608,6 +565,10 @@
             g1 = (by_chunk(b2, 1 + k, i, d2q[k].astype(BF)) * d1q[k]).astype(BF)
             w = dot(da_w[k], g1)
             da = da - (pk * mask) * (w[0:8] + w[8:16])
+        for k in range(2):
+            g1 = (by_chunk(b2, 1 + k, i, g2c[k]) * d1c[k]).astype(BF)
+            w = dot_t(xw, g1)
+            gcw1[k] += w[0:24] + w[24:48]
         ma = mask * alpha
         du = da * (1.0 - a1 * a1) + ma * (2.0 * a1)
         dls = (du * sg * e - ma) * (3.5 * (1.0 - t * t))
@@ -622,92 +583,114 @@
         g1 = (by_chunk(b2, 0, i, g2) * d1a).astype(BF)
         w = dot_t(xw, g1)
         gaw1[...] += w[0:24] + w[24:48]
+        gmisc[2:3, :] += fold(closs)
         gmisc[3:4, :] += fold(mask * (alpha * lp - sm))
         gmisc[4:5, :] += fold(mask * (lp - 6.0))
         gmisc[5:6, :] += fold(mask)
 
-    mine = actor_sum.mine
-    mine[...] = jnp.zeros_like(mine)
+    def pack(at, value):
+        k = 0 if at < R_CUT else 1
+        put(sums[k].mine, at - k * R_CUT, value)
+
+    row8 = lax.broadcasted_iota(jnp.int32, (8, HID), 0)
+    cols = jnp.zeros((8, HID), F32)
+    for k in range(2):
+        s = scale[k : k + 1, :]
+        cols = jnp.where(row8 == k, gw2b[1 + k] * s, cols)
+        cols = jnp.where(row8 == 2 + k, gcw3[k, 0:1, :] + gcw3[k, 1:2, :], cols)
+    cols = jnp.where(row8 == 4, gw2b[0], cols)
+    for t in sums:
+        rows = t.mine.shape[1]
+        full = R_CUT if t is sums[0] else R_END - R_CUT
+        for p in range(full // rows, n):
+            t.mine[p] = jnp.zeros((rows, 128), F32)
+    for m in range(3):
+        for h in range(2):
+            at = slice(h * 128, (h + 1) * 128)
+            w = gw2[m, :, at]
+            if m > 0:
+                w = w * scale[m - 1 : m, at]
+            pack((2 * m + h) * HID, w)
     for h in range(2):
         at = slice(h * 128, (h + 1) * 128)
-        put(mine, h * HID, gw2[0, :, at])
-        put(mine, R_AW1 + 24 * h, gaw1[:, at])
-        put(mine, R_AW3 + 16 * h, gaw3[:, at])
-        put(mine, R_ACOL + 8 * h, gw2b[0, :, at])
-    put(mine, R_AB3, gcol[...])
-    put(mine, R_MISC, gmisc[...])
-    for c in range(len(actor_sum.parts)):
-        actor_sum.step(0, c)
-    for j in range(1, last + 1):
-        if when[j] >= nt:
-            critic_sum.step(j, 0)
-    for j in range(1, last + 1):
-        for c in range(len(actor_sum.parts)):
-            actor_sum.step(j, c)
-    critic_sum.all_sent()
-    actor_sum.all_sent()
+        pack(R_AW1 + 24 * h, gaw1[:, at])
+        for k in range(2):
+            pack(R_CW1 + 48 * k + 24 * h, gcw1[k, :, at])
+        pack(R_AW3 + 16 * h, gaw3[:, at])
+        pack(R_COL + 8 * h, cols[:, at])
+    pack(R_AB3, gcol[...])
+    pack(R_MISC, gmisc[...])
+    pl.semaphore_wait(barrier, len(partners))
+    for j in range(2 * ns + 1):
+        for t in sums:
+            for c in range(len(t.parts)):
+                t.step(j, c)
+    for t in sums:
+        t.all_sent()
 
 
 def summed_grads(ready, n, cap):
     tab, got, idx_s, *weights, scal = ready
     slots = n * cap
     T = min(TILE, slots)
-    rows_c, rows_a = piece_rows(R_CEND, n), piece_rows(R_AEND, n)
+    heights = piece_rows(R_CUT, n), piece_rows(R_END - R_CUT, n)
     vm = pl.BlockSpec(memory_space=pltpu.VMEM)
     sm = pl.BlockSpec(memory_space=pltpu.SMEM)
+    scratch = [
+        pltpu.VMEM((T, 128), F32),
+        pltpu.VMEM((3, HID, HID), F32),
+        pltpu.VMEM((3, 8, HID), F32),
+        pltpu.VMEM((24, HID), F32),
+        pltpu.VMEM((2, 24, HID), F32),
+        pltpu.VMEM((16, HID), F32),
+        pltpu.VMEM((2, 16, HID), F32),
+        pltpu.VMEM((16, 128), F32),
+        pltpu.VMEM((8, 128), F32),
+    ]
+    for groups, height, chunks in zip(stage_groups(n), heights, CHUNKS):
+        scratch += sum_scratch(groups, n, height, chunks)
     return pl.pallas_call(
         functools.partial(net_kernel, n=n, cap=cap, slots=slots),
-        out_shape=[pltpu.VMEM((n, rows_c, 128), F32), pltpu.VMEM((n, rows_a, 128), F32)],
+        out_shape=[pltpu.VMEM((n, height, 128), F32) for height in heights],
         in_specs=[sm] * 2 + [vm] * (2 + len(weights)),
         out_specs=[vm, vm],
-        scratch_shapes=[
-            pltpu.VMEM((T, 128), F32),
-            pltpu.VMEM((slots // T, 24, T), F32),
-            pltpu.VMEM((slots // T, 8, T), F32),
-            pltpu.VMEM((3, HID, HID), F32),
-            pltpu.VMEM((3, 8, HID), F32),
-            pltpu.VMEM((24, HID), F32),
-            pltpu.VMEM((2, 24, HID), F32),
-            pltpu.VMEM((16, HID), F32),
-            pltpu.VMEM((2, 16, HID), F32),
-            pltpu.VMEM((16, 128), F32),
-            pltpu.VMEM((8, 128), F32),
-        ]
-        + sum_scratch(n, rows_c, 1)
-        + sum_scratch(n, rows_a, CHUNKS),
-        compiler_params=pltpu.CompilerParams(collective_id=1, has_side_effects=True, vmem_limit_bytes=34 << 20),
+        scratch_shapes=scratch,
+        compiler_params=pltpu.CompilerParams(collective_id=1, has_side_effects=True, vmem_limit_bytes=36 << 20),
         name="networks",
     )(idx_s, scal, tab, got, *weights)
 
 
-def finish_kernel(scal, gc, ga, aw1, ab1, aw2, ab2, aw3, ab3, cw1, cb1, cw2, cb2, cw3, cb3, da, losses):
-    misc = jnp.sum(ga[R_MISC : R_MISC + 8, :], axis=1, keepdims=True)
+def finish_kernel(scal, gq, gp, aw1, ab1, aw2, ab2, aw3, ab3, cw1, cb1, cw2, cb2, cw3, cb3, da, losses):
+    def part(at, count):
+        return gq[at : at + count, :] if at < R_CUT else gp[at - R_CUT : at - R_CUT + count, :]
+
+    misc = jnp.sum(part(R_MISC, 8), axis=1, keepdims=True)
     inv = 1.0 / misc[5:6]
 
-    def rows(g, at, count):
-        return jnp.concatenate([g[at : at + count, :], g[at + count : at + 2 * count, :]], axis=1) * inv
-
-    aw2[...] = rows(ga, 0, HID)
-    cw2[0] = rows(gc, 0, HID)
-    cw2[1] = rows(gc, 2 * HID, HID)
-    w = rows(ga, R_AW1, 24)
+    def rows(at, count):
+        return jnp.concatenate([part(at, count), part(at + count, count)], axis=1) * inv
+
+    aw2[...] = rows(0, HID)
+    cw2[0] = rows(2 * HID, HID)
+    cw2[1] = rows(4 * HID, HID)
+    w = rows(R_AW1, 24)
     aw1[0:16, :] = w[8:24]
     aw1[16:17, :] = w[7:8]
     ab1[...] = w[6:7]
     for k in range(2):
-        w = rows(gc, R_CW1 + 48 * k, 24)
+        w = rows(R_CW1 + 48 * k, 24)
         cw1[0:16, k, :] = w[8:24]
         cw1[16:17, k, :] = w[7:8]
         cw1[17:23, k, :] = w[0:6]
         cb1[k : k + 1, :] = w[6:7]
-    w = rows(ga, R_AW3, 16)
+    w = rows(R_AW3, 16)
     aw3[0:6, :] = w[0:6]
     aw3[6:12, :] = w[8:14]
-    c = rows(gc, R_CCOL, 8)
+    c = rows(R_COL, 8)
     cb2[...] = c[0:2]
     cw3[...] = c[2:4]
-    ab2[...] = rows(ga, R_ACOL, 8)[0:1]
-    b = jnp.sum(ga[R_AB3 : R_AB3 + 16, :], axis=1, keepdims=True) * inv
+    ab2[...] = c[4:5]
+    b = jnp.sum(part(R_AB3, 16), axis=1, keepdims=True) * inv
     diag = lax.broadcasted_iota(jnp.int32, (16, 128), 0) == lax.broadcasted_iota(jnp.int32, (16, 128), 1)
     b = jnp.sum(jnp.where(diag, b, 0.0), axis=0, keepdims=True)
     ab3[...] = jnp.concatenate([b[:, 0:6], b[:, 8:14]], axis=1)
@@ -717,7 +700,7 @@
     losses[...] = jnp.concatenate([m[2:3], m[3:4], -scal[4] * m[4:5]], axis=1)
 
 
-def finish(critics, others, scal):
+def finish(first, second, scal):
     vm = pl.BlockSpec(memory_space=pltpu.VMEM)
     shapes = [
         (OBS, HID), (1, HID), (HID, HID), (1, HID), (12, HID), (1, 12),
@@ -730,7 +713,7 @@
         out_specs=[vm] * len(shapes),
         compiler_params=pltpu.CompilerParams(vmem_limit_bytes=16 << 20),
         name="finish",
-    )(scal, critics.reshape(-1, 128), others.reshape(-1, 128)))
+    )(scal, first.reshape(-1, 128), second.reshape(-1, 128)))
     outs[4] = outs[4].T
     outs[6] = outs[6].transpose(1, 0, 2)
     for k, shape in ((1, (HID,)), (3, (HID,)), (5, (12,)), (11, (2,)), (12, ()), (13, (3,))):

time: 105 us -> 100 us (0.952)
  Pallas kernels: 103 us -> 98.8 us
    pallas_call x1, Pallas kernels: 86.3 us -> 82 us  [summed_grads(): pl.pallas_call(functools.partial(net_kernel, n=n, cap=cap, slots=slots),...]
where the time goes in v8:
time: 100 us
  Pallas kernels  98.8 us (99%)
  between operations  1.32 us (1%)
    pallas_call x1, Pallas kernels, summed_grads(): pl.pallas_call(functools.partial(net_kernel, n=n, cap=cap, slots=slots),...  82 us
    pallas_call x1, Pallas kernels, prepare(): pl.pallas_call(functools.partial(prepare_kernel, n=n, cap=cap), out_shape...  15.7 us

profile of v8, /device:TPU:0, one launch (start us, length us, event | category | flops | bytes accessed | tf_op | source)
XLA Modules:
  0.0 100.1 jit_solution(9444334006111299558)
XLA Ops:
  1.3 15.7 %exchange_and_prepare.1 = (f32[16384,128]{1,0:T(8,128)S(1)}, s32[32,8,128]{2,1,0:T(8,128)S(1)}, s32[32,2,128]{2,1,0:T(2,128)S(4)}, bf16[1280,72]{1,0:T(8,128)(2,...) custom-call(s32[1,32,256]{2,1,0:T(8,128)} %idx_h.1, ...), custom_call_target="tpu_custom_call" | custom-call | tf_op jit(solution)/shard_map/exchange_and_prepare/pallas_call | solution.py:240
  17.0 82.0 %networks.1 = (f32[32,40,128]{2,1,0:T(8,128)S(1)}, f32[32,16,128]{2,1,0:T(8,128)S(1)}) custom-call(s32[32,2,128]{2,1,0:T(2,128)S(4)} %get-tuple-element.45.idx_s, f32[8]{0:T(128)S(4)} %get-tuple-element.44.scal, f32[16384,128]{1,0:T(8,128)S(1)} %get-tuple-element.46.tab, s32[32,8,128]{2,1,0:T(8,128)S(1)} %get-tuple-element.47.got, ...), custom_call_target="tpu_custom_call" | custom-call | tf_op jit(solution)/shard_map/networks/pallas_call | solution.py:652
  99.1 1.0 %finish.1 = (f32[17,256]{1,0:T(8,128)}, f32[1,256]{1,0:T(1,128)}, f32[256,256]{1,0:T(8,128)}, f32[1,256]{1,0:T(1,128)}, f32[12,256]{1,0:T(8,128)}, /*index=5*/f3...) custom-call(f32[8]{0:T(128)S(4)} %get-tuple-element.44.scal, ...), custom_call_target="tpu_custom_call" | custom-call | tf_op jit(solution)/shard_map/finish/pallas_call | solution.py:709

commit v9 on v8

--- a/solution.py
+++ b/solution.py
@@ -15,7 +15,7 @@
 PRIME = 65521
 TILE = 1024
 CHUNKS = (2, 1)
-VARIANTS = 8
+VARIANTS = 4
 R_AW1 = 6 * HID
 R_CW1 = R_AW1 + 48
 R_AW3 = R_CW1 + 96
@@ -172,6 +172,7 @@
     col[...] = rowbuf[...].T
     scale[...] = jnp.zeros_like(scale)
     scale[0:2, :] = 0.5 * jw3[...]
+    scale[7:8, :] = jnp.ones((1, HID), F32)
     for k in range(2):
         scal[k] = jb3[k]
         scal[2 + k] = lb3[k]
@@ -435,9 +436,11 @@
     jb3_s = (scal[0], scal[1])
     lb3_s = (scal[2], scal[3])
 
+    one = scale[7:8, 0:1]
+
     def act32(u):
         t = jnp.tanh(u)
-        p = 1.0 + t
+        p = one + t
         h = u * p
         return h, p + h * (2.0 - p)
 
@@ -456,7 +459,8 @@
     def by_chunk(w, l, i, x):
         nq = T // HID
         return jnp.concatenate(
-            [dot(w[l, lax.rem(i * nq + q, VARIANTS)], x[:, q * HID : (q + 1) * HID]) for q in range(nq)], axis=1
+            [dot(w[l, q % VARIANTS if nq % VARIANTS == 0 else lax.rem(i * nq + q, VARIANTS)], x[:, q * HID : (q + 1) * HID]) for q in range(nq)],
+            axis=1,
         )
 
     def exact(w, h):

time: 100 us -> 96.3 us (0.963)
  Pallas kernels: 98.8 us -> 94.8 us
    pallas_call x1, Pallas kernels: 82 us -> 79.2 us  [summed_grads(): pl.pallas_call(functools.partial(net_kernel, n=n, cap=cap, slots=slots),...]
    pallas_call x1, Pallas kernels: 15.7 us -> 14.6 us  [prepare(): pl.pallas_call(functools.partial(prepare_kernel, n=n, cap=cap), out_shape...]
where the time goes in v9:
time: 96.3 us; the launch traced here: 96.1 us
  Pallas kernels  94.8 us (98%)
  between operations  1.32 us (1%)
    pallas_call x1, Pallas kernels, summed_grads(): pl.pallas_call(functools.partial(net_kernel, n=n, cap=cap, slots=slots),...  79.2 us
    pallas_call x1, Pallas kernels, prepare(): pl.pallas_call(functools.partial(prepare_kernel, n=n, cap=cap), out_shape...  14.6 us

profile of v9, /device:TPU:0, one launch (start us, length us, event | category | flops | bytes accessed | tf_op | source)
XLA Modules:
  0.0 96.1 jit_solution(1178397813578899151)
XLA Ops:
  1.3 14.6 %exchange_and_prepare.1 = (f32[16384,128]{1,0:T(8,128)S(1)}, s32[32,8,128]{2,1,0:T(8,128)S(1)}, s32[32,2,128]{2,1,0:T(2,128)S(4)}, bf16[1280,72]{1,0:T(8,128)(2,...) custom-call(s32[1,32,256]{2,1,0:T(8,128)} %idx_h.1, ...), custom_call_target="tpu_custom_call" | custom-call | tf_op jit(solution)/shard_map/exchange_and_prepare/pallas_call | solution.py:241
  15.9 79.2 %networks.1 = (f32[32,40,128]{2,1,0:T(8,128)S(1)}, f32[32,16,128]{2,1,0:T(8,128)S(1)}) custom-call(s32[32,2,128]{2,1,0:T(2,128)S(4)} %get-tuple-element.45.idx_s, f32[8]{0:T(128)S(4)} %get-tuple-element.44.scal, f32[16384,128]{1,0:T(8,128)S(1)} %get-tuple-element.46.tab, s32[32,8,128]{2,1,0:T(8,128)S(1)} %get-tuple-element.47.got, ...), custom_call_target="tpu_custom_call" | custom-call | tf_op jit(solution)/shard_map/networks/pallas_call | solution.py:656
  95.1 1.0 %finish.1 = (f32[17,256]{1,0:T(8,128)}, f32[1,256]{1,0:T(1,128)}, f32[256,256]{1,0:T(8,128)}, f32[1,256]{1,0:T(1,128)}, f32[12,256]{1,0:T(8,128)}, /*index=5*/f3...) custom-call(f32[8]{0:T(128)S(4)} %get-tuple-element.44.scal, ...), custom_call_target="tpu_custom_call" | custom-call | tf_op jit(solution)/shard_map/finish/pallas_call | solution.py:713

commit v10 on v9

--- a/solution.py
+++ b/solution.py
@@ -76,7 +76,7 @@
     idx_h, seed_h, cnt_h, buf_h, aw2_h, jw2_h, lw2_h,
     aw1_h, ab1_h, ab2_h, aw3_h, jw1_h, jb1_h, jb2_h, jw3_h, lw1_h, lb1_h, lb2_h, lw3_h,
     ab3_h, jb3_h, lb3_h, level,
-    tab, got, idx_s, w1all, fa, f2, b2, head, headb, da_w, qw, col, scale, scal,
+    tab, got, idx_s, w1all, f2, f2v, b2, b2v, head, headb, da_w, qw, col, scale, scal,
     idx_v, seed_v, cnt_v, buf, w2, aw1, ab1, ab2, aw3, jw1, jb1, jb2, jw3, lw1, lb1, lb2, lw3,
     ab3, jb3, lb3, msg, land, flat, tmp, rowbuf, in_sems, sems,
     *, n, cap,
@@ -138,18 +138,21 @@
             ref[l, v] = got_
             left = want - got_.astype(F32)
 
+    def pieces(ref, l, w):
+        hi, lo = split(w)
+        ref[l, 0:HID, :] = hi.astype(BF)
+        ref[l, HID:, :] = lo.astype(BF)
+
     for l in range(5):
         w = 0.5 * w2[l]
         wt = w.T
-        roundings(f2, l, wt)
-        if l == 0:
-            hi, lo = split(wt)
-            fa[0:HID, :] = hi.astype(BF)
-            fa[HID:, :] = lo.astype(BF)
-        if l == 0:
-            roundings(b2, l, w)
-        elif l < 3:
-            roundings(b2, l, w * (0.5 * jw3[l - 1 : l, :]))
+        pieces(f2, l, wt)
+        if l in (1, 2):
+            roundings(f2v, l - 1, wt)
+            w = w * (0.5 * jw3[l - 1 : l, :])
+            pieces(b2, l - 1, w)
+        if l < 3:
+            roundings(b2v, l, w)
     tmp[0:12, :] = aw3[...]
     r8 = lax.broadcasted_iota(jnp.int32, (8, HID), 0)
     w_head = jnp.concatenate([jnp.where(r8 < 6, tmp[0:8, :], 0.0), jnp.where(r8 < 6, tmp[6:14, :], 0.0)], axis=0)
@@ -227,8 +230,9 @@
         pltpu.VMEM((n, 8, 128), jnp.int32),
         pltpu.SMEM((n, rows, 128), jnp.int32),
         pltpu.VMEM((5 * HID, 72), BF),
-        pltpu.VMEM((2 * HID, HID), BF),
-        pltpu.VMEM((5, VARIANTS, HID, HID), BF),
+        pltpu.VMEM((5, 2 * HID, HID), BF),
+        pltpu.VMEM((2, VARIANTS, HID, HID), BF),
+        pltpu.VMEM((2, 2 * HID, HID), BF),
         pltpu.VMEM((3, VARIANTS, HID, HID), BF),
         pltpu.VMEM((32, HID), BF),
         pltpu.VMEM((HID, 32), BF),
@@ -242,7 +246,7 @@
         functools.partial(prepare_kernel, n=n, cap=cap),
         out_shape=out,
         in_specs=[hbm] * 22 + [sm],
-        out_specs=[vm, vm, sm] + [vm] * 10 + [sm],
+        out_specs=[vm, vm, sm] + [vm] * 11 + [sm],
         scratch_shapes=[
             pltpu.VMEM((1, n, cap), jnp.int32),
             pltpu.VMEM((1, n, cap), jnp.int32),
@@ -403,7 +407,7 @@
 
 
 def net_kernel(
-    idx_s, scal, tab, got, w1all, fa, f2, b2, head, headb, da_w, qw, col, scale,
+    idx_s, scal, tab, got, w1all, f2, f2v, b2, b2v, head, headb, da_w, qw, col, scale,
     sum_q, sum_p,
     xrow, gw2, gw2b, gaw1, gcw1, gaw3, gcw3, gcol, gmisc, *rest,
     n, cap, slots,
@@ -448,8 +452,15 @@
         h, d = act32(u)
         return h.astype(BF), d
 
-    def layer2(i, l, h):
-        return act(by_chunk(f2, l, i, h) + col[:, l : l + 1])
+    def both(w, x):
+        r = dot(w, x)
+        return r[:HID] + r[HID:]
+
+    def layer2(l, h):
+        return act(both(f2[l], h) + col[:, l : l + 1])
+
+    def layer2_once(i, l, h):
+        return act(by_chunk(f2v, l - 1, i, h) + col[:, l : l + 1])
 
     def first(l0, l1, x24):
         hi, lo = split(x24)
@@ -465,9 +476,9 @@
 
     def exact(w, h):
         hb = h.astype(BF)
-        r = dot(w[...], hb)
+        r = dot(w, hb)
         half = r.shape[0] // 2
-        lo = dot(w[0:half, :], (h - hb.astype(F32)).astype(BF))
+        lo = dot(w[0:half], (h - hb.astype(F32)).astype(BF))
         return hb, r[:half] + (r[half:] + lo)
 
     def head_out(o):
@@ -526,25 +537,25 @@
         hn, _ = act(un)
         h1a, d1a = act32(ua[0:HID])
         h1c, d1c = zip(*[act(ua[(1 + k) * HID : (2 + k) * HID]) for k in range(2)])
-        hn, _ = layer2(i, 0, hn)
+        hn, _ = layer2(0, hn)
         r = dot(head[...], hn)
         mean, _, ls = head_out(r[0:16] + r[16:32])
         a2, _, lp2 = sample(mean, ls, eps[8:16], live)
-        h1a, r = exact(fa, h1a)
+        h1a, r = exact(f2[0], h1a)
         h2a, d2a = act32(r + col[:, 0:1])
-        h2a, r = exact(head, h2a)
+        h2a, r = exact(head[...], h2a)
         mean, t, ls = head_out(r)
         a1, sg, lp = sample(mean, ls, e, live)
         un = first(3, 5, jnp.concatenate([jnp.where(live, a2, n_lo), xt[24:40]], axis=0))
-        h2c, d2c = zip(*[layer2(i, 1 + k, h1c[k]) for k in range(2)])
+        h2c, d2c = zip(*[layer2(1 + k, h1c[k]) for k in range(2)])
         qc = [q_of(k, h2c[k], jb3_s[k]) for k in range(2)]
         uq = first(1, 3, jnp.concatenate([jnp.where(live, a1, xa[0:8]), xt[0:16]], axis=0))
         ht = [act(un[k * HID : (k + 1) * HID])[0] for k in range(2)]
-        ht = [layer2(i, 3 + k, ht[k])[0] for k in range(2)]
+        ht = [layer2(3 + k, ht[k])[0] for k in range(2)]
         qt = [q_of(2 + k, ht[k], lb3_s[k]) for k in range(2)]
         h1q, d1q = zip(*[act(uq[k * HID : (k + 1) * HID]) for k in range(2)])
         y = reward + GAMMA * (1.0 - done) * (softmin(qt[0], qt[1]) - alpha * lp2)
-        h2q, d2q = zip(*[layer2(i, 1 + k, h1q[k]) for k in range(2)])
+        h2q, d2q = zip(*[layer2_once(i, 1 + k, h1q[k]) for k in range(2)])
         qq = [q_of(k, h2q[k], jb3_s[k]) for k in range(2)]
 
         closs = jnp.zeros((1, T), F32)
@@ -566,11 +577,11 @@
         p0 = 1.0 / (1.0 + jnp.exp(4.0 * (qq[0] - qq[1])))
         da = jnp.zeros((8, T), F32)
         for k, pk in enumerate((p0, 1.0 - p0)):
-            g1 = (by_chunk(b2, 1 + k, i, d2q[k].astype(BF)) * d1q[k]).astype(BF)
+            g1 = (by_chunk(b2v, 1 + k, i, d2q[k].astype(BF)) * d1q[k]).astype(BF)
             w = dot(da_w[k], g1)
             da = da - (pk * mask) * (w[0:8] + w[8:16])
         for k in range(2):
-            g1 = (by_chunk(b2, 1 + k, i, g2c[k]) * d1c[k]).astype(BF)
+            g1 = (both(b2[k], g2c[k]) * d1c[k]).astype(BF)
             w = dot_t(xw, g1)
             gcw1[k] += w[0:24] + w[24:48]
         ma = mask * alpha
@@ -584,7 +595,7 @@
         r = dot_t(jnp.concatenate([h1a, ones], axis=0), g2)
         gw2[0] += r[0:HID]
         gw2b[0] += r[HID : HID + 8]
-        g1 = (by_chunk(b2, 0, i, g2) * d1a).astype(BF)
+        g1 = (by_chunk(b2v, 0, i, g2) * d1a).astype(BF)
         w = dot_t(xw, g1)
         gaw1[...] += w[0:24] + w[24:48]
         gmisc[2:3, :] += fold(closs)

time: 96.3 us -> 102 us (1.059)
  Pallas kernels: 94.8 us -> 101 us
    pallas_call x1, Pallas kernels: 79.2 us -> 85.1 us  [summed_grads(): pl.pallas_call(functools.partial(net_kernel, n=n, cap=cap, slots=slots),...]
where the time goes in v10:
time: 102 us
  Pallas kernels  101 us (99%)
  between operations  1.32 us (1%)
    pallas_call x1, Pallas kernels, summed_grads(): pl.pallas_call(functools.partial(net_kernel, n=n, cap=cap, slots=slots),...  85.1 us
    pallas_call x1, Pallas kernels, prepare(): pl.pallas_call(functools.partial(prepare_kernel, n=n, cap=cap), out_shape...  14.4 us

profile of v10, /device:TPU:0, one launch (start us, length us, event | category | flops | bytes accessed | tf_op | source)
XLA Modules:
  0.0 101.9 jit_solution(8154498132719815095)
XLA Ops:
  1.3 14.4 %exchange_and_prepare.1 = (f32[16384,128]{1,0:T(8,128)S(1)}, s32[32,8,128]{2,1,0:T(8,128)S(1)}, s32[32,2,128]{2,1,0:T(2,128)S(4)}, bf16[1280,72]{1,0:T(8,128)(2,...) custom-call(s32[1,32,256]{2,1,0:T(8,128)} %idx_h.1, ...), custom_call_target="tpu_custom_call" | custom-call | tf_op jit(solution)/shard_map/exchange_and_prepare/pallas_call | solution.py:245
  15.7 85.1 %networks.1 = (f32[32,40,128]{2,1,0:T(8,128)S(1)}, f32[32,16,128]{2,1,0:T(8,128)S(1)}) custom-call(s32[32,2,128]{2,1,0:T(2,128)S(4)} %get-tuple-element.46.idx_s, f32[8]{0:T(128)S(4)} %get-tuple-element.45.scal, f32[16384,128]{1,0:T(8,128)S(1)} %get-tuple-element.47.tab, s32[32,8,128]{2,1,0:T(8,128)S(1)} %get-tuple-element.48.got, ...), custom_call_target="tpu_custom_call" | custom-call | tf_op jit(solution)/shard_map/networks/pallas_call | solution.py:667
  100.8 1.0 %finish.1 = (f32[17,256]{1,0:T(8,128)}, f32[1,256]{1,0:T(1,128)}, f32[256,256]{1,0:T(8,128)}, f32[1,256]{1,0:T(1,128)}, f32[12,256]{1,0:T(8,128)}, /*index=5*/f3...) custom-call(f32[8]{0:T(128)S(4)} %get-tuple-element.45.scal, ...), custom_call_target="tpu_custom_call" | custom-call | tf_op jit(solution)/shard_map/finish/pallas_call | solution.py:724
